TPU v7x, 512 devices: a whole 4x8x8 slice. The times are simulated.
512 devices in a mesh: comp: 4 (over z_lo), band: 64 (over x, z_hi, y), cores: 2 (over core).
Axes of the slice: x: 4, y: 8, z: 8 (z_hi: 2, z_lo: 4; z = z_hi * 4 + z_lo), core: 2. Of those that a mesh axis runs over, the one named last changes fastest.
Arguments:
- latent: float32 [2, 4, 128, 240], P(None, None, 'band'), may hold values from -2.5 to 2.5
- section_inputs: bfloat16 [4, 2, 128, 76800], P('comp', None, 'band', 'cores'), may hold values from -6 to 6
- in_weight: float32 [4, 320], P(None, 'cores'), may hold values from -3 to 3
- conv_weight: bfloat16 [4, 921600], P('comp', 'cores'), may hold values from -0.109375 to 0.109375
- out_weight: bfloat16 [320, 4], P('cores'), may hold values from -0.3125 to 0.3125
- timesteps: int32 [4], replicated, may hold values from 0 to 999, as said below
- plan: float32 [1000], replicated, may hold values from 0.04 to 0.95
Outputs:
- denoised: float32 [2, 4, 128, 240], P(None, 'comp', 'band')
- handoff: bfloat16 [4, 2, 128, 76800], P('comp', None, 'band', 'cores')
Inputs may be any that keep to these rules, and one draw needn't show every extreme that they name: `timesteps`: falling from step to step, the first entry 999 and the last 0.
All inputs are finite; a program needn't handle non-finite values.
Results may differ from a plain program's by a relative error of at most 0.015.
Values may be sent and summed in bfloat16 or wider, within the bound.
No kernel may reach another device: no remote copies, remote signals or barrier semaphores. Data moves between devices by JAX's collectives and lax.ppermute only.
A program may use at most 64 MiB of HBM per device.

v0:
```python
import jax
import jax.numpy as jnp
from jax import lax
from jax.sharding import PartitionSpec as P

STEPS = 3


def extended(cells, sides, width):
    for axis, dim in sides:
        count = lax.axis_size(axis)
        ends = count - 1
        head = lax.slice_in_dim(cells, 0, width, axis=dim)
        tail = lax.slice_in_dim(cells, cells.shape[dim] - width, cells.shape[dim], axis=dim)
        cells = jnp.concatenate(
            [
                lax.ppermute(tail, axis, [(i, (i + 1) % count) for i in range(ends)]),
                cells,
                lax.ppermute(head, axis, [((i + 1) % count, i) for i in range(ends)]),
            ],
            axis=dim,
        )
    return cells


def broadcast(value, axis, source):
    kept = jnp.where(lax.axis_index(axis) == source, value, 0).astype(value.dtype)
    return lax.psum(kept, axis)


def passed_along(value, axis, steps):
    count = lax.axis_size(axis)
    initial, last = (max(0, -steps), min(count, count - steps))
    return lax.ppermute(value, axis, [(source, source + steps) for source in range(initial, last)])


def conv_add(total, padded, weight):
    rows = total.shape[1]
    cols = total.shape[3]
    for shift_row in range(3):
        for shift_col in range(3):
            window = padded[:, shift_row : shift_row + rows, :, shift_col : shift_col + cols]
            total = total + jnp.einsum(
                "friq,oi->froq",
                window,
                weight[:, shift_row, shift_col, :],
                preferred_element_type=jnp.float32,
            )
    return total


def widen_cols(padded):
    return jnp.pad(padded, ((0, 0), (0, 0), (0, 0), (1, 1)))


def block(acts, weight):
    active = jax.nn.silu(acts.astype(jnp.float32)).astype(jnp.bfloat16)
    empty = jnp.zeros(acts.shape[:2] + (weight.shape[0], acts.shape[3]), jnp.float32)
    whole = lax.all_gather(active, "cores", axis=2, tiled=True)
    padded = widen_cols(extended(whole, (("band", 1),), 1))
    total = conv_add(empty, padded, weight)
    return (acts.astype(jnp.float32) + total).astype(jnp.bfloat16)


def body(latent, section_inputs, in_weight, conv_weight, out_weight, timesteps, plan):
    position = lax.axis_index("comp")
    last_comp = lax.axis_size("comp") - 1
    frames = latent.shape[0]
    rows = latent.shape[2]
    cols = latent.shape[3]
    channels = in_weight.shape[1]
    width = in_weight.shape[1] * lax.axis_size("cores")
    share = latent.shape[1] // lax.axis_size("comp")
    weight = conv_weight[0].reshape(channels, 3, 3, width)
    received = section_inputs[0].reshape(frames, rows, channels, cols)
    state = latent
    cond = received
    output = received
    for step in range(STEPS):
        proj = jnp.einsum("fjrq,jo->froq", state, in_weight, precision=lax.Precision.HIGHEST)
        first = (proj + cond.astype(jnp.float32)).astype(jnp.bfloat16)
        current = jnp.where(position == 0, first, received)
        output = block(current, weight)
        partial_noise = jnp.einsum(
            "froq,oj->fjrq", output, out_weight, preferred_element_type=jnp.float32
        )
        noise = lax.psum(partial_noise, "cores")
        noise = broadcast(noise, "comp", last_comp)
        alpha_now = plan[timesteps[step]]
        alpha_next = plan[timesteps[step + 1]]
        state = (
            jnp.sqrt(alpha_next / alpha_now) * (state - jnp.sqrt(1.0 - alpha_now) * noise)
            + jnp.sqrt(1.0 - alpha_next) * noise
        )
        if step + 1 < STEPS:
            received = passed_along(output, "comp", 1)
    state = lax.dynamic_slice_in_dim(state, position * share, share, 1)
    return (state, output.reshape(frames, rows, channels * cols)[None])


def solution(mesh):
    in_specs = (
        P(None, None, "band", None),
        P("comp", None, "band", "cores"),
        P(None, "cores"),
        P("comp", "cores"),
        P("cores", None),
        P(),
        P(),
    )
    out_specs = (P(None, "comp", "band", None), P("comp", None, "band", "cores"))
    return jax.shard_map(body, mesh=mesh, in_specs=in_specs, out_specs=out_specs, check_vma=False)
```

profile of v0, /device:TPU:62, one launch (start us, length us, event | category | flops | bytes accessed | tf_op | source)
XLA Modules:
  0.0 211.6 jit_solution(5612997130433371607)
XLA Ops:
  2.4 2.5 %multiply_convert_fusion = (bf16[2,2,160,240]{3,2,1,0:T(8,128)(2,1)S(1)}, f32[2,2,160,240]{3,2,1,0:T(8,128)}) fusion(bf16[2,2,160,240]{3,2,1,0:T(8,128)(2,1)S(1)} %reshape_squeeze.6, f32[2,4,2,240]{3,2,1,0:T(2,128)} %param.7, f32[4,160]{1,0:T(4,128)S(1)} %copy-done, pred[]{:T(512)S(6)} %eq.5), kind=kOutput, calls=%fused_computation.116 | convolution fusion | flops 8908800 | bytes 1246721 | tf_op jit(solution)/shard_map/fjrq,jo->froq/dot_general | solution.py:80
  4.9 2.3 %all_gather.9 = bf16[2,2,320,240]{3,2,1,0:T(8,128)(2,1)S(1)} all-gather(bf16[2,2,160,240]{3,2,1,0:T(8,128)(2,1)S(1)} %get-tuple-element.29), channel_id=1, replica_groups=mesh['comp'=4,'band'=64,'cores'=2] {'cores'}, dimensions={2}, use_global_device_ids=true | all-gather | bytes 921600 | tf_op jit(solution)/shard_map/all_gather | solution.py:59
  8.0 10.1 %collective-permute-start = (bf16[2,1,320,240]{3,2,1,0:T(8,128)(2,1)}, bf16[2,1,320,240]{3,2,1,0:T(8,128)(2,1)}, u32[]{:S(2)}, u32[]{:S(2)}) collective-permute-start(bf16[2,1,320,240]{3,2,1,0:T(8,128)(2,1)} %get-tuple-element.19), channel_id=1, source_target_pairs={{0,2},{2,4},{4,6},{6,8},{8,10},{10,12},{12,14},{14,16},{16,18},{18... | collective-permute-start | bytes 921608 | tf_op jit(solution)/shard_map/ppermute | solution.py:17
  18.2 1.9 collective-permute-start.1
  20.1 20.1 %reduce = bf16[460800]{0:T(1024)(128)(2,1)S(1)} reduce(bf16[1,460800]{1,0:T(2,128)(2,1)} %param.10, bf16[]{:T(256)} %constant.38), dimensions={0}, to_apply=%param.10.reduce_sub_computation | reduce | bytes 1843202 | tf_op args[3]
  42.0 2.6 %fusion.104 = (bf16[160,1,1,320]{3,2,1,0:T(2,128)(2,1)S(1)}, bf16[160,1,1,320]{3,2,1,0:T(2,128)(2,1)S(1)}, bf16[160,1,1,320]{3,2,1,0:T(2,128)(2,1)}, bf16[160,1,...) fusion(bf16[160,3,3,320]{3,2,1,0:T(4,128)(2,1)S(1)} %reshape_sq, ...), kind=kLoop, calls=%fused_computation.152 | loop fusion | bytes 1843200 | tf_op jit(solution)/shard_map/slice | solution.py:46
  65.2 3.4 %collective-permute-start.2 = (bf16[2,2,160,240]{3,2,1,0:T(8,128)(2,1)S(1)}, bf16[2,2,160,240]{3,2,1,0:T(8,128)(2,1)S(1)}, u32[]{:S(2)}, u32[]{:S(2)}) collective-permute-start(bf16[2,2,160,240]{3,2,1,0:T(8,128)(2,1)S(1)} %fusion.30), channel_id=1, source_target_pairs={{0,128},{128,256},{256,384},{1,129},{129,257},{257,385},{2,130},{1... | collective-permute-start | bytes 921608 | tf_op jit(solution)/shard_map/ppermute | solution.py:34
  68.7 3.4 %psum.42 = f32[2,4,2,240]{3,1,2,0:T(4,128)S(1)} all-reduce(f32[2,4,2,240]{3,1,2,0:T(4,128)S(1)} %convolution_bitcast_fusion.5), channel_id=1, replica_groups=mesh['comp'=4,'band'=64,'cores'=2] {'cores'}, use_global_device_ids=true, to_apply=%region_0.1 | all-reduce | flops 3840 | bytes 30720 | tf_op jit(solution)/shard_map/psum | solution.py:87
  72.1 16.9 %psum.43 = f32[2,4,2,240]{3,1,2,0:T(4,128)S(1)} all-reduce(f32[2,4,2,240]{3,1,2,0:T(4,128)S(1)} %broadcast_select_fusion.4), channel_id=1, replica_groups=mesh['comp'=4,'band'=64,'cores'=2] {'comp'}, use_global_device_ids=true, to_apply=%region_1.2 | all-reduce | flops 3840 | bytes 30720 | tf_op jit(solution)/shard_map/psum | solution.py:28
  89.9 2.4 %all_gather.10 = bf16[2,2,320,240]{3,2,1,0:T(8,128)(2,1)S(1)} all-gather(bf16[2,2,160,240]{3,2,1,0:T(8,128)(2,1)S(1)} %get-tuple-element.31), channel_id=1, replica_groups=mesh['comp'=4,'band'=64,'cores'=2] {'cores'}, dimensions={2}, use_global_device_ids=true | all-gather | bytes 921600 | tf_op jit(solution)/shard_map/all_gather | solution.py:59
  92.4 9.9 %collective-permute-start.3 = (bf16[2,1,320,240]{3,2,1,0:T(8,128)(2,1)S(1)}, bf16[2,1,320,240]{3,2,1,0:T(8,128)(2,1)S(1)}, u32[]{:S(2)}, u32[]{:S(2)}) collective-permute-start(bf16[2,1,320,240]{3,2,1,0:T(8,128)(2,1)S(1)} %get-tuple-element.17), channel_id=1, source_target_pairs={{0,2},{2,4},{4,6},{6,8},{8,10},{10,12},{12,14},{14,16},{16,18},{18... | collective-permute-start | bytes 921608 | tf_op jit(solution)/shard_map/ppermute | solution.py:17
  102.3 1.9 collective-permute-start.4
  106.7 5.8 %collective-permute-done.3 = bf16[2,1,320,240]{3,2,1,0:T(8,128)(2,1)S(1)} collective-permute-done((bf16[2,1,320,240]{3,2,1,0:T(8,128)(2,1)S(1)}, bf16[2,1,320,240]{3,2,1,0:T(8,128)(2,1)S(1)}, u32[]{:S(2)}, u32[]{:S(2)}) %collective-permute-start.3) | collective-permute-done | bytes 307232 | tf_op jit(solution)/shard_map/ppermute | solution.py:17
  112.5 13.4 %collective-permute-done.4 = bf16[2,1,320,240]{3,2,1,0:T(8,128)(2,1)S(1)} collective-permute-done((bf16[2,1,320,240]{3,2,1,0:T(8,128)(2,1)S(1)}, bf16[2,1,320,240]{3,2,1,0:T(8,128)(2,1)S(1)}, u32[]{:S(2)}, u32[]{:S(2)}) %collective-permute-start.4) | collective-permute-done | bytes 307232 | tf_op jit(solution)/shard_map/ppermute | solution.py:19
  131.3 3.4 %psum.44 = f32[2,4,2,240]{3,1,2,0:T(4,128)S(1)} all-reduce(f32[2,4,2,240]{3,1,2,0:T(4,128)S(1)} %convolution_bitcast_fusion.4), channel_id=1, replica_groups=mesh['comp'=4,'band'=64,'cores'=2] {'cores'}, use_global_device_ids=true, to_apply=%region_2.3 | all-reduce | flops 3840 | bytes 30720 | tf_op jit(solution)/shard_map/psum | solution.py:87
  134.7 16.2 %psum.45 = f32[2,4,2,240]{3,1,2,0:T(4,128)S(1)} all-reduce(f32[2,4,2,240]{3,1,2,0:T(4,128)S(1)} %broadcast_select_fusion.3), channel_id=1, replica_groups=mesh['comp'=4,'band'=64,'cores'=2] {'comp'}, use_global_device_ids=true, to_apply=%region_3.4 | all-reduce | flops 3840 | bytes 30720 | tf_op jit(solution)/shard_map/psum | solution.py:28
  150.9 2.7 %fusion.43 = (bf16[2,2,160,240]{3,2,1,0:T(8,128)(2,1)S(1)}, bf16[2,2,160,240]{3,2,1,0:T(8,128)(2,1)}) fusion(bf16[2,2,160,240]{3,2,1,0:T(8,128)(2,1)S(1)} %collective-permute-done.5, pred[]{:T(512)S(6)} %eq.5, bf16[2,2,160,240]{3,2,1,0:T(8,128)(2,1)} %copy-done.9, f32[2,4,2,240]{3,1,2,0:T(4,128)S(1)} %multiply_add_fusion, f32[4,160]{1,0:T(4,128)S(1)} %copy-done), kind=kOutput, calls=%fused_computation.67 | convolution fusion | flops 8908800 | bytes 1246721 | tf_op jit(solution)/shard_map/fjrq,jo->froq/dot_general | solution.py:80
  153.6 2.3 %all_gather.11 = bf16[2,2,320,240]{3,2,1,0:T(8,128)(2,1)S(1)} all-gather(bf16[2,2,160,240]{3,2,1,0:T(8,128)(2,1)S(1)} %get-tuple-element.33), channel_id=1, replica_groups=mesh['comp'=4,'band'=64,'cores'=2] {'cores'}, dimensions={2}, use_global_device_ids=true | all-gather | bytes 921600 | tf_op jit(solution)/shard_map/all_gather | solution.py:59
  156.7 1.9 collective-permute-start.6
  158.7 3.9 %collective-permute-start.7 = (bf16[2,1,320,240]{3,2,1,0:T(8,128)(2,1)}, bf16[2,1,320,240]{3,2,1,0:T(8,128)(2,1)S(1)}, u32[]{:S(2)}, u32[]{:S(2)}) collective-permute-start(bf16[2,1,320,240]{3,2,1,0:T(8,128)(2,1)} %get-tuple-element.16), channel_id=1, source_target_pairs={{2,0},{4,2},{6,4},{8,6},{10,8},{12,10},{14,12},{16,14},{18,16},{20... | collective-permute-start | bytes 921608 | tf_op jit(solution)/shard_map/ppermute | solution.py:19
  165.0 4.5 %collective-permute-done.6 = bf16[2,1,320,240]{3,2,1,0:T(8,128)(2,1)} collective-permute-done((bf16[2,1,320,240]{3,2,1,0:T(8,128)(2,1)}, bf16[2,1,320,240]{3,2,1,0:T(8,128)(2,1)}, u32[]{:S(2)}, u32[]{:S(2)}) %collective-permute-start.6) | collective-permute-done | bytes 307232 | tf_op jit(solution)/shard_map/ppermute | solution.py:17
  169.5 14.1 %collective-permute-done.7 = bf16[2,1,320,240]{3,2,1,0:T(8,128)(2,1)S(1)} collective-permute-done((bf16[2,1,320,240]{3,2,1,0:T(8,128)(2,1)}, bf16[2,1,320,240]{3,2,1,0:T(8,128)(2,1)S(1)}, u32[]{:S(2)}, u32[]{:S(2)}) %collective-permute-start.7) | collective-permute-done | bytes 307232 | tf_op jit(solution)/shard_map/ppermute | solution.py:19
  191.7 3.4 %psum.46 = f32[2,4,2,240]{3,1,2,0:T(4,128)S(1)} all-reduce(f32[2,4,2,240]{3,1,2,0:T(4,128)S(1)} %convolution_bitcast_fusion.3), channel_id=1, replica_groups=mesh['comp'=4,'band'=64,'cores'=2] {'cores'}, use_global_device_ids=true, to_apply=%region_4.5 | all-reduce | flops 3840 | bytes 30720 | tf_op jit(solution)/shard_map/psum | solution.py:87
  195.1 16.0 %psum.47 = f32[2,4,2,240]{3,1,2,0:T(4,128)S(1)} all-reduce(f32[2,4,2,240]{3,1,2,0:T(4,128)S(1)} %broadcast_select_fusion.2), channel_id=1, replica_groups=mesh['comp'=4,'band'=64,'cores'=2] {'comp'}, use_global_device_ids=true, to_apply=%region_5.6 | all-reduce | flops 3840 | bytes 30720 | tf_op jit(solution)/shard_map/psum | solution.py:28
  (83 shorter events, 31.2 us)
Async XLA Ops:
  0.6 1.8 copy-start
  2.4 2.5 %copy-start.9 = (bf16[2,2,160,240]{3,2,1,0:T(8,128)(2,1)}, bf16[2,2,160,240]{3,2,1,0:T(8,128)(2,1)S(1)}, u32[]{:S(2)}) copy-start(bf16[2,2,160,240]{3,2,1,0:T(8,128)(2,1)S(1)} %reshape_squeeze.6) | copy-start | bytes 921604
  8.0 49.4 %collective-permute-start = (bf16[2,1,320,240]{3,2,1,0:T(8,128)(2,1)}, bf16[2,1,320,240]{3,2,1,0:T(8,128)(2,1)}, u32[]{:S(2)}, u32[]{:S(2)}) collective-permute-start(bf16[2,1,320,240]{3,2,1,0:T(8,128)(2,1)} %get-tuple-element.19), channel_id=1, source_target_pairs={{0,2},{2,4},{4,6},{6,8},{8,10},{10,12},{12,14},{14,16},{16,18},{18... | collective-permute-start | bytes 921608 | tf_op jit(solution)/shard_map/ppermute | solution.py:17
  18.2 39.3 %collective-permute-start.1 = (bf16[2,1,320,240]{3,2,1,0:T(8,128)(2,1)}, bf16[2,1,320,240]{3,2,1,0:T(8,128)(2,1)}, u32[]{:S(2)}, u32[]{:S(2)}) collective-permute-start(bf16[2,1,320,240]{3,2,1,0:T(8,128)(2,1)} %get-tuple-element.20), channel_id=1, source_target_pairs={{2,0},{4,2},{6,4},{8,6},{10,8},{12,10},{14,12},{16,14},{18,16},{20... | collective-permute-start | bytes 921608 | tf_op jit(solution)/shard_map/ppermute | solution.py:19
  41.9 2.6 %copy-start.13 = (s32[4]{0:T(128)S(1)}, s32[4]{0:T(128)}, u32[]{:S(2)}) copy-start(s32[4]{0:T(128)} %param.12) | copy-start | bytes 52
  41.9 10.9 %copy-start.14 = (f32[1000]{0:T(1024)S(1)}, f32[1000]{0:T(1024)}, u32[]{:S(2)}) copy-start(f32[1000]{0:T(1024)} %param.13) | copy-start | bytes 12004
  57.4 1.9 copy-start.2
  59.3 0.9 copy-start.3
  60.3 0.9 copy-start.1
  63.3 1.4 copy-start.5
  64.7 3.9 %copy-start.11 = (bf16[160,4]{0,1:T(4,128)(2,1)S(1)}, bf16[160,4]{0,1:T(4,128)(2,1)}, u32[]{:S(2)}) copy-start(bf16[160,4]{0,1:T(4,128)(2,1)} %param.11) | copy-start | bytes 3844
  64.7 24.3 %copy-start.10 = (bf16[2,2,160,240]{3,2,1,0:T(8,128)(2,1)S(1)}, bf16[2,2,160,240]{3,2,1,0:T(8,128)(2,1)}, u32[]{:S(2)}) copy-start(bf16[2,2,160,240]{3,2,1,0:T(8,128)(2,1)} %copy-done.9) | copy-start | bytes 921604
  64.7 24.3 %copy-start.12 = (f32[2,4,2,240]{3,2,1,0:T(2,128)S(1)}, f32[2,4,2,240]{3,2,1,0:T(2,128)}, u32[]{:S(2)}) copy-start(f32[2,4,2,240]{3,2,1,0:T(2,128)} %param.7) | copy-start | bytes 46084
  65.2 23.8 %collective-permute-start.2 = (bf16[2,2,160,240]{3,2,1,0:T(8,128)(2,1)S(1)}, bf16[2,2,160,240]{3,2,1,0:T(8,128)(2,1)S(1)}, u32[]{:S(2)}, u32[]{:S(2)}) collective-permute-start(bf16[2,2,160,240]{3,2,1,0:T(8,128)(2,1)S(1)} %fusion.30), channel_id=1, source_target_pairs={{0,128},{128,256},{256,384},{1,129},{129,257},{257,385},{2,130},{1... | collective-permute-start | bytes 921608 | tf_op jit(solution)/shard_map/ppermute | solution.py:34
  89.9 16.5 %copy-start.4 = (bf16[160,1,1,320]{3,2,1,0:T(2,128)(2,1)S(1)}, bf16[160,1,1,320]{3,2,1,0:T(2,128)(2,1)}, u32[]{:S(2)}) copy-start(bf16[160,1,1,320]{3,2,1,0:T(2,128)(2,1)} %get-tuple-element.9) | copy-start | bytes 307204
  92.4 20.2 %collective-permute-start.3 = (bf16[2,1,320,240]{3,2,1,0:T(8,128)(2,1)S(1)}, bf16[2,1,320,240]{3,2,1,0:T(8,128)(2,1)S(1)}, u32[]{:S(2)}, u32[]{:S(2)}) collective-permute-start(bf16[2,1,320,240]{3,2,1,0:T(8,128)(2,1)S(1)} %get-tuple-element.17), channel_id=1, source_target_pairs={{0,2},{2,4},{4,6},{6,8},{8,10},{10,12},{12,14},{14,16},{16,18},{18... | collective-permute-start | bytes 921608 | tf_op jit(solution)/shard_map/ppermute | solution.py:17
  102.3 23.6 %collective-permute-start.4 = (bf16[2,1,320,240]{3,2,1,0:T(8,128)(2,1)S(1)}, bf16[2,1,320,240]{3,2,1,0:T(8,128)(2,1)S(1)}, u32[]{:S(2)}, u32[]{:S(2)}) collective-permute-start(bf16[2,1,320,240]{3,2,1,0:T(8,128)(2,1)S(1)} %get-tuple-element.18), channel_id=1, source_target_pairs={{2,0},{4,2},{6,4},{8,6},{10,8},{12,10},{14,12},{16,14},{18,16},{20... | collective-permute-start | bytes 921608 | tf_op jit(solution)/shard_map/ppermute | solution.py:19
  129.8 21.1 %collective-permute-start.5 = (bf16[2,2,160,240]{3,2,1,0:T(8,128)(2,1)S(1)}, bf16[2,2,160,240]{3,2,1,0:T(8,128)(2,1)S(1)}, u32[]{:S(2)}, u32[]{:S(2)}) collective-permute-start(bf16[2,2,160,240]{3,2,1,0:T(8,128)(2,1)S(1)} %fusion.29), channel_id=1, source_target_pairs={{0,128},{128,256},{256,384},{1,129},{129,257},{257,385},{2,130},{1... | collective-permute-start | bytes 921608 | tf_op jit(solution)/shard_map/ppermute | solution.py:34
  150.9 2.7 %copy-start.6 = (bf16[2,2,160,240]{3,2,1,0:T(8,128)(2,1)}, bf16[2,2,160,240]{3,2,1,0:T(8,128)(2,1)S(1)}, u32[]{:S(2)}) copy-start(bf16[2,2,160,240]{3,2,1,0:T(8,128)(2,1)S(1)} %collective-permute-done.5) | copy-start | bytes 921604
  156.7 12.8 %collective-permute-start.6 = (bf16[2,1,320,240]{3,2,1,0:T(8,128)(2,1)}, bf16[2,1,320,240]{3,2,1,0:T(8,128)(2,1)}, u32[]{:S(2)}, u32[]{:S(2)}) collective-permute-start(bf16[2,1,320,240]{3,2,1,0:T(8,128)(2,1)} %get-tuple-element.15), channel_id=1, source_target_pairs={{0,2},{2,4},{4,6},{6,8},{8,10},{10,12},{12,14},{14,16},{16,18},{18... | collective-permute-start | bytes 921608 | tf_op jit(solution)/shard_map/ppermute | solution.py:17
  158.7 25.0 %collective-permute-start.7 = (bf16[2,1,320,240]{3,2,1,0:T(8,128)(2,1)}, bf16[2,1,320,240]{3,2,1,0:T(8,128)(2,1)S(1)}, u32[]{:S(2)}, u32[]{:S(2)}) collective-permute-start(bf16[2,1,320,240]{3,2,1,0:T(8,128)(2,1)} %get-tuple-element.16), channel_id=1, source_target_pairs={{2,0},{4,2},{6,4},{8,6},{10,8},{12,10},{14,12},{16,14},{18,16},{20... | collective-permute-start | bytes 921608 | tf_op jit(solution)/shard_map/ppermute | solution.py:19
  188.6 1.0 copy-start.7
  188.6 1.1 copy-start.8
where the time goes:
time: 213 us; the launch traced here: 212 us
  blocking collectives  66 us (31%)
  waiting for transfers between devices  37.8 us (18%)
  starting transfers between devices  34.4 us (16%)
  other arithmetic  24.5 us (12%)
  matrix products  20.7 us (10%)
  between operations  15.6 us (7%)
  local copies, waits for them, and re-layouts  12.5 us (6%)
    psum x3, blocking collectives, broadcast(): return lax.psum(kept, axis)  49 us
    ppermute x3, waiting for transfers between devices, extended(): lax.ppermute(head, axis, [((i + 1) % count, i) for i in range(ends)])  27.5 us
    ppermute x3, starting transfers between devices, extended(): lax.ppermute(tail, axis, [(i, (i + 1) % count) for i in range(ends)])  22 us
    unnamed x1, other arithmetic  20.1 us
    dot_general x27, matrix products, conv_add(): jnp.einsum('friq,oi->froq', window, weight[:, shift_row, shift_col, :], p...  14.2 us
    ppermute x3, waiting for transfers between devices, extended(): lax.ppermute(tail, axis, [(i, (i + 1) % count) for i in range(ends)])  10.3 us
    psum x3, blocking collectives, body(): noise = lax.psum(partial_noise, 'cores')  10.1 us
    ppermute x3, starting transfers between devices, extended(): lax.ppermute(head, axis, [((i + 1) % count, i) for i in range(ends)])  7.76 us
  transfers between devices with their start and end apart: 8, of which 4 were waited for; matrix products, arithmetic and copies ran while one was open for 13% of the time, Pallas kernels for 0%

commit v1 on v0

v1 whole, which is shorter than its diff:
```python
import functools

import jax
import jax.numpy as jnp
from jax import lax
from jax.experimental import pallas as pl
from jax.experimental.pallas import tpu as pltpu
from jax.sharding import PartitionSpec as P

STEPS = 3
TAPS = 3
LANES = 128
FRAME = 256
MESSAGE_EXTRA = 16
VMEM_BYTES = 48 * 1024 * 1024


def params():
    return pltpu.CompilerParams(vmem_limit_bytes=VMEM_BYTES)


def in_vmem():
    return pl.BlockSpec(memory_space=pltpu.VMEM)


def weight_kernel(flat_ref, out_ref, held):
    lane = lax.broadcasted_iota(jnp.int32, (80, LANES), 1)
    low = lane < 64

    def rows(start):
        return flat_ref[pl.ds(start, 80, stride=45), :]

    def swapped(value):
        return pltpu.roll(value, 64, axis=1)

    for dq in range(TAPS):
        for parity in range(2):
            tails = []
            for dr in range(TAPS):
                start = 45 * parity + 5 * (3 * dr + dq)
                place, half = start // 2, start % 2
                first, second, third = (rows(place + n) for n in range(3))
                if half:
                    one = swapped(jnp.where(low, second, first))
                    two = swapped(jnp.where(low, third, second))
                    tail_low = False
                else:
                    one, two = first, second
                    tail_low = True
                held[2 * dr, pl.ds(parity, 80, stride=2), :] = one
                held[2 * dr + 1, pl.ds(parity, 80, stride=2), :] = two
                wants_low = dr != 1
                tails.append(third if tail_low == wants_low else swapped(third))
            held[6, pl.ds(parity, 80, stride=2), :] = jnp.where(low, tails[0], tails[1])
            held[7, pl.ds(parity, 80, stride=2), :] = tails[2]
        at = dq * 160
        for tile in range(7):
            out_ref[at : at + 160, tile * LANES : (tile + 1) * LANES] = held[tile].astype(jnp.bfloat16)
        out_ref[at : at + 160, 896:960] = held[7, :, :64].astype(jnp.bfloat16)


def prepare_kernel(core, feat_ref, latent_ref, own_ref, message_ref, state_ref):
    own_ref[...] = jnp.zeros_like(own_ref)
    state_ref[...] = jnp.zeros_like(state_ref)
    for half in range(2):
        for frame in range(2):
            for row in range(2):
                own_ref[row, half * 160 : half * 160 + 160, frame * FRAME : frame * FRAME + 240] = feat_ref[
                    half, frame, row
                ]
    for frame in range(2):
        for row in range(2):
            state_ref[row, 0:4, frame * FRAME : frame * FRAME + 240] = latent_ref[frame, :, row, :]
    me = core()
    message_ref[0:320, :] = own_ref[me]
    state = state_ref[me, 0:4, :]
    high = state.astype(jnp.bfloat16).astype(jnp.float32)
    left = state - high
    middle = left.astype(jnp.bfloat16).astype(jnp.float32)
    low = left - middle
    parts = jnp.concatenate([high, middle, low, jnp.zeros_like(low)], axis=0)
    message_ref[320:336, :] = parts.astype(jnp.bfloat16)


def step_kernel(
    step,
    core,
    plane,
    coef_ref,
    rec_ref,
    edge_ref,
    cond_ref,
    cond_edge_ref,
    state_in_ref,
    in_weight_ref,
    out_weight_ref,
    mine_ref,
    other_ref,
    out_ref,
    state_ref,
    final_ref,
    raw,
    active,
    sums,
    mine,
    other,
    sems,
):
    copies = [
        pltpu.make_async_copy(mine_ref, mine, sems.at[0]),
        pltpu.make_async_copy(other_ref, other, sems.at[1]),
    ]
    for copy in copies:
        copy.start()
    me = core()
    at = plane()
    sources = [
        (1 - me, rec_ref.at[0], cond_ref.at[0]),
        (2 - me, rec_ref.at[1], cond_ref.at[1]),
        (2 * me, edge_ref, cond_edge_ref),
    ]
    lanes = lax.broadcasted_iota(jnp.int32, (1, 2 * FRAME), 1)
    inside = (lanes % FRAME) < 240
    rate, scale_now, scale_next = (coef_ref[0, n] for n in range(3))

    @pl.when(at == 0)
    def _():
        for number, (slot, rec, cond) in enumerate(sources):
            if step == 0:
                if number < 2:
                    state = state_in_ref[number]
                else:
                    extra = edge_ref[320:336, :].astype(jnp.float32)
                    state = (extra[0:4] + extra[4:8]) + extra[8:12]
                    state = jnp.concatenate([state, jnp.zeros_like(state)], axis=0)
            else:
                state = state_in_ref[slot]
                noise = jnp.dot(out_weight_ref[...], rec[0:320, :], preferred_element_type=jnp.float32)[0:8]
                state = rate * (state - scale_now * noise) + scale_next * noise
            state_ref[slot] = state
            for chunk in range(0, 320, 32):
                total = cond[chunk : chunk + 32, :].astype(jnp.float32)
                weight = in_weight_ref[chunk : chunk + 32, :]
                proj = weight[:, 0:1] * state[0:1, :]
                for latent in range(1, 4):
                    proj = proj + weight[:, latent : latent + 1] * state[latent : latent + 1, :]
                raw[slot, chunk : chunk + 32, :] = (proj + total).astype(jnp.bfloat16)

    @pl.when(at != 0)
    def _():
        state_ref[...] = jnp.zeros_like(state_ref)
        for slot, rec, _ in sources:
            raw[slot] = rec[0:320, :]

    for slot in range(3):
        for chunk in range(0, 320, 64):
            value = raw[slot, chunk : chunk + 64, :].astype(jnp.float32)
            value = 0.5 * value * (1.0 + jnp.tanh(0.5 * value))
            place = slot * 256 + chunk if chunk < 256 else 768 + slot * 64
            active[place : place + 64, :] = value.astype(jnp.bfloat16)

    for half, (copy, weight) in enumerate(zip(copies, (mine, other))):
        copy.wait()
        offset = me * 160 if half == 0 else (1 - me) * 160
        sums[...] = jnp.dot(weight[...], active[...], preferred_element_type=jnp.float32)
        for chunk in range(0, 160, 32):
            channels = pl.ds(pl.multiple_of(offset + chunk, 32), 32)
            total = sums[160 + chunk : 160 + chunk + 32, :]
            total = total + pltpu.roll(sums[chunk : chunk + 32, :], 1, axis=1)
            total = total + pltpu.roll(sums[320 + chunk : 320 + chunk + 32, :], 2 * FRAME - 1, axis=1)
            total = total + raw[1, channels, :].astype(jnp.float32)
            out_ref[channels, :] = jnp.where(inside, total, 0.0).astype(jnp.bfloat16)

    if step == STEPS - 1:
        rate, scale_now, scale_next = (coef_ref[1, n] for n in range(3))
        final_ref[...] = rate * state_ref[1]

        @pl.when(at == 3)
        def _():
            noise = jnp.dot(out_weight_ref[...], out_ref[...], preferred_element_type=jnp.float32)[0:8]
            final_ref[...] = (scale_next - rate * scale_now) * noise
    else:
        final_ref[...] = jnp.zeros_like(final_ref)


def prepare(feats, latent):
    core = functools.partial(lax.axis_index, "cores")
    return pl.pallas_call(
        functools.partial(prepare_kernel, core),
        out_shape=[
            jax.ShapeDtypeStruct((2, 320, 2 * FRAME), jnp.bfloat16),
            jax.ShapeDtypeStruct((320 + MESSAGE_EXTRA, 2 * FRAME), jnp.bfloat16),
            jax.ShapeDtypeStruct((2, 8, 2 * FRAME), jnp.float32),
        ],
        in_specs=[in_vmem()] * 2,
        out_specs=[in_vmem()] * 3,
        compiler_params=params(),
        name="prepare",
    )(feats, latent)


def relaid_weight(weight):
    flat = lax.optimization_barrier(weight.astype(jnp.float32)).reshape(-1, LANES)
    return pl.pallas_call(
        weight_kernel,
        out_shape=jax.ShapeDtypeStruct((480, 960), jnp.bfloat16),
        in_specs=[in_vmem()],
        out_specs=in_vmem(),
        scratch_shapes=[pltpu.VMEM((8, 160, LANES), jnp.float32)],
        compiler_params=params(),
        name="relay",
    )(flat)


def run_step(step, coefs, rec, edge, cond, cond_edge, state, in_weight, out_weight, mine, other):
    core = functools.partial(lax.axis_index, "cores")
    plane = functools.partial(lax.axis_index, "comp")
    return pl.pallas_call(
        functools.partial(step_kernel, step, core, plane),
        out_shape=[
            jax.ShapeDtypeStruct((320, 2 * FRAME), jnp.bfloat16),
            jax.ShapeDtypeStruct((3, 8, 2 * FRAME), jnp.float32),
            jax.ShapeDtypeStruct((8, 2 * FRAME), jnp.float32),
        ],
        in_specs=[pl.BlockSpec(memory_space=pltpu.SMEM)] + [in_vmem()] * 7 + [pl.BlockSpec(memory_space=pl.ANY)] * 2,
        out_specs=[in_vmem()] * 3,
        scratch_shapes=[
            pltpu.VMEM((3, 320, 2 * FRAME), jnp.bfloat16),
            pltpu.VMEM((960, 2 * FRAME), jnp.bfloat16),
            pltpu.VMEM((480, 2 * FRAME), jnp.float32),
            pltpu.VMEM((480, 960), jnp.bfloat16),
            pltpu.VMEM((480, 960), jnp.bfloat16),
            pltpu.SemaphoreType.DMA((2,)),
        ],
        compiler_params=params(),
        name=f"step{step}",
    )(coefs, rec, edge, cond, cond_edge, state, in_weight, out_weight, mine, other)


def links(comps, bands):
    def index(comp, band, core):
        return (comp * bands + band) * 2 + core

    edges, diagonals, onward, swap = [], [], [], []
    for comp in range(comps):
        later = (comp + 1) % comps
        for band in range(bands):
            for core in range(2):
                me = index(comp, band, core)
                onward.append((me, index(later, band, core)))
                swap.append((me, index(comp, band, 1 - core)))
                reached = band + 2 * core - 1
                if 0 <= reached < bands:
                    edges.append((me, index(comp, reached, 1 - core)))
                    diagonals.append((me, index(later, reached, 1 - core)))
    return edges, diagonals, onward, swap


def body(latent, section_inputs, in_weight, conv_weight, out_weight, timesteps, plan):
    axes = ("comp", "band", "cores")
    edges, diagonals, onward, swap = links(lax.axis_size("comp"), lax.axis_size("band"))
    plane = lax.axis_index("comp")
    core = lax.axis_index("cores")

    feats = section_inputs[0].reshape(2, 2, 160, 240)
    feats = lax.all_gather(feats, "cores")
    cond, message, state = prepare(feats, latent)
    cond_edge = lax.ppermute(message, axes, edges)

    mine = relaid_weight(conv_weight)
    other = lax.ppermute(mine, axes, swap)
    small = jnp.concatenate([in_weight, out_weight.T.astype(jnp.float32)], axis=0)
    small = lax.all_gather(small, "cores")
    in_columns = jnp.concatenate([small[0, 0:4], small[1, 0:4]], axis=1).T
    in_columns = jnp.pad(in_columns, ((0, 0), (0, 4)))
    out_rows = jnp.concatenate([small[0, 4:8], small[1, 4:8]], axis=1)
    out_rows = jnp.pad(out_rows, ((0, 12), (0, 0))).astype(jnp.bfloat16)

    alphas = plan[timesteps]
    rates = jnp.sqrt(alphas[1:] / alphas[:-1])
    scales = jnp.sqrt(1.0 - alphas)
    coefs = jnp.stack([rates, scales[:-1], scales[1:]], axis=1)

    rec, edge = cond, cond_edge
    for step in range(STEPS):
        pair = coefs[max(step - 1, 0) : max(step - 1, 0) + 2]
        out, state, final = run_step(
            step, pair, rec, edge, cond, cond_edge, state, in_columns, out_rows, mine, other
        )
        if step + 1 < STEPS:
            edge = lax.ppermute(out, axes, diagonals)
            rec = lax.all_gather(lax.ppermute(out, axes, onward), "cores")

    whole = lax.all_gather(out, "cores")
    share = lax.dynamic_slice_in_dim(whole, core * 160, 160, axis=1)
    share = share.reshape(2, 160, 2, FRAME)[..., :240].transpose(2, 0, 1, 3)
    handoff = share.reshape(1, 2, 2, 160 * 240)

    total = lax.psum(final[0:4], "comp")
    total = lax.all_gather(lax.dynamic_slice_in_dim(total, plane, 1, axis=0)[0], "cores")
    denoised = total.reshape(2, 2, FRAME)[..., :240].transpose(1, 0, 2)[:, None]
    return denoised, handoff


def solution(mesh):
    in_specs = (
        P(None, None, "band", None),
        P("comp", None, "band", "cores"),
        P(None, "cores"),
        P("comp", "cores"),
        P("cores", None),
        P(),
        P(),
    )
    out_specs = (P(None, "comp", "band", None), P("comp", None, "band", "cores"))
    return jax.shard_map(body, mesh=mesh, in_specs=in_specs, out_specs=out_specs, check_vma=False)
```

time: 213 us -> 121 us (0.57)
  the two profiles are of different devices: /device:TPU:62 before, /device:TPU:63 now
where the time goes in v1:
time: 121 us; the launch traced here: 120 us
  waiting for transfers between devices  41.9 us (35%)
  starting transfers between devices  27.2 us (22%)
  blocking collectives  23.4 us (19%)
  Pallas kernels  15.3 us (13%)
  local copies, waits for them, and re-layouts  7.65 us (6%)
  other arithmetic  3.89 us (3%)
    ppermute x2, waiting for transfers between devices, body(): rec = lax.all_gather(lax.ppermute(out, axes, onward), 'cores')  41.9 us
    pallas_call x3, Pallas kernels, run_step(): pl.pallas_call(functools.partial(step_kernel, step, core, plane), out_sha...  14 us
    ppermute x2, starting transfers between devices, body(): edge = lax.ppermute(out, axes, diagonals)  10.9 us
    ppermute x1, starting transfers between devices, body(): cond_edge = lax.ppermute(message, axes, edges)  10.1 us
    psum x1, blocking collectives, body(): total = lax.psum(final[0:4], 'comp')  6.78 us
    all_gather x2, blocking collectives, body(): rec = lax.all_gather(lax.ppermute(out, axes, onward), 'cores')  6.21 us
    ppermute x2, starting transfers between devices, body(): rec = lax.all_gather(lax.ppermute(out, axes, onward), 'cores')  4.23 us
    all_gather x1, blocking collectives, body(): lax.all_gather(lax.dynamic_slice_in_dim(total, plane, 1, axis=0)[0], 'cor...  3.59 us
  transfers between devices with their start and end apart: 6, of which 2 were waited for; matrix products, arithmetic and copies ran while one was open for 4% of the time, Pallas kernels for 0%

profile of v1, /device:TPU:63, one launch (start us, length us, event | category | flops | bytes accessed | tf_op | source)
XLA Modules:
  0.0 120.3 jit_solution(10936078939411360449)
XLA Ops:
  0.6 1.7 %all_gather_reshape_squeeze.3 = bf16[1,2,2,160,240]{4,3,2,1,0:T(8,128)(2,1)S(1)} reshape(bf16[1,2,2,38400]{3,2,1,0:T(2,128)(2,1)} %param.8) | data formatting | bytes 614400 | tf_op jit(solution)/shard_map/all_gather;reshape;squeeze | solution.py:266
  2.4 2.6 %all_gather.30.feat_ref = bf16[2,2,2,160,240]{4,3,2,1,0:T(8,128)(2,1)S(1)} all-gather(bf16[1,2,2,160,240]{4,3,2,1,0:T(8,128)(2,1)S(1)} %all_gather_reshape_squeeze.3), channel_id=1, replica_groups=mesh['comp'=4,'band'=64,'cores'=2] {'cores'}, dimensions={0}, use_global_device_ids=true | all-gather | bytes 921600 | tf_op jit(solution)/shard_map/all_gather | solution.py:266
  5.7 0.8 prepare.1
  6.5 10.1 %collective-permute-start = (bf16[336,512]{1,0:T(8,128)(2,1)}, bf16[336,512]{1,0:T(8,128)(2,1)S(1)}, u32[]{:S(2)}, u32[]{:S(2)}) collective-permute-start(bf16[336,512]{1,0:T(8,128)(2,1)} %get-tuple-element.12), channel_id=1, source_target_pairs={{1,2},{2,1},{3,4},{4,3},{5,6},{6,5},{7,8},{8,7},{9,10},{10,9},{11,... | collective-permute-start | bytes 1032200 | tf_op jit(solution)/shard_map/ppermute | solution.py:268
  16.6 3.5 %convert_element_type.16 = f32[1,460800]{1,0:T(1,128)S(1)} convert(bf16[1,460800]{1,0:T(2,128)(2,1)} %param.10) | non-fusion elementwise | flops 460800 | bytes 2764800 | tf_op jit(solution)/shard_map/convert_element_type | solution.py:203
  20.7 1.9 %collective-permute-start.1 = (bf16[480,960]{1,0:T(8,128)(2,1)S(1)}, bf16[480,960]{1,0:T(8,128)(2,1)S(1)}, u32[]{:S(2)}, u32[]{:S(2)}) collective-permute-start(bf16[480,960]{1,0:T(8,128)(2,1)S(1)} %relay.1.mine_ref), channel_id=1, source_target_pairs={{0,1},{1,0},{2,3},{3,2},{4,5},{5,4},{6,7},{7,6},{8,9},{9,8},{10,11... | collective-permute-start | bytes 2764808 | tf_op jit(solution)/shard_map/ppermute | solution.py:271
  23.5 2.0 %all-gather = f32[16,160]{1,0:T(8,128)S(1)} all-gather(f32[8,160]{1,0:T(8,128)S(1)} %pad_maximum_fusion), channel_id=2, replica_groups=mesh['comp'=4,'band'=64,'cores'=2] {'cores'}, dimensions={0}, use_global_device_ids=true | all-gather | bytes 15360 | tf_op jit(solution)/shard_map/all_gather | solution.py:273
  26.2 4.6 %step0.1 = (bf16[320,512]{1,0:T(8,128)(2,1)S(1)}, f32[3,8,512]{2,1,0:T(8,128)S(1)}, f32[8,512]{1,0:T(8,128)}) custom-call(f32[2,3]{1,0:T(2,128)S(1)} %get-tuple-element.30.coef_ref, bf16[2,320,512]{2,1,0:T(8,128)(2,1)S(1)} %get-tuple-element.11.rec_ref.cond_ref, bf16[336,512]{1,0:T(8,128)(2,1)S(1)} %collective-permute-done.edge_ref.cond_edge_ref, ...), custom_call_target="tpu_custom_call" | custom-call | tf_op jit(solution)/shard_map/step0/pallas_call | solution.py:218
  30.8 2.3 %collective-permute-start.2 = (bf16[320,512]{1,0:T(8,128)(2,1)S(1)}, bf16[320,512]{1,0:T(8,128)(2,1)S(1)}, u32[]{:S(2)}, u32[]{:S(2)}) collective-permute-start(bf16[320,512]{1,0:T(8,128)(2,1)S(1)} %get-tuple-element.14), channel_id=1, source_target_pairs={{0,128},{1,129},{2,130},{3,131},{4,132},{5,133},{6,134},{7,135},{8... | collective-permute-start | bytes 983048 | tf_op jit(solution)/shard_map/ppermute | solution.py:292
  33.1 9.0 %collective-permute-start.3 = (bf16[320,512]{1,0:T(8,128)(2,1)S(1)}, bf16[320,512]{1,0:T(8,128)(2,1)S(1)}, u32[]{:S(2)}, u32[]{:S(2)}) collective-permute-start(bf16[320,512]{1,0:T(8,128)(2,1)S(1)} %get-tuple-element.14), channel_id=1, source_target_pairs={{1,130},{2,129},{3,132},{4,131},{5,134},{6,133},{7,136},{8,135},{9... | collective-permute-start | bytes 983048 | tf_op jit(solution)/shard_map/ppermute | solution.py:291
  42.1 19.0 %collective-permute-done.2 = bf16[320,512]{1,0:T(8,128)(2,1)S(1)} collective-permute-done((bf16[320,512]{1,0:T(8,128)(2,1)S(1)}, bf16[320,512]{1,0:T(8,128)(2,1)S(1)}, u32[]{:S(2)}, u32[]{:S(2)}) %collective-permute-start.2) | collective-permute-done | bytes 327712 | tf_op jit(solution)/shard_map/ppermute | solution.py:292
  61.1 3.3 %all-gather.1 = bf16[640,512]{1,0:T(8,128)(2,1)S(1)} all-gather(bf16[320,512]{1,0:T(8,128)(2,1)S(1)} %collective-permute-done.2), channel_id=3, replica_groups=mesh['comp'=4,'band'=64,'cores'=2] {'cores'}, dimensions={0}, use_global_device_ids=true | all-gather | bytes 983040 | tf_op jit(solution)/shard_map/all_gather | solution.py:292
  64.5 4.8 %step1.1 = (bf16[320,512]{1,0:T(8,128)(2,1)}, f32[3,8,512]{2,1,0:T(8,128)S(1)}, f32[8,512]{1,0:T(8,128)}) custom-call(f32[2,3]{1,0:T(2,128)S(1)} %get-tuple-element.30.coef_ref, bf16[2,320,512]{2,1,0:T(8,128)(2,1)S(1)} %bitcast.36, bf16[320,512]{1,0:T(8,128)(2,1)S(1)} %collective-permute-done.3.edge_ref, ...), custom_call_target="tpu_custom_call" | custom-call | tf_op jit(solution)/shard_map/step1/pallas_call | solution.py:218
  69.2 1.9 %collective-permute-start.4 = (bf16[320,512]{1,0:T(8,128)(2,1)}, bf16[320,512]{1,0:T(8,128)(2,1)}, u32[]{:S(2)}, u32[]{:S(2)}) collective-permute-start(bf16[320,512]{1,0:T(8,128)(2,1)} %get-tuple-element.16), channel_id=1, source_target_pairs={{0,128},{1,129},{2,130},{3,131},{4,132},{5,133},{6,134},{7,135},{8... | collective-permute-start | bytes 983048 | tf_op jit(solution)/shard_map/ppermute | solution.py:292
  71.1 1.9 %collective-permute-start.5 = (bf16[320,512]{1,0:T(8,128)(2,1)}, bf16[320,512]{1,0:T(8,128)(2,1)S(1)}, u32[]{:S(2)}, u32[]{:S(2)}) collective-permute-start(bf16[320,512]{1,0:T(8,128)(2,1)} %get-tuple-element.16), channel_id=1, source_target_pairs={{1,130},{2,129},{3,132},{4,131},{5,134},{6,133},{7,136},{8,135},{9... | collective-permute-start | bytes 983048 | tf_op jit(solution)/shard_map/ppermute | solution.py:291
  73.1 22.9 %collective-permute-done.4 = bf16[320,512]{1,0:T(8,128)(2,1)} collective-permute-done((bf16[320,512]{1,0:T(8,128)(2,1)}, bf16[320,512]{1,0:T(8,128)(2,1)}, u32[]{:S(2)}, u32[]{:S(2)}) %collective-permute-start.4) | collective-permute-done | bytes 327712 | tf_op jit(solution)/shard_map/ppermute | solution.py:292
  96.0 2.9 %all-gather.2 = bf16[640,512]{1,0:T(8,128)(2,1)S(1)} all-gather(bf16[320,512]{1,0:T(8,128)(2,1)} %collective-permute-done.4), channel_id=4, replica_groups=mesh['comp'=4,'band'=64,'cores'=2] {'cores'}, dimensions={0}, use_global_device_ids=true | all-gather | bytes 983040 | tf_op jit(solution)/shard_map/all_gather | solution.py:292
  98.9 0.7 copy-done.1
  99.6 1.0 copy-done.2
  100.6 4.7 %step2.1 = (bf16[320,512]{1,0:T(8,128)(2,1)S(1)}, f32[3,8,512]{2,1,0:T(8,128)}, f32[8,512]{1,0:T(8,128)S(1)}) custom-call(f32[2,3]{1,0:T(2,128)S(1)} %get-tuple-element.31.coef_ref, bf16[2,320,512]{2,1,0:T(8,128)(2,1)S(1)} %bitcast.35, bf16[320,512]{1,0:T(8,128)(2,1)S(1)} %copy-done.2, bf16[2,320,512]{2,1,0:T(8,128)(2,1)S(1)} %get-tuple-element.11.rec_ref.cond_ref, ...), custom_call_target="tpu_custom_call" | custom-call | tf_op jit(solution)/shard_map/step2/pallas_call | solution.py:218
  105.3 6.8 %psum.7 = f32[4,512]{1,0:T(4,128)S(1)} all-reduce(f32[4,512]{1,0:T(4,128)S(1)} %slice.52), channel_id=1, replica_groups=mesh['comp'=4,'band'=64,'cores'=2] {'comp'}, use_global_device_ids=true, to_apply=%region_0.1 | all-reduce | flops 2048 | bytes 16384 | tf_op jit(solution)/shard_map/psum | solution.py:299
  112.1 3.6 %all-gather.4 = f32[2,1,512]{2,1,0:T(1,128)S(1)} all-gather(f32[1,1,512]{2,1,0:T(1,128)S(1)} %dynamic-slice_bitcast_fusion), channel_id=1, replica_groups=mesh['comp'=4,'band'=64,'cores'=2] {'cores'}, dimensions={0}, use_global_device_ids=true | all-gather | bytes 6144 | tf_op jit(solution)/shard_map/all_gather | solution.py:300
  116.3 2.3 %all-gather.3 = bf16[640,512]{1,0:T(8,128)(2,1)S(1)} all-gather(bf16[320,512]{1,0:T(8,128)(2,1)S(1)} %get-tuple-element.19), channel_id=5, replica_groups=mesh['comp'=4,'band'=64,'cores'=2] {'cores'}, dimensions={0}, use_global_device_ids=true | all-gather | bytes 983040 | tf_op jit(solution)/shard_map/all_gather | solution.py:294
  119.0 1.4 %reshape.19 = bf16[1,2,2,38400]{3,2,1,0:T(2,128)(2,1)} reshape(bf16[2,2,160,240]{3,2,1,0:T(8,128)(2,1)S(1)} %copy.36) | data formatting | bytes 614400 | tf_op jit(solution)/shard_map/reshape | solution.py:297
  (47 shorter events, 3.8 us)
Async XLA Ops:
  0.6 22.1 %copy-start = (f32[1000]{0:T(1024)S(1)}, f32[1000]{0:T(1024)}, u32[]{:S(2)}) copy-start(f32[1000]{0:T(1024)} %param.13) | copy-start | bytes 12004
  4.9 0.7 copy-start.3
  6.5 19.7 %collective-permute-start = (bf16[336,512]{1,0:T(8,128)(2,1)}, bf16[336,512]{1,0:T(8,128)(2,1)S(1)}, u32[]{:S(2)}, u32[]{:S(2)}) collective-permute-start(bf16[336,512]{1,0:T(8,128)(2,1)} %get-tuple-element.12), channel_id=1, source_target_pairs={{1,2},{2,1},{3,4},{4,3},{5,6},{6,5},{7,8},{8,7},{9,10},{10,9},{11,... | collective-permute-start | bytes 1032200 | tf_op jit(solution)/shard_map/ppermute | solution.py:268
  20.1 2.5 %copy-start.6 = (s32[4]{0:T(128)S(1)}, s32[4]{0:T(128)}, u32[]{:S(2)}) copy-start(s32[4]{0:T(128)} %param.12) | copy-start | bytes 52
  20.2 3.3 %copy-start.5 = (bf16[160,4]{0,1:T(4,128)(2,1)S(1)}, bf16[160,4]{0,1:T(4,128)(2,1)}, u32[]{:S(2)}) copy-start(bf16[160,4]{0,1:T(4,128)(2,1)} %param.11) | copy-start | bytes 3844
  20.2 3.3 %copy-start.4 = (f32[4,160]{1,0:T(4,128)S(1)}, f32[4,160]{1,0:T(4,128)}, u32[]{:S(2)}) copy-start(f32[4,160]{1,0:T(4,128)} %param.9) | copy-start | bytes 7684
  20.7 5.5 %collective-permute-start.1 = (bf16[480,960]{1,0:T(8,128)(2,1)S(1)}, bf16[480,960]{1,0:T(8,128)(2,1)S(1)}, u32[]{:S(2)}, u32[]{:S(2)}) collective-permute-start(bf16[480,960]{1,0:T(8,128)(2,1)S(1)} %relay.1.mine_ref), channel_id=1, source_target_pairs={{0,1},{1,0},{2,3},{3,2},{4,5},{5,4},{6,7},{7,6},{8,9},{9,8},{10,11... | collective-permute-start | bytes 2764808 | tf_op jit(solution)/shard_map/ppermute | solution.py:271
  30.8 30.3 %collective-permute-start.2 = (bf16[320,512]{1,0:T(8,128)(2,1)S(1)}, bf16[320,512]{1,0:T(8,128)(2,1)S(1)}, u32[]{:S(2)}, u32[]{:S(2)}) collective-permute-start(bf16[320,512]{1,0:T(8,128)(2,1)S(1)} %get-tuple-element.14), channel_id=1, source_target_pairs={{0,128},{1,129},{2,130},{3,131},{4,132},{5,133},{6,134},{7,135},{8... | collective-permute-start | bytes 983048 | tf_op jit(solution)/shard_map/ppermute | solution.py:292
  33.1 31.3 %collective-permute-start.3 = (bf16[320,512]{1,0:T(8,128)(2,1)S(1)}, bf16[320,512]{1,0:T(8,128)(2,1)S(1)}, u32[]{:S(2)}, u32[]{:S(2)}) collective-permute-start(bf16[320,512]{1,0:T(8,128)(2,1)S(1)} %get-tuple-element.14), channel_id=1, source_target_pairs={{1,130},{2,129},{3,132},{4,131},{5,134},{6,133},{7,136},{8,135},{9... | collective-permute-start | bytes 983048 | tf_op jit(solution)/shard_map/ppermute | solution.py:291
  69.2 26.8 %collective-permute-start.4 = (bf16[320,512]{1,0:T(8,128)(2,1)}, bf16[320,512]{1,0:T(8,128)(2,1)}, u32[]{:S(2)}, u32[]{:S(2)}) collective-permute-start(bf16[320,512]{1,0:T(8,128)(2,1)} %get-tuple-element.16), channel_id=1, source_target_pairs={{0,128},{1,129},{2,130},{3,131},{4,132},{5,133},{6,134},{7,135},{8... | collective-permute-start | bytes 983048 | tf_op jit(solution)/shard_map/ppermute | solution.py:292
  71.1 27.8 %collective-permute-start.5 = (bf16[320,512]{1,0:T(8,128)(2,1)}, bf16[320,512]{1,0:T(8,128)(2,1)S(1)}, u32[]{:S(2)}, u32[]{:S(2)}) collective-permute-start(bf16[320,512]{1,0:T(8,128)(2,1)} %get-tuple-element.16), channel_id=1, source_target_pairs={{1,130},{2,129},{3,132},{4,131},{5,134},{6,133},{7,136},{8,135},{9... | collective-permute-start | bytes 983048 | tf_op jit(solution)/shard_map/ppermute | solution.py:291
  98.9 0.7 copy-start.1
  99.6 1.0 copy-start.2

commit v2 on v1

--- a/solution.py
+++ b/solution.py
@@ -91,6 +91,8 @@
     edge_ref,
     cond_ref,
     cond_edge_ref,
+    noise_ref,
+    noise_edge_ref,
     state_in_ref,
     in_weight_ref,
     out_weight_ref,
@@ -102,22 +104,13 @@
     raw,
     active,
     sums,
-    mine,
-    other,
-    sems,
 ):
-    copies = [
-        pltpu.make_async_copy(mine_ref, mine, sems.at[0]),
-        pltpu.make_async_copy(other_ref, other, sems.at[1]),
-    ]
-    for copy in copies:
-        copy.start()
     me = core()
     at = plane()
     sources = [
-        (1 - me, rec_ref.at[0], cond_ref.at[0]),
-        (2 - me, rec_ref.at[1], cond_ref.at[1]),
-        (2 * me, edge_ref, cond_edge_ref),
+        (1 - me, rec_ref.at[0], cond_ref.at[0], noise_ref.at[0]),
+        (2 - me, rec_ref.at[1], cond_ref.at[1], noise_ref.at[1]),
+        (2 * me, edge_ref, cond_edge_ref, noise_edge_ref),
     ]
     lanes = lax.broadcasted_iota(jnp.int32, (1, 2 * FRAME), 1)
     inside = (lanes % FRAME) < 240
@@ -125,17 +118,17 @@
 
     @pl.when(at == 0)
     def _():
-        for number, (slot, rec, cond) in enumerate(sources):
+        for number, (slot, _, cond, noise_row) in enumerate(sources):
             if step == 0:
                 if number < 2:
                     state = state_in_ref[number]
                 else:
-                    extra = edge_ref[320:336, :].astype(jnp.float32)
+                    extra = cond_edge_ref[320:336, :].astype(jnp.float32)
                     state = (extra[0:4] + extra[4:8]) + extra[8:12]
                     state = jnp.concatenate([state, jnp.zeros_like(state)], axis=0)
             else:
                 state = state_in_ref[slot]
-                noise = jnp.dot(out_weight_ref[...], rec[0:320, :], preferred_element_type=jnp.float32)[0:8]
+                noise = noise_row[...]
                 state = rate * (state - scale_now * noise) + scale_next * noise
             state_ref[slot] = state
             for chunk in range(0, 320, 32):
@@ -149,7 +142,7 @@
     @pl.when(at != 0)
     def _():
         state_ref[...] = jnp.zeros_like(state_ref)
-        for slot, rec, _ in sources:
+        for slot, rec, _, _ in sources:
             raw[slot] = rec[0:320, :]
 
     for slot in range(3):
@@ -159,8 +152,7 @@
             place = slot * 256 + chunk if chunk < 256 else 768 + slot * 64
             active[place : place + 64, :] = value.astype(jnp.bfloat16)
 
-    for half, (copy, weight) in enumerate(zip(copies, (mine, other))):
-        copy.wait()
+    for half, weight in enumerate((mine_ref, other_ref)):
         offset = me * 160 if half == 0 else (1 - me) * 160
         sums[...] = jnp.dot(weight[...], active[...], preferred_element_type=jnp.float32)
         for chunk in range(0, 160, 32):
@@ -171,16 +163,20 @@
             total = total + raw[1, channels, :].astype(jnp.float32)
             out_ref[channels, :] = jnp.where(inside, total, 0.0).astype(jnp.bfloat16)
 
+    final_ref[...] = jnp.zeros_like(final_ref)
+
+    @pl.when(at == 3)
+    def _():
+        noise = jnp.dot(out_weight_ref[...], out_ref[...], preferred_element_type=jnp.float32)[0:8]
+        if step == STEPS - 1:
+            noise = (coef_ref[1, 2] - coef_ref[1, 0] * coef_ref[1, 1]) * noise
+        final_ref[...] = noise
+
     if step == STEPS - 1:
-        rate, scale_now, scale_next = (coef_ref[1, n] for n in range(3))
-        final_ref[...] = rate * state_ref[1]
-
-        @pl.when(at == 3)
+
+        @pl.when(at == 0)
         def _():
-            noise = jnp.dot(out_weight_ref[...], out_ref[...], preferred_element_type=jnp.float32)[0:8]
-            final_ref[...] = (scale_next - rate * scale_now) * noise
-    else:
-        final_ref[...] = jnp.zeros_like(final_ref)
+            final_ref[...] = coef_ref[1, 0] * state_ref[1]
 
 
 def prepare(feats, latent):
@@ -212,7 +208,7 @@
     )(flat)
 
 
-def run_step(step, coefs, rec, edge, cond, cond_edge, state, in_weight, out_weight, mine, other):
+def run_step(step, coefs, rec, edge, cond, cond_edge, noise, noise_edge, state, in_weight, out_weight, mine, other):
     core = functools.partial(lax.axis_index, "cores")
     plane = functools.partial(lax.axis_index, "comp")
     return pl.pallas_call(
@@ -222,43 +218,46 @@
             jax.ShapeDtypeStruct((3, 8, 2 * FRAME), jnp.float32),
             jax.ShapeDtypeStruct((8, 2 * FRAME), jnp.float32),
         ],
-        in_specs=[pl.BlockSpec(memory_space=pltpu.SMEM)] + [in_vmem()] * 7 + [pl.BlockSpec(memory_space=pl.ANY)] * 2,
+        in_specs=[pl.BlockSpec(memory_space=pltpu.SMEM)] + [in_vmem()] * 11,
         out_specs=[in_vmem()] * 3,
         scratch_shapes=[
             pltpu.VMEM((3, 320, 2 * FRAME), jnp.bfloat16),
             pltpu.VMEM((960, 2 * FRAME), jnp.bfloat16),
             pltpu.VMEM((480, 2 * FRAME), jnp.float32),
-            pltpu.VMEM((480, 960), jnp.bfloat16),
-            pltpu.VMEM((480, 960), jnp.bfloat16),
-            pltpu.SemaphoreType.DMA((2,)),
         ],
         compiler_params=params(),
         name=f"step{step}",
-    )(coefs, rec, edge, cond, cond_edge, state, in_weight, out_weight, mine, other)
+    )(coefs, rec, edge, cond, cond_edge, noise, noise_edge, state, in_weight, out_weight, mine, other)
 
 
 def links(comps, bands):
     def index(comp, band, core):
         return (comp * bands + band) * 2 + core
 
-    edges, diagonals, onward, swap = [], [], [], []
+    edges, swap = [], []
+    onward, diagonals = [], []
+    noise_onward, noise_diagonals = [], []
     for comp in range(comps):
-        later = (comp + 1) % comps
+        last = comp == comps - 1
+        later = 0 if last else comp + 1
         for band in range(bands):
             for core in range(2):
                 me = index(comp, band, core)
-                onward.append((me, index(later, band, core)))
+                (noise_onward if last else onward).append((me, index(later, band, core)))
                 swap.append((me, index(comp, band, 1 - core)))
                 reached = band + 2 * core - 1
                 if 0 <= reached < bands:
                     edges.append((me, index(comp, reached, 1 - core)))
-                    diagonals.append((me, index(later, reached, 1 - core)))
-    return edges, diagonals, onward, swap
+                    pair = (me, index(later, reached, 1 - core))
+                    (noise_diagonals if last else diagonals).append(pair)
+    return edges, swap, onward, diagonals, noise_onward, noise_diagonals
 
 
 def body(latent, section_inputs, in_weight, conv_weight, out_weight, timesteps, plan):
     axes = ("comp", "band", "cores")
-    edges, diagonals, onward, swap = links(lax.axis_size("comp"), lax.axis_size("band"))
+    edges, swap, onward, diagonals, noise_onward, noise_diagonals = links(
+        lax.axis_size("comp"), lax.axis_size("band")
+    )
     plane = lax.axis_index("comp")
     core = lax.axis_index("cores")
 
@@ -282,14 +281,20 @@
     coefs = jnp.stack([rates, scales[:-1], scales[1:]], axis=1)
 
     rec, edge = cond, cond_edge
+    noise_edge = jnp.zeros((8, 2 * FRAME), jnp.float32)
+    noise = jnp.zeros((2, 8, 2 * FRAME), jnp.float32)
     for step in range(STEPS):
         pair = coefs[max(step - 1, 0) : max(step - 1, 0) + 2]
         out, state, final = run_step(
-            step, pair, rec, edge, cond, cond_edge, state, in_columns, out_rows, mine, other
+            step, pair, rec, edge, cond, cond_edge, noise, noise_edge, state, in_columns, out_rows, mine, other
         )
         if step + 1 < STEPS:
+            rec = lax.ppermute(out, axes, onward)
             edge = lax.ppermute(out, axes, diagonals)
-            rec = lax.all_gather(lax.ppermute(out, axes, onward), "cores")
+            noise = lax.ppermute(final, axes, noise_onward)
+            noise_edge = lax.ppermute(final, axes, noise_diagonals)
+            noise = lax.all_gather(noise, "cores")
+            rec = lax.all_gather(rec, "cores")
 
     whole = lax.all_gather(out, "cores")
     share = lax.dynamic_slice_in_dim(whole, core * 160, 160, axis=1)

time: 121 us -> 105 us (0.87)
  the two profiles are of different devices: /device:TPU:63 before, /device:TPU:61 now
where the time goes in v2:
time: 105 us
  starting transfers between devices  33.2 us (32%)
  blocking collectives  25.6 us (24%)
  waiting for transfers between devices  22.2 us (21%)
  Pallas kernels  11.3 us (11%)
  local copies, waits for them, and re-layouts  7.67 us (7%)
  other arithmetic  3.89 us (4%)
    ppermute x2, waiting for transfers between devices, body(): noise = lax.ppermute(final, axes, noise_onward)  22.2 us
    ppermute x2, starting transfers between devices, body(): edge = lax.ppermute(out, axes, diagonals)  11.7 us
    ppermute x1, starting transfers between devices, body(): cond_edge = lax.ppermute(message, axes, edges)  10.1 us
    pallas_call x3, Pallas kernels, run_step(): pl.pallas_call(functools.partial(step_kernel, step, core, plane), out_sha...  9.93 us
    psum x1, blocking collectives, body(): total = lax.psum(final[0:4], 'comp')  6.75 us
    all_gather x2, blocking collectives, body(): rec = lax.all_gather(rec, 'cores')  4.74 us
    ppermute x2, starting transfers between devices, body(): rec = lax.ppermute(out, axes, onward)  4.36 us
    all_gather x2, blocking collectives, body(): noise = lax.all_gather(noise, 'cores')  3.85 us
  transfers between devices with their start and end apart: 10, of which 2 were waited for; matrix products, arithmetic and copies ran while one was open for 5% of the time, Pallas kernels for 1%

profile of v2, /device:TPU:61, one launch (start us, length us, event | category | flops | bytes accessed | tf_op | source)
XLA Modules:
  0.0 104.8 jit_solution(10812920238611001297)
XLA Ops:
  0.6 1.7 %all_gather_reshape_squeeze.3 = bf16[1,2,2,160,240]{4,3,2,1,0:T(8,128)(2,1)S(1)} reshape(bf16[1,2,2,38400]{3,2,1,0:T(2,128)(2,1)} %param.8) | data formatting | bytes 614400 | tf_op jit(solution)/shard_map/all_gather;reshape;squeeze | solution.py:265
  2.4 2.6 %all_gather.42.feat_ref = bf16[2,2,2,160,240]{4,3,2,1,0:T(8,128)(2,1)S(1)} all-gather(bf16[1,2,2,160,240]{4,3,2,1,0:T(8,128)(2,1)S(1)} %all_gather_reshape_squeeze.3), channel_id=1, replica_groups=mesh['comp'=4,'band'=64,'cores'=2] {'cores'}, dimensions={0}, use_global_device_ids=true | all-gather | bytes 921600 | tf_op jit(solution)/shard_map/all_gather | solution.py:265
  6.5 10.1 %collective-permute-start = (bf16[336,512]{1,0:T(8,128)(2,1)}, bf16[336,512]{1,0:T(8,128)(2,1)S(1)}, u32[]{:S(2)}, u32[]{:S(2)}) collective-permute-start(bf16[336,512]{1,0:T(8,128)(2,1)} %get-tuple-element.14), channel_id=1, source_target_pairs={{1,2},{2,1},{3,4},{4,3},{5,6},{6,5},{7,8},{8,7},{9,10},{10,9},{11,... | collective-permute-start | bytes 1032200 | tf_op jit(solution)/shard_map/ppermute | solution.py:267
  16.6 3.5 %convert_element_type.16 = f32[1,460800]{1,0:T(1,128)S(1)} convert(bf16[1,460800]{1,0:T(2,128)(2,1)} %param.10) | non-fusion elementwise | flops 460800 | bytes 2764800 | tf_op jit(solution)/shard_map/convert_element_type | solution.py:199
  20.7 1.9 %collective-permute-start.1 = (bf16[480,960]{1,0:T(8,128)(2,1)S(1)}, bf16[480,960]{1,0:T(8,128)(2,1)S(1)}, u32[]{:S(2)}, u32[]{:S(2)}) collective-permute-start(bf16[480,960]{1,0:T(8,128)(2,1)S(1)} %relay.1.mine_ref), channel_id=1, source_target_pairs={{0,1},{1,0},{2,3},{3,2},{4,5},{5,4},{6,7},{7,6},{8,9},{9,8},{10,11... | collective-permute-start | bytes 2764808 | tf_op jit(solution)/shard_map/ppermute | solution.py:270
  23.5 2.0 %all-gather = f32[16,160]{1,0:T(8,128)S(1)} all-gather(f32[8,160]{1,0:T(8,128)S(1)} %pad_maximum_fusion), channel_id=2, replica_groups=mesh['comp'=4,'band'=64,'cores'=2] {'cores'}, dimensions={0}, use_global_device_ids=true | all-gather | bytes 15360 | tf_op jit(solution)/shard_map/all_gather | solution.py:272
  26.3 2.8 %step0.1 = (bf16[320,512]{1,0:T(8,128)(2,1)S(1)}, f32[3,8,512]{2,1,0:T(8,128)S(1)}, f32[8,512]{1,0:T(8,128)S(1)}) custom-call(f32[2,3]{1,0:T(2,128)S(1)} %get-tuple-element.34.coef_ref, bf16[2,320,512]{2,1,0:T(8,128)(2,1)S(1)} %get-tuple-element.13.rec_ref.cond_ref, bf16[336,512]{1,0:T(8,128)(2,1)S(1)} %collective-permute-done.edge_ref.cond_edge_ref, ...), custom_call_target="tpu_custom_call" | custom-call | tf_op jit(solution)/shard_map/step0/pallas_call | solution.py:214
  29.1 2.3 %collective-permute-start.2 = (bf16[320,512]{1,0:T(8,128)(2,1)S(1)}, bf16[320,512]{1,0:T(8,128)(2,1)S(1)}, u32[]{:S(2)}, u32[]{:S(2)}) collective-permute-start(bf16[320,512]{1,0:T(8,128)(2,1)S(1)} %get-tuple-element.16), channel_id=1, source_target_pairs={{0,128},{1,129},{2,130},{3,131},{4,132},{5,133},{6,134},{7,135},{8... | collective-permute-start | bytes 983048 | tf_op jit(solution)/shard_map/ppermute | solution.py:292
  31.5 8.7 %collective-permute-start.3 = (bf16[320,512]{1,0:T(8,128)(2,1)S(1)}, bf16[320,512]{1,0:T(8,128)(2,1)S(1)}, u32[]{:S(2)}, u32[]{:S(2)}) collective-permute-start(bf16[320,512]{1,0:T(8,128)(2,1)S(1)} %get-tuple-element.16), channel_id=1, source_target_pairs={{1,130},{2,129},{3,132},{4,131},{5,134},{6,133},{7,136},{8,135},{9... | collective-permute-start | bytes 983048 | tf_op jit(solution)/shard_map/ppermute | solution.py:293
  40.2 1.3 %collective-permute-start.4 = (f32[8,512]{1,0:T(8,128)S(1)}, f32[8,512]{1,0:T(8,128)S(1)}, u32[]{:S(2)}, u32[]{:S(2)}) collective-permute-start(f32[8,512]{1,0:T(8,128)S(1)} %get-tuple-element.17), channel_id=1, source_target_pairs={{384,0},{385,1},{386,2},{387,3},{388,4},{389,5},{390,6},{391,7},{3... | collective-permute-start | bytes 49160 | tf_op jit(solution)/shard_map/ppermute | solution.py:294
  42.8 10.7 %collective-permute-done.4 = f32[8,512]{1,0:T(8,128)S(1)} collective-permute-done((f32[8,512]{1,0:T(8,128)S(1)}, f32[8,512]{1,0:T(8,128)S(1)}, u32[]{:S(2)}, u32[]{:S(2)}) %collective-permute-start.4) | collective-permute-done | bytes 16416 | tf_op jit(solution)/shard_map/ppermute | solution.py:294
  53.4 1.8 %all-gather.2 = f32[16,512]{1,0:T(8,128)S(1)} all-gather(f32[8,512]{1,0:T(8,128)S(1)} %collective-permute-done.4), channel_id=4, replica_groups=mesh['comp'=4,'band'=64,'cores'=2] {'cores'}, dimensions={0}, use_global_device_ids=true | all-gather | bytes 49152 | tf_op jit(solution)/shard_map/all_gather | solution.py:296
  55.2 2.3 %all-gather.1 = bf16[640,512]{1,0:T(8,128)(2,1)S(1)} all-gather(bf16[320,512]{1,0:T(8,128)(2,1)S(1)} %collective-permute-done.2), channel_id=3, replica_groups=mesh['comp'=4,'band'=64,'cores'=2] {'cores'}, dimensions={0}, use_global_device_ids=true | all-gather | bytes 983040 | tf_op jit(solution)/shard_map/all_gather | solution.py:297
  57.5 3.6 %step1.1 = (bf16[320,512]{1,0:T(8,128)(2,1)}, f32[3,8,512]{2,1,0:T(8,128)S(1)}, f32[8,512]{1,0:T(8,128)S(1)}) custom-call(f32[2,3]{1,0:T(2,128)S(1)} %get-tuple-element.34.coef_ref, bf16[2,320,512]{2,1,0:T(8,128)(2,1)S(1)} %bitcast.38, bf16[320,512]{1,0:T(8,128)(2,1)S(1)} %collective-permute-done.3.edge_ref, ...), custom_call_target="tpu_custom_call" | custom-call | tf_op jit(solution)/shard_map/step1/pallas_call | solution.py:214
  61.1 2.0 %collective-permute-start.6 = (bf16[320,512]{1,0:T(8,128)(2,1)}, bf16[320,512]{1,0:T(8,128)(2,1)}, u32[]{:S(2)}, u32[]{:S(2)}) collective-permute-start(bf16[320,512]{1,0:T(8,128)(2,1)} %get-tuple-element.19), channel_id=1, source_target_pairs={{0,128},{1,129},{2,130},{3,131},{4,132},{5,133},{6,134},{7,135},{8... | collective-permute-start | bytes 983048 | tf_op jit(solution)/shard_map/ppermute | solution.py:292
  63.1 3.0 %collective-permute-start.7 = (bf16[320,512]{1,0:T(8,128)(2,1)}, bf16[320,512]{1,0:T(8,128)(2,1)S(1)}, u32[]{:S(2)}, u32[]{:S(2)}) collective-permute-start(bf16[320,512]{1,0:T(8,128)(2,1)} %get-tuple-element.19), channel_id=1, source_target_pairs={{1,130},{2,129},{3,132},{4,131},{5,134},{6,133},{7,136},{8,135},{9... | collective-permute-start | bytes 983048 | tf_op jit(solution)/shard_map/ppermute | solution.py:293
  68.7 11.5 %collective-permute-done.8 = f32[8,512]{1,0:T(8,128)} collective-permute-done((f32[8,512]{1,0:T(8,128)S(1)}, f32[8,512]{1,0:T(8,128)}, u32[]{:S(2)}, u32[]{:S(2)}) %collective-permute-start.8) | collective-permute-done | bytes 16416 | tf_op jit(solution)/shard_map/ppermute | solution.py:294
  80.3 2.0 %all-gather.4 = f32[16,512]{1,0:T(8,128)S(1)} all-gather(f32[8,512]{1,0:T(8,128)} %collective-permute-done.8), channel_id=6, replica_groups=mesh['comp'=4,'band'=64,'cores'=2] {'cores'}, dimensions={0}, use_global_device_ids=true | all-gather | bytes 49152 | tf_op jit(solution)/shard_map/all_gather | solution.py:296
  82.3 2.5 %all-gather.3 = bf16[640,512]{1,0:T(8,128)(2,1)S(1)} all-gather(bf16[320,512]{1,0:T(8,128)(2,1)} %collective-permute-done.6), channel_id=5, replica_groups=mesh['comp'=4,'band'=64,'cores'=2] {'cores'}, dimensions={0}, use_global_device_ids=true | all-gather | bytes 983040 | tf_op jit(solution)/shard_map/all_gather | solution.py:297
  86.5 3.5 %step2.1 = (bf16[320,512]{1,0:T(8,128)(2,1)S(1)}, f32[3,8,512]{2,1,0:T(8,128)}, f32[8,512]{1,0:T(8,128)S(1)}) custom-call(f32[2,3]{1,0:T(2,128)S(1)} %get-tuple-element.35.coef_ref, bf16[2,320,512]{2,1,0:T(8,128)(2,1)S(1)} %bitcast.37, bf16[320,512]{1,0:T(8,128)(2,1)S(1)} %copy-done.2, bf16[2,320,512]{2,1,0:T(8,128)(2,1)S(1)} %get-tuple-element.13.rec_ref.cond_ref, ...), custom_call_target="tpu_custom_call" | custom-call | tf_op jit(solution)/shard_map/step2/pallas_call | solution.py:214
  90.0 6.8 %psum.7 = f32[4,512]{1,0:T(4,128)S(1)} all-reduce(f32[4,512]{1,0:T(4,128)S(1)} %slice.52), channel_id=1, replica_groups=mesh['comp'=4,'band'=64,'cores'=2] {'comp'}, use_global_device_ids=true, to_apply=%region_0.1 | all-reduce | flops 2048 | bytes 16384 | tf_op jit(solution)/shard_map/psum | solution.py:304
  96.8 3.4 %all-gather.6 = f32[2,1,512]{2,1,0:T(1,128)S(1)} all-gather(f32[1,1,512]{2,1,0:T(1,128)S(1)} %dynamic-slice_bitcast_fusion), channel_id=1, replica_groups=mesh['comp'=4,'band'=64,'cores'=2] {'cores'}, dimensions={0}, use_global_device_ids=true | all-gather | bytes 6144 | tf_op jit(solution)/shard_map/all_gather | solution.py:305
  100.8 2.3 %all-gather.5 = bf16[640,512]{1,0:T(8,128)(2,1)S(1)} all-gather(bf16[320,512]{1,0:T(8,128)(2,1)S(1)} %get-tuple-element.23), channel_id=7, replica_groups=mesh['comp'=4,'band'=64,'cores'=2] {'cores'}, dimensions={0}, use_global_device_ids=true | all-gather | bytes 983040 | tf_op jit(solution)/shard_map/all_gather | solution.py:299
  103.4 1.4 %reshape.19 = bf16[1,2,2,38400]{3,2,1,0:T(2,128)(2,1)} reshape(bf16[2,2,160,240]{3,2,1,0:T(8,128)(2,1)S(1)} %copy.36) | data formatting | bytes 614400 | tf_op jit(solution)/shard_map/reshape | solution.py:302
  (59 shorter events, 10.2 us)
Async XLA Ops:
  0.6 22.1 %copy-start = (f32[1000]{0:T(1024)S(1)}, f32[1000]{0:T(1024)}, u32[]{:S(2)}) copy-start(f32[1000]{0:T(1024)} %param.13) | copy-start | bytes 12004
  4.9 0.7 copy-start.3
  6.5 19.7 %collective-permute-start = (bf16[336,512]{1,0:T(8,128)(2,1)}, bf16[336,512]{1,0:T(8,128)(2,1)S(1)}, u32[]{:S(2)}, u32[]{:S(2)}) collective-permute-start(bf16[336,512]{1,0:T(8,128)(2,1)} %get-tuple-element.14), channel_id=1, source_target_pairs={{1,2},{2,1},{3,4},{4,3},{5,6},{6,5},{7,8},{8,7},{9,10},{10,9},{11,... | collective-permute-start | bytes 1032200 | tf_op jit(solution)/shard_map/ppermute | solution.py:267
  20.2 2.5 %copy-start.6 = (s32[4]{0:T(128)S(1)}, s32[4]{0:T(128)}, u32[]{:S(2)}) copy-start(s32[4]{0:T(128)} %param.12) | copy-start | bytes 52
  20.2 3.3 %copy-start.5 = (bf16[160,4]{0,1:T(4,128)(2,1)S(1)}, bf16[160,4]{0,1:T(4,128)(2,1)}, u32[]{:S(2)}) copy-start(bf16[160,4]{0,1:T(4,128)(2,1)} %param.11) | copy-start | bytes 3844
  20.2 3.3 %copy-start.4 = (f32[4,160]{1,0:T(4,128)S(1)}, f32[4,160]{1,0:T(4,128)}, u32[]{:S(2)}) copy-start(f32[4,160]{1,0:T(4,128)} %param.9) | copy-start | bytes 7684
  20.7 5.5 %collective-permute-start.1 = (bf16[480,960]{1,0:T(8,128)(2,1)S(1)}, bf16[480,960]{1,0:T(8,128)(2,1)S(1)}, u32[]{:S(2)}, u32[]{:S(2)}) collective-permute-start(bf16[480,960]{1,0:T(8,128)(2,1)S(1)} %relay.1.mine_ref), channel_id=1, source_target_pairs={{0,1},{1,0},{2,3},{3,2},{4,5},{5,4},{6,7},{7,6},{8,9},{9,8},{10,11... | collective-permute-start | bytes 2764808 | tf_op jit(solution)/shard_map/ppermute | solution.py:270
  29.1 26.1 %collective-permute-start.2 = (bf16[320,512]{1,0:T(8,128)(2,1)S(1)}, bf16[320,512]{1,0:T(8,128)(2,1)S(1)}, u32[]{:S(2)}, u32[]{:S(2)}) collective-permute-start(bf16[320,512]{1,0:T(8,128)(2,1)S(1)} %get-tuple-element.16), channel_id=1, source_target_pairs={{0,128},{1,129},{2,130},{3,131},{4,132},{5,133},{6,134},{7,135},{8... | collective-permute-start | bytes 983048 | tf_op jit(solution)/shard_map/ppermute | solution.py:292
  31.5 26.0 %collective-permute-start.3 = (bf16[320,512]{1,0:T(8,128)(2,1)S(1)}, bf16[320,512]{1,0:T(8,128)(2,1)S(1)}, u32[]{:S(2)}, u32[]{:S(2)}) collective-permute-start(bf16[320,512]{1,0:T(8,128)(2,1)S(1)} %get-tuple-element.16), channel_id=1, source_target_pairs={{1,130},{2,129},{3,132},{4,131},{5,134},{6,133},{7,136},{8,135},{9... | collective-permute-start | bytes 983048 | tf_op jit(solution)/shard_map/ppermute | solution.py:293
  40.2 13.3 %collective-permute-start.4 = (f32[8,512]{1,0:T(8,128)S(1)}, f32[8,512]{1,0:T(8,128)S(1)}, u32[]{:S(2)}, u32[]{:S(2)}) collective-permute-start(f32[8,512]{1,0:T(8,128)S(1)} %get-tuple-element.17), channel_id=1, source_target_pairs={{384,0},{385,1},{386,2},{387,3},{388,4},{389,5},{390,6},{391,7},{3... | collective-permute-start | bytes 49160 | tf_op jit(solution)/shard_map/ppermute | solution.py:294
  41.5 16.1 %collective-permute-start.5 = (f32[8,512]{1,0:T(8,128)S(1)}, f32[8,512]{1,0:T(8,128)S(1)}, u32[]{:S(2)}, u32[]{:S(2)}) collective-permute-start(f32[8,512]{1,0:T(8,128)S(1)} %get-tuple-element.17), channel_id=1, source_target_pairs={{385,2},{386,1},{387,4},{388,3},{389,6},{390,5},{391,8},{392,7},{3... | collective-permute-start | bytes 49160 | tf_op jit(solution)/shard_map/ppermute | solution.py:295
  61.1 21.2 %collective-permute-start.6 = (bf16[320,512]{1,0:T(8,128)(2,1)}, bf16[320,512]{1,0:T(8,128)(2,1)}, u32[]{:S(2)}, u32[]{:S(2)}) collective-permute-start(bf16[320,512]{1,0:T(8,128)(2,1)} %get-tuple-element.19), channel_id=1, source_target_pairs={{0,128},{1,129},{2,130},{3,131},{4,132},{5,133},{6,134},{7,135},{8... | collective-permute-start | bytes 983048 | tf_op jit(solution)/shard_map/ppermute | solution.py:292
  63.1 21.7 %collective-permute-start.7 = (bf16[320,512]{1,0:T(8,128)(2,1)}, bf16[320,512]{1,0:T(8,128)(2,1)S(1)}, u32[]{:S(2)}, u32[]{:S(2)}) collective-permute-start(bf16[320,512]{1,0:T(8,128)(2,1)} %get-tuple-element.19), channel_id=1, source_target_pairs={{1,130},{2,129},{3,132},{4,131},{5,134},{6,133},{7,136},{8,135},{9... | collective-permute-start | bytes 983048 | tf_op jit(solution)/shard_map/ppermute | solution.py:293
  66.1 14.2 %collective-permute-start.8 = (f32[8,512]{1,0:T(8,128)S(1)}, f32[8,512]{1,0:T(8,128)}, u32[]{:S(2)}, u32[]{:S(2)}) collective-permute-start(f32[8,512]{1,0:T(8,128)S(1)} %get-tuple-element.20), channel_id=1, source_target_pairs={{384,0},{385,1},{386,2},{387,3},{388,4},{389,5},{390,6},{391,7},{3... | collective-permute-start | bytes 49160 | tf_op jit(solution)/shard_map/ppermute | solution.py:294
  67.4 17.4 %collective-permute-start.9 = (f32[8,512]{1,0:T(8,128)S(1)}, f32[8,512]{1,0:T(8,128)S(1)}, u32[]{:S(2)}, u32[]{:S(2)}) collective-permute-start(f32[8,512]{1,0:T(8,128)S(1)} %get-tuple-element.20), channel_id=1, source_target_pairs={{385,2},{386,1},{387,4},{388,3},{389,6},{390,5},{391,8},{392,7},{3... | collective-permute-start | bytes 49160 | tf_op jit(solution)/shard_map/ppermute | solution.py:295
  84.8 0.7 copy-start.1
  85.5 1.0 copy-start.2

commit v3 on v2

--- a/solution.py
+++ b/solution.py
@@ -12,7 +12,7 @@
 LANES = 128
 FRAME = 256
 MESSAGE_EXTRA = 16
-VMEM_BYTES = 48 * 1024 * 1024
+VMEM_BYTES = 14 * 1024 * 1024
 
 
 def params():
@@ -59,7 +59,9 @@
         out_ref[at : at + 160, 896:960] = held[7, :, :64].astype(jnp.bfloat16)
 
 
-def prepare_kernel(core, feat_ref, latent_ref, own_ref, message_ref, state_ref):
+def prepare_kernel(core, feat_ref, latent_ref, own_ref, message_ref, state_ref, latent, sem):
+    copy = pltpu.make_async_copy(latent_ref, latent, sem)
+    copy.start()
     own_ref[...] = jnp.zeros_like(own_ref)
     state_ref[...] = jnp.zeros_like(state_ref)
     for half in range(2):
@@ -68,11 +70,12 @@
                 own_ref[row, half * 160 : half * 160 + 160, frame * FRAME : frame * FRAME + 240] = feat_ref[
                     half, frame, row
                 ]
+    me = core()
+    message_ref[0:320, :] = own_ref[me]
+    copy.wait()
     for frame in range(2):
         for row in range(2):
-            state_ref[row, 0:4, frame * FRAME : frame * FRAME + 240] = latent_ref[frame, :, row, :]
-    me = core()
-    message_ref[0:320, :] = own_ref[me]
+            state_ref[row, 0:4, frame * FRAME : frame * FRAME + 240] = latent[frame, :, row, :]
     state = state_ref[me, 0:4, :]
     high = state.astype(jnp.bfloat16).astype(jnp.float32)
     left = state - high
@@ -82,18 +85,60 @@
     message_ref[320:336, :] = parts.astype(jnp.bfloat16)
 
 
+def swish(value):
+    value = value.astype(jnp.float32)
+    return (0.5 * value * (1.0 + jnp.tanh(0.5 * value))).astype(jnp.bfloat16)
+
+
+def project(slot, state, cond, in_weight_ref, raw):
+    for chunk in range(0, 320, 32):
+        total = cond[chunk : chunk + 32, :].astype(jnp.float32)
+        weight = in_weight_ref[chunk : chunk + 32, :]
+        proj = weight[:, 0:1] * state[0:1, :]
+        for latent in range(1, 4):
+            proj = proj + weight[:, latent : latent + 1] * state[latent : latent + 1, :]
+        raw[slot, chunk : chunk + 32, :] = (proj + total).astype(jnp.bfloat16)
+
+
+def latent_kernel(
+    core, plane, coef_ref, noise_ref, noise_edge_ref, state_in_ref, in_weight_ref, cond_ref, cond_edge_ref, input_ref, state_ref
+):
+    me = core()
+    at = plane()
+
+    @pl.when(at == 0)
+    def _():
+        rate, scale_now, scale_next = (coef_ref[0, n] for n in range(3))
+        for slot, noise_row, cond in (
+            (1 - me, noise_ref.at[0], cond_ref.at[0]),
+            (2 - me, noise_ref.at[1], cond_ref.at[1]),
+            (2 * me, noise_edge_ref, cond_edge_ref),
+        ):
+            noise = noise_row[...]
+            state = state_in_ref[slot]
+            state = rate * (state - scale_now * noise) + scale_next * noise
+            state_ref[slot] = state
+            project(slot, state, cond, in_weight_ref, input_ref)
+
+    @pl.when(at != 0)
+    def _():
+        state_ref[...] = jnp.zeros_like(state_ref)
+
+
+def edge_kernel(edge_ref, out_ref):
+    for chunk in range(0, 320, 64):
+        out_ref[chunk : chunk + 64, :] = swish(edge_ref[chunk : chunk + 64, :])
+
+
 def step_kernel(
     step,
     core,
     plane,
     coef_ref,
+    input_ref,
+    state_in_ref,
+    edge_ref,
     rec_ref,
-    edge_ref,
-    cond_ref,
-    cond_edge_ref,
-    noise_ref,
-    noise_edge_ref,
-    state_in_ref,
     in_weight_ref,
     out_weight_ref,
     mine_ref,
@@ -107,50 +152,42 @@
 ):
     me = core()
     at = plane()
-    sources = [
-        (1 - me, rec_ref.at[0], cond_ref.at[0], noise_ref.at[0]),
-        (2 - me, rec_ref.at[1], cond_ref.at[1], noise_ref.at[1]),
-        (2 * me, edge_ref, cond_edge_ref, noise_edge_ref),
-    ]
     lanes = lax.broadcasted_iota(jnp.int32, (1, 2 * FRAME), 1)
     inside = (lanes % FRAME) < 240
-    rate, scale_now, scale_next = (coef_ref[0, n] for n in range(3))
+
+    def activate(slot, rows):
+        start = pl.multiple_of(slot * 256, 256)
+        tail = pl.multiple_of(768 + slot * 64, 64)
+        for chunk in range(0, 320, 64):
+            place = start + chunk if chunk < 256 else tail
+            active[pl.ds(place, 64), :] = rows(chunk)
 
     @pl.when(at == 0)
     def _():
-        for number, (slot, _, cond, noise_row) in enumerate(sources):
-            if step == 0:
-                if number < 2:
-                    state = state_in_ref[number]
-                else:
-                    extra = cond_edge_ref[320:336, :].astype(jnp.float32)
-                    state = (extra[0:4] + extra[4:8]) + extra[8:12]
-                    state = jnp.concatenate([state, jnp.zeros_like(state)], axis=0)
-            else:
-                state = state_in_ref[slot]
-                noise = noise_row[...]
-                state = rate * (state - scale_now * noise) + scale_next * noise
-            state_ref[slot] = state
-            for chunk in range(0, 320, 32):
-                total = cond[chunk : chunk + 32, :].astype(jnp.float32)
-                weight = in_weight_ref[chunk : chunk + 32, :]
-                proj = weight[:, 0:1] * state[0:1, :]
-                for latent in range(1, 4):
-                    proj = proj + weight[:, latent : latent + 1] * state[latent : latent + 1, :]
-                raw[slot, chunk : chunk + 32, :] = (proj + total).astype(jnp.bfloat16)
+        if step == 0:
+            extra = edge_ref[320:336, :].astype(jnp.float32)
+            halo = (extra[0:4] + extra[4:8]) + extra[8:12]
+            halo = jnp.concatenate([halo, jnp.zeros_like(halo)], axis=0)
+            for slot, state, cond in (
+                (1 - me, state_in_ref[0], rec_ref.at[0]),
+                (2 - me, state_in_ref[1], rec_ref.at[1]),
+                (2 * me, halo, edge_ref),
+            ):
+                state_ref[slot] = state
+                project(slot, state, cond, in_weight_ref, raw)
+        else:
+            state_ref[...] = state_in_ref[...]
+            raw[...] = input_ref[...]
+        for slot in range(3):
+            activate(slot, lambda chunk, slot=slot: swish(raw[slot, chunk : chunk + 64, :]))
 
     @pl.when(at != 0)
     def _():
         state_ref[...] = jnp.zeros_like(state_ref)
-        for slot, rec, _, _ in sources:
-            raw[slot] = rec[0:320, :]
-
-    for slot in range(3):
-        for chunk in range(0, 320, 64):
-            value = raw[slot, chunk : chunk + 64, :].astype(jnp.float32)
-            value = 0.5 * value * (1.0 + jnp.tanh(0.5 * value))
-            place = slot * 256 + chunk if chunk < 256 else 768 + slot * 64
-            active[place : place + 64, :] = value.astype(jnp.bfloat16)
+        raw[1] = rec_ref[me]
+        for row in range(2):
+            activate(row + 1 - me, lambda chunk, row=row: swish(rec_ref[row, chunk : chunk + 64, :]))
+        activate(2 * me, lambda chunk: swish(edge_ref[chunk : chunk + 64, :]))
 
     for half, weight in enumerate((mine_ref, other_ref)):
         offset = me * 160 if half == 0 else (1 - me) * 160
@@ -188,8 +225,9 @@
             jax.ShapeDtypeStruct((320 + MESSAGE_EXTRA, 2 * FRAME), jnp.bfloat16),
             jax.ShapeDtypeStruct((2, 8, 2 * FRAME), jnp.float32),
         ],
-        in_specs=[in_vmem()] * 2,
+        in_specs=[in_vmem(), pl.BlockSpec(memory_space=pl.ANY)],
         out_specs=[in_vmem()] * 3,
+        scratch_shapes=[pltpu.VMEM(latent.shape, latent.dtype), pltpu.SemaphoreType.DMA],
         compiler_params=params(),
         name="prepare",
     )(feats, latent)
@@ -208,7 +246,40 @@
     )(flat)
 
 
-def run_step(step, coefs, rec, edge, cond, cond_edge, noise, noise_edge, state, in_weight, out_weight, mine, other):
+def hint(micros):
+    return pl.CostEstimate(flops=int(micros * 1e9), bytes_accessed=0, transcendentals=0)
+
+
+def run_latent(coefs, noise, noise_edge, state, in_weight, cond, cond_edge):
+    core = functools.partial(lax.axis_index, "cores")
+    plane = functools.partial(lax.axis_index, "comp")
+    return pl.pallas_call(
+        functools.partial(latent_kernel, core, plane),
+        out_shape=[
+            jax.ShapeDtypeStruct((3, 320, 2 * FRAME), jnp.bfloat16),
+            jax.ShapeDtypeStruct((3, 8, 2 * FRAME), jnp.float32),
+        ],
+        in_specs=[pl.BlockSpec(memory_space=pltpu.SMEM)] + [in_vmem()] * 6,
+        out_specs=[in_vmem()] * 2,
+        compiler_params=params(),
+        cost_estimate=hint(3),
+        name="latent",
+    )(coefs, noise, noise_edge, state, in_weight, cond, cond_edge)
+
+
+def run_edge(edge):
+    return pl.pallas_call(
+        edge_kernel,
+        out_shape=jax.ShapeDtypeStruct((320, 2 * FRAME), jnp.bfloat16),
+        in_specs=[in_vmem()],
+        out_specs=in_vmem(),
+        compiler_params=params(),
+        cost_estimate=hint(20),
+        name="edge",
+    )(edge)
+
+
+def run_step(step, coefs, rec, edge, inputs, state, in_weight, out_weight, mine, other):
     core = functools.partial(lax.axis_index, "cores")
     plane = functools.partial(lax.axis_index, "comp")
     return pl.pallas_call(
@@ -218,7 +289,7 @@
             jax.ShapeDtypeStruct((3, 8, 2 * FRAME), jnp.float32),
             jax.ShapeDtypeStruct((8, 2 * FRAME), jnp.float32),
         ],
-        in_specs=[pl.BlockSpec(memory_space=pltpu.SMEM)] + [in_vmem()] * 11,
+        in_specs=[pl.BlockSpec(memory_space=pltpu.SMEM)] + [in_vmem()] * 8,
         out_specs=[in_vmem()] * 3,
         scratch_shapes=[
             pltpu.VMEM((3, 320, 2 * FRAME), jnp.bfloat16),
@@ -227,7 +298,23 @@
         ],
         compiler_params=params(),
         name=f"step{step}",
-    )(coefs, rec, edge, cond, cond_edge, noise, noise_edge, state, in_weight, out_weight, mine, other)
+    )(coefs, inputs, state, edge, rec, in_weight, out_weight, mine, other)
+
+
+def copy_kernel(in_ref, out_ref):
+    out_ref[...] = in_ref[...]
+
+
+def copied(row):
+    return pl.pallas_call(
+        copy_kernel,
+        out_shape=jax.ShapeDtypeStruct(row.shape, row.dtype),
+        in_specs=[in_vmem()],
+        out_specs=in_vmem(),
+        compiler_params=params(),
+        cost_estimate=hint(20),
+        name="copy_row",
+    )(row)
 
 
 def links(comps, bands):
@@ -264,6 +351,7 @@
     feats = section_inputs[0].reshape(2, 2, 160, 240)
     feats = lax.all_gather(feats, "cores")
     cond, message, state = prepare(feats, latent)
+    conv_weight, message = lax.optimization_barrier((conv_weight, message))
     cond_edge = lax.ppermute(message, axes, edges)
 
     mine = relaid_weight(conv_weight)
@@ -281,20 +369,20 @@
     coefs = jnp.stack([rates, scales[:-1], scales[1:]], axis=1)
 
     rec, edge = cond, cond_edge
-    noise_edge = jnp.zeros((8, 2 * FRAME), jnp.float32)
-    noise = jnp.zeros((2, 8, 2 * FRAME), jnp.float32)
+    inputs = jnp.zeros((3, 16, LANES), jnp.bfloat16)
     for step in range(STEPS):
         pair = coefs[max(step - 1, 0) : max(step - 1, 0) + 2]
-        out, state, final = run_step(
-            step, pair, rec, edge, cond, cond_edge, noise, noise_edge, state, in_columns, out_rows, mine, other
-        )
+        out, state, final = run_step(step, pair, rec, edge, inputs, state, in_columns, out_rows, mine, other)
         if step + 1 < STEPS:
+            edge = lax.ppermute(out, axes, diagonals)
             rec = lax.ppermute(out, axes, onward)
-            edge = lax.ppermute(out, axes, diagonals)
-            noise = lax.ppermute(final, axes, noise_onward)
+            rec = lax.all_gather(rec, "cores")
+            noise = lax.all_gather(lax.ppermute(final, axes, noise_onward), "cores")
             noise_edge = lax.ppermute(final, axes, noise_diagonals)
-            noise = lax.all_gather(noise, "cores")
-            rec = lax.all_gather(rec, "cores")
+            state = copied(state)
+            inputs, state = run_latent(
+                coefs[step : step + 2], noise, noise_edge, state, in_columns, cond, cond_edge
+            )
 
     whole = lax.all_gather(out, "cores")
     share = lax.dynamic_slice_in_dim(whole, core * 160, 160, axis=1)

time: 105 us -> 103 us (0.981)
  the two profiles are of different devices: /device:TPU:61 before, /device:TPU:7 now
where the time goes in v3:
time: 103 us; the launch traced here: 102 us
  blocking collectives  45.4 us (44%)
  starting transfers between devices  31.1 us (30%)
  Pallas kernels  12 us (12%)
  local copies, waits for them, and re-layouts  7.56 us (7%)
  other arithmetic  3.89 us (4%)
    all_gather x2, blocking collectives, body(): noise = lax.all_gather(lax.ppermute(final, axes, noise_onward), 'cores')  14 us
    psum x1, blocking collectives, body(): total = lax.psum(final[0:4], 'comp')  13 us
    ppermute x1, starting transfers between devices, body(): other = lax.ppermute(mine, axes, swap)  12.6 us
    pallas_call x3, Pallas kernels, run_step(): pl.pallas_call(functools.partial(step_kernel, step, core, plane), out_sha...  8.45 us
    all_gather x2, blocking collectives, body(): rec = lax.all_gather(rec, 'cores')  7.87 us
    ppermute x2, starting transfers between devices, body(): rec = lax.ppermute(out, axes, onward)  6.91 us
    all_gather x1, blocking collectives, body(): lax.all_gather(lax.dynamic_slice_in_dim(total, plane, 1, axis=0)[0], 'cor...  3.87 us
    convert_element_type x1, other arithmetic, relaid_weight(): weight.astype(jnp.float32)  3.53 us
  transfers between devices with their start and end apart: 10, of which 1 were waited for; matrix products, arithmetic and copies ran while one was open for 6% of the time, Pallas kernels for 3%

profile of v3, /device:TPU:7, one launch (start us, length us, event | category | flops | bytes accessed | tf_op | source)
XLA Modules:
  0.0 101.7 jit_solution(4848613210709784996)
XLA Ops:
  0.6 1.7 %all_gather_reshape_squeeze.3 = bf16[1,2,2,160,240]{4,3,2,1,0:T(8,128)(2,1)S(1)} reshape(bf16[1,2,2,38400]{3,2,1,0:T(2,128)(2,1)} %param.8) | data formatting | bytes 614400 | tf_op jit(solution)/shard_map/all_gather;reshape;squeeze | solution.py:352
  2.4 2.6 %all_gather.42.feat_ref = bf16[2,2,2,160,240]{4,3,2,1,0:T(8,128)(2,1)S(1)} all-gather(bf16[1,2,2,160,240]{4,3,2,1,0:T(8,128)(2,1)S(1)} %all_gather_reshape_squeeze.3), channel_id=1, replica_groups=mesh['comp'=4,'band'=64,'cores'=2] {'cores'}, dimensions={0}, use_global_device_ids=true | all-gather | bytes 921600 | tf_op jit(solution)/shard_map/all_gather | solution.py:352
  5.8 3.5 %collective-permute-start = (bf16[336,512]{1,0:T(8,128)(2,1)S(1)}, bf16[336,512]{1,0:T(8,128)(2,1)S(1)}, u32[]{:S(2)}, u32[]{:S(2)}) collective-permute-start(bf16[336,512]{1,0:T(8,128)(2,1)S(1)} %get-tuple-element.21), channel_id=1, source_target_pairs={{1,2},{2,1},{3,4},{4,3},{5,6},{6,5},{7,8},{8,7},{9,10},{10,9},{11,... | collective-permute-start | bytes 1032200 | tf_op jit(solution)/shard_map/ppermute | solution.py:355
  9.3 3.5 %convert_element_type.16 = f32[1,460800]{1,0:T(1,128)S(1)} convert(bf16[1,460800]{1,0:T(2,128)(2,1)} %param.10) | non-fusion elementwise | flops 460800 | bytes 2764800 | tf_op jit(solution)/shard_map/convert_element_type | solution.py:237
  13.4 12.6 %collective-permute-start.1 = (bf16[480,960]{1,0:T(8,128)(2,1)S(1)}, bf16[480,960]{1,0:T(8,128)(2,1)S(1)}, u32[]{:S(2)}, u32[]{:S(2)}) collective-permute-start(bf16[480,960]{1,0:T(8,128)(2,1)S(1)} %relay.1.mine_ref), channel_id=1, source_target_pairs={{0,1},{1,0},{2,3},{3,2},{4,5},{5,4},{6,7},{7,6},{8,9},{9,8},{10,11... | collective-permute-start | bytes 2764808 | tf_op jit(solution)/shard_map/ppermute | solution.py:358
  26.9 1.8 %all-gather = f32[16,160]{1,0:T(8,128)S(1)} all-gather(f32[8,160]{1,0:T(8,128)S(1)} %pad_maximum_fusion), channel_id=2, replica_groups=mesh['comp'=4,'band'=64,'cores'=2] {'cores'}, dimensions={0}, use_global_device_ids=true | all-gather | bytes 15360 | tf_op jit(solution)/shard_map/all_gather | solution.py:360
  31.0 3.3 %step0.1 = (bf16[320,512]{1,0:T(8,128)(2,1)S(1)}, f32[3,8,512]{2,1,0:T(8,128)S(1)}, f32[8,512]{1,0:T(8,128)S(1)}) custom-call(f32[2,3]{1,0:T(2,128)S(1)} %get-tuple-element.46.coef_ref, bf16[3,16,128]{2,1,0:T(8,128)(2,1)S(1)} %broadcast_in_dim.10.input_ref, f32[2,8,512]{2,1,0:T(8,128)S(1)} %get-tuple-element.19.state_in_ref, ...), custom_call_target="tpu_custom_call" | custom-call | tf_op jit(solution)/shard_map/step0/pallas_call | solution.py:285
  34.3 1.3 %collective-permute-start.2 = (f32[8,512]{1,0:T(8,128)S(1)}, f32[8,512]{1,0:T(8,128)S(1)}, u32[]{:S(2)}, u32[]{:S(2)}) collective-permute-start(f32[8,512]{1,0:T(8,128)S(1)} %get-tuple-element.24), channel_id=1, source_target_pairs={{384,0},{385,1},{386,2},{387,3},{388,4},{389,5},{390,6},{391,7},{3... | collective-permute-start | bytes 49160 | tf_op jit(solution)/shard_map/ppermute | solution.py:380
  36.9 1.3 %collective-permute-start.4 = (bf16[320,512]{1,0:T(8,128)(2,1)S(1)}, bf16[320,512]{1,0:T(8,128)(2,1)S(1)}, u32[]{:S(2)}, u32[]{:S(2)}) collective-permute-start(bf16[320,512]{1,0:T(8,128)(2,1)S(1)} %get-tuple-element.28), channel_id=1, source_target_pairs={{1,130},{2,129},{3,132},{4,131},{5,134},{6,133},{7,136},{8,135},{9... | collective-permute-start | bytes 983048 | tf_op jit(solution)/shard_map/ppermute | solution.py:377
  38.2 1.5 %collective-permute-start.5 = (bf16[320,512]{1,0:T(8,128)(2,1)S(1)}, bf16[320,512]{1,0:T(8,128)(2,1)S(1)}, u32[]{:S(2)}, u32[]{:S(2)}) collective-permute-start(bf16[320,512]{1,0:T(8,128)(2,1)S(1)} %get-tuple-element.28), channel_id=1, source_target_pairs={{0,128},{1,129},{2,130},{3,131},{4,132},{5,133},{6,134},{7,135},{8... | collective-permute-start | bytes 983048 | tf_op jit(solution)/shard_map/ppermute | solution.py:378
  40.6 6.3 %all-gather.1 = f32[16,512]{1,0:T(8,128)S(1)} all-gather(f32[8,512]{1,0:T(8,128)S(1)} %collective-permute-done.2), channel_id=3, replica_groups=mesh['comp'=4,'band'=64,'cores'=2] {'cores'}, dimensions={0}, use_global_device_ids=true | all-gather | bytes 49152 | tf_op jit(solution)/shard_map/all_gather | solution.py:380
  46.9 1.4 %latent.2 = (bf16[3,320,512]{2,1,0:T(8,128)(2,1)S(1)}, f32[3,8,512]{2,1,0:T(8,128)S(1)}) custom-call(f32[2,3]{1,0:T(2,128)S(1)} %get-tuple-element.46.coef_ref, f32[2,8,512]{2,1,0:T(8,128)S(1)} %bitcast.40, f32[8,512]{1,0:T(8,128)S(1)} %collective-permute-done.3.noise_edge_ref, f32[3,8,512]{2,1,0:T(8,128)S(1)} %copy_row.2.state_in_ref, ...), custom_call_target="tpu_custom_call" | custom-call | flops 3000000000 | tf_op jit(solution)/shard_map/latent/pallas_call | solution.py:256
  48.3 4.2 %all-gather.2 = bf16[640,512]{1,0:T(8,128)(2,1)S(1)} all-gather(bf16[320,512]{1,0:T(8,128)(2,1)S(1)} %collective-permute-done.5), channel_id=4, replica_groups=mesh['comp'=4,'band'=64,'cores'=2] {'cores'}, dimensions={0}, use_global_device_ids=true | all-gather | bytes 983040 | tf_op jit(solution)/shard_map/all_gather | solution.py:379
  52.5 2.3 %step1.1 = (bf16[320,512]{1,0:T(8,128)(2,1)S(1)}, f32[3,8,512]{2,1,0:T(8,128)S(1)}, f32[8,512]{1,0:T(8,128)S(1)}) custom-call(f32[2,3]{1,0:T(2,128)S(1)} %get-tuple-element.46.coef_ref, bf16[3,320,512]{2,1,0:T(8,128)(2,1)S(1)} %get-tuple-element.26.input_ref, f32[3,8,512]{2,1,0:T(8,128)S(1)} %get-tuple-element.27.state_in_ref, ...), custom_call_target="tpu_custom_call" | custom-call | tf_op jit(solution)/shard_map/step1/pallas_call | solution.py:285
  57.4 1.6 %collective-permute-start.8 = (bf16[320,512]{1,0:T(8,128)(2,1)S(1)}, bf16[320,512]{1,0:T(8,128)(2,1)S(1)}, u32[]{:S(2)}, u32[]{:S(2)}) collective-permute-start(bf16[320,512]{1,0:T(8,128)(2,1)S(1)} %get-tuple-element.33), channel_id=1, source_target_pairs={{1,130},{2,129},{3,132},{4,131},{5,134},{6,133},{7,136},{8,135},{9... | collective-permute-start | bytes 983048 | tf_op jit(solution)/shard_map/ppermute | solution.py:377
  59.0 5.4 %collective-permute-start.9 = (bf16[320,512]{1,0:T(8,128)(2,1)S(1)}, bf16[320,512]{1,0:T(8,128)(2,1)S(1)}, u32[]{:S(2)}, u32[]{:S(2)}) collective-permute-start(bf16[320,512]{1,0:T(8,128)(2,1)S(1)} %get-tuple-element.33), channel_id=1, source_target_pairs={{0,128},{1,129},{2,130},{3,131},{4,132},{5,133},{6,134},{7,135},{8... | collective-permute-start | bytes 983048 | tf_op jit(solution)/shard_map/ppermute | solution.py:378
  64.5 7.7 %all-gather.3 = f32[16,512]{1,0:T(8,128)S(1)} all-gather(f32[8,512]{1,0:T(8,128)S(1)} %collective-permute-done.6), channel_id=5, replica_groups=mesh['comp'=4,'band'=64,'cores'=2] {'cores'}, dimensions={0}, use_global_device_ids=true | all-gather | bytes 49152 | tf_op jit(solution)/shard_map/all_gather | solution.py:380
  72.2 1.4 %latent.3 = (bf16[3,320,512]{2,1,0:T(8,128)(2,1)S(1)}, f32[3,8,512]{2,1,0:T(8,128)S(1)}) custom-call(f32[2,3]{1,0:T(2,128)S(1)} %get-tuple-element.47.coef_ref, f32[2,8,512]{2,1,0:T(8,128)S(1)} %bitcast.39, f32[8,512]{1,0:T(8,128)S(1)} %collective-permute-done.7.noise_edge_ref, f32[3,8,512]{2,1,0:T(8,128)S(1)} %copy_row.3.state_in_ref, ...), custom_call_target="tpu_custom_call" | custom-call | flops 3000000000 | tf_op jit(solution)/shard_map/latent/pallas_call | solution.py:256
  73.6 3.7 %all-gather.4 = bf16[640,512]{1,0:T(8,128)(2,1)S(1)} all-gather(bf16[320,512]{1,0:T(8,128)(2,1)S(1)} %collective-permute-done.9), channel_id=6, replica_groups=mesh['comp'=4,'band'=64,'cores'=2] {'cores'}, dimensions={0}, use_global_device_ids=true | all-gather | bytes 983040 | tf_op jit(solution)/shard_map/all_gather | solution.py:379
  77.3 2.9 %step2.1 = (bf16[320,512]{1,0:T(8,128)(2,1)S(1)}, f32[3,8,512]{2,1,0:T(8,128)}, f32[8,512]{1,0:T(8,128)S(1)}) custom-call(f32[2,3]{1,0:T(2,128)S(1)} %get-tuple-element.47.coef_ref, bf16[3,320,512]{2,1,0:T(8,128)(2,1)S(1)} %get-tuple-element.31.input_ref, f32[3,8,512]{2,1,0:T(8,128)S(1)} %get-tuple-element.32.state_in_ref, ...), custom_call_target="tpu_custom_call" | custom-call | tf_op jit(solution)/shard_map/step2/pallas_call | solution.py:285
  80.2 13.0 %psum.7 = f32[4,512]{1,0:T(4,128)S(1)} all-reduce(f32[4,512]{1,0:T(4,128)S(1)} %slice.54), channel_id=1, replica_groups=mesh['comp'=4,'band'=64,'cores'=2] {'comp'}, use_global_device_ids=true, to_apply=%region_0.1 | all-reduce | flops 2048 | bytes 16384 | tf_op jit(solution)/shard_map/psum | solution.py:392
  93.2 3.9 %all-gather.6 = f32[2,1,512]{2,1,0:T(1,128)S(1)} all-gather(f32[1,1,512]{2,1,0:T(1,128)S(1)} %dynamic-slice_bitcast_fusion), channel_id=1, replica_groups=mesh['comp'=4,'band'=64,'cores'=2] {'cores'}, dimensions={0}, use_global_device_ids=true | all-gather | bytes 6144 | tf_op jit(solution)/shard_map/all_gather | solution.py:393
  97.7 2.3 %all-gather.5 = bf16[640,512]{1,0:T(8,128)(2,1)S(1)} all-gather(bf16[320,512]{1,0:T(8,128)(2,1)S(1)} %get-tuple-element.35), channel_id=7, replica_groups=mesh['comp'=4,'band'=64,'cores'=2] {'cores'}, dimensions={0}, use_global_device_ids=true | all-gather | bytes 983040 | tf_op jit(solution)/shard_map/all_gather | solution.py:387
  100.4 1.4 %reshape.19 = bf16[1,2,2,38400]{3,2,1,0:T(2,128)(2,1)} reshape(bf16[2,2,160,240]{3,2,1,0:T(8,128)(2,1)S(1)} %copy.44) | data formatting | bytes 614400 | tf_op jit(solution)/shard_map/reshape | solution.py:390
  (58 shorter events, 10.3 us)
Async XLA Ops:
  0.6 25.5 %copy-start = (f32[1000]{0:T(1024)S(1)}, f32[1000]{0:T(1024)}, u32[]{:S(2)}) copy-start(f32[1000]{0:T(1024)} %param.13) | copy-start | bytes 12004
  4.9 0.7 copy-start.1
  5.8 25.2 %collective-permute-start = (bf16[336,512]{1,0:T(8,128)(2,1)S(1)}, bf16[336,512]{1,0:T(8,128)(2,1)S(1)}, u32[]{:S(2)}, u32[]{:S(2)}) collective-permute-start(bf16[336,512]{1,0:T(8,128)(2,1)S(1)} %get-tuple-element.21), channel_id=1, source_target_pairs={{1,2},{2,1},{3,4},{4,3},{5,6},{6,5},{7,8},{8,7},{9,10},{10,9},{11,... | collective-permute-start | bytes 1032200 | tf_op jit(solution)/shard_map/ppermute | solution.py:355
  12.8 13.2 %copy-start.4 = (s32[4]{0:T(128)S(1)}, s32[4]{0:T(128)}, u32[]{:S(2)}) copy-start(s32[4]{0:T(128)} %param.12) | copy-start | bytes 52
  12.8 14.0 %copy-start.3 = (bf16[160,4]{0,1:T(4,128)(2,1)S(1)}, bf16[160,4]{0,1:T(4,128)(2,1)}, u32[]{:S(2)}) copy-start(bf16[160,4]{0,1:T(4,128)(2,1)} %param.11) | copy-start | bytes 3844
  12.9 14.0 %copy-start.2 = (f32[4,160]{1,0:T(4,128)S(1)}, f32[4,160]{1,0:T(4,128)}, u32[]{:S(2)}) copy-start(f32[4,160]{1,0:T(4,128)} %param.9) | copy-start | bytes 7684
  13.4 17.6 %collective-permute-start.1 = (bf16[480,960]{1,0:T(8,128)(2,1)S(1)}, bf16[480,960]{1,0:T(8,128)(2,1)S(1)}, u32[]{:S(2)}, u32[]{:S(2)}) collective-permute-start(bf16[480,960]{1,0:T(8,128)(2,1)S(1)} %relay.1.mine_ref), channel_id=1, source_target_pairs={{0,1},{1,0},{2,3},{3,2},{4,5},{5,4},{6,7},{7,6},{8,9},{9,8},{10,11... | collective-permute-start | bytes 2764808 | tf_op jit(solution)/shard_map/ppermute | solution.py:358
  34.3 6.3 %collective-permute-start.2 = (f32[8,512]{1,0:T(8,128)S(1)}, f32[8,512]{1,0:T(8,128)S(1)}, u32[]{:S(2)}, u32[]{:S(2)}) collective-permute-start(f32[8,512]{1,0:T(8,128)S(1)} %get-tuple-element.24), channel_id=1, source_target_pairs={{384,0},{385,1},{386,2},{387,3},{388,4},{389,5},{390,6},{391,7},{3... | collective-permute-start | bytes 49160 | tf_op jit(solution)/shard_map/ppermute | solution.py:380
  35.6 11.3 %collective-permute-start.3 = (f32[8,512]{1,0:T(8,128)S(1)}, f32[8,512]{1,0:T(8,128)S(1)}, u32[]{:S(2)}, u32[]{:S(2)}) collective-permute-start(f32[8,512]{1,0:T(8,128)S(1)} %get-tuple-element.24), channel_id=1, source_target_pairs={{385,2},{386,1},{387,4},{388,3},{389,6},{390,5},{391,8},{392,7},{3... | collective-permute-start | bytes 49160 | tf_op jit(solution)/shard_map/ppermute | solution.py:381
  36.9 15.6 %collective-permute-start.4 = (bf16[320,512]{1,0:T(8,128)(2,1)S(1)}, bf16[320,512]{1,0:T(8,128)(2,1)S(1)}, u32[]{:S(2)}, u32[]{:S(2)}) collective-permute-start(bf16[320,512]{1,0:T(8,128)(2,1)S(1)} %get-tuple-element.28), channel_id=1, source_target_pairs={{1,130},{2,129},{3,132},{4,131},{5,134},{6,133},{7,136},{8,135},{9... | collective-permute-start | bytes 983048 | tf_op jit(solution)/shard_map/ppermute | solution.py:377
  38.2 10.1 %collective-permute-start.5 = (bf16[320,512]{1,0:T(8,128)(2,1)S(1)}, bf16[320,512]{1,0:T(8,128)(2,1)S(1)}, u32[]{:S(2)}, u32[]{:S(2)}) collective-permute-start(bf16[320,512]{1,0:T(8,128)(2,1)S(1)} %get-tuple-element.28), channel_id=1, source_target_pairs={{0,128},{1,129},{2,130},{3,131},{4,132},{5,133},{6,134},{7,135},{8... | collective-permute-start | bytes 983048 | tf_op jit(solution)/shard_map/ppermute | solution.py:378
  54.8 9.7 %collective-permute-start.6 = (f32[8,512]{1,0:T(8,128)S(1)}, f32[8,512]{1,0:T(8,128)S(1)}, u32[]{:S(2)}, u32[]{:S(2)}) collective-permute-start(f32[8,512]{1,0:T(8,128)S(1)} %get-tuple-element.29), channel_id=1, source_target_pairs={{384,0},{385,1},{386,2},{387,3},{388,4},{389,5},{390,6},{391,7},{3... | collective-permute-start | bytes 49160 | tf_op jit(solution)/shard_map/ppermute | solution.py:380
  56.1 16.0 %collective-permute-start.7 = (f32[8,512]{1,0:T(8,128)S(1)}, f32[8,512]{1,0:T(8,128)S(1)}, u32[]{:S(2)}, u32[]{:S(2)}) collective-permute-start(f32[8,512]{1,0:T(8,128)S(1)} %get-tuple-element.29), channel_id=1, source_target_pairs={{385,2},{386,1},{387,4},{388,3},{389,6},{390,5},{391,8},{392,7},{3... | collective-permute-start | bytes 49160 | tf_op jit(solution)/shard_map/ppermute | solution.py:381
  57.4 19.9 %collective-permute-start.8 = (bf16[320,512]{1,0:T(8,128)(2,1)S(1)}, bf16[320,512]{1,0:T(8,128)(2,1)S(1)}, u32[]{:S(2)}, u32[]{:S(2)}) collective-permute-start(bf16[320,512]{1,0:T(8,128)(2,1)S(1)} %get-tuple-element.33), channel_id=1, source_target_pairs={{1,130},{2,129},{3,132},{4,131},{5,134},{6,133},{7,136},{8,135},{9... | collective-permute-start | bytes 983048 | tf_op jit(solution)/shard_map/ppermute | solution.py:377
  59.0 14.6 %collective-permute-start.9 = (bf16[320,512]{1,0:T(8,128)(2,1)S(1)}, bf16[320,512]{1,0:T(8,128)(2,1)S(1)}, u32[]{:S(2)}, u32[]{:S(2)}) collective-permute-start(bf16[320,512]{1,0:T(8,128)(2,1)S(1)} %get-tuple-element.33), channel_id=1, source_target_pairs={{0,128},{1,129},{2,130},{3,131},{4,132},{5,133},{6,134},{7,135},{8... | collective-permute-start | bytes 983048 | tf_op jit(solution)/shard_map/ppermute | solution.py:378

commit v4 on v3

--- a/solution.py
+++ b/solution.py
@@ -101,28 +101,42 @@
 
 
 def latent_kernel(
-    core, plane, coef_ref, noise_ref, noise_edge_ref, state_in_ref, in_weight_ref, cond_ref, cond_edge_ref, input_ref, state_ref
+    core,
+    plane,
+    coef_ref,
+    noise_ref,
+    noise_edge_ref,
+    local_ref,
+    state_in_ref,
+    in_weight_ref,
+    cond_ref,
+    cond_edge_ref,
+    input_ref,
+    state_ref,
 ):
     me = core()
     at = plane()
 
+    rate, scale_now, scale_next = (coef_ref[0, n] for n in range(3))
+
+    def moved(state, noise):
+        return rate * (state - scale_now * noise) + scale_next * noise
+
     @pl.when(at == 0)
     def _():
-        rate, scale_now, scale_next = (coef_ref[0, n] for n in range(3))
         for slot, noise_row, cond in (
             (1 - me, noise_ref.at[0], cond_ref.at[0]),
             (2 - me, noise_ref.at[1], cond_ref.at[1]),
             (2 * me, noise_edge_ref, cond_edge_ref),
         ):
-            noise = noise_row[...]
-            state = state_in_ref[slot]
-            state = rate * (state - scale_now * noise) + scale_next * noise
+            state = moved(state_in_ref[slot], noise_row[...])
             state_ref[slot] = state
             project(slot, state, cond, in_weight_ref, input_ref)
 
     @pl.when(at != 0)
     def _():
         state_ref[...] = jnp.zeros_like(state_ref)
+        state_ref[1] = moved(state_in_ref[1], local_ref[...])
 
 
 def edge_kernel(edge_ref, out_ref):
@@ -135,10 +149,10 @@
     core,
     plane,
     coef_ref,
+    edge_ref,
+    rec_ref,
     input_ref,
     state_in_ref,
-    edge_ref,
-    rec_ref,
     in_weight_ref,
     out_weight_ref,
     mine_ref,
@@ -176,14 +190,15 @@
                 state_ref[slot] = state
                 project(slot, state, cond, in_weight_ref, raw)
         else:
-            state_ref[...] = state_in_ref[...]
             raw[...] = input_ref[...]
         for slot in range(3):
             activate(slot, lambda chunk, slot=slot: swish(raw[slot, chunk : chunk + 64, :]))
 
     @pl.when(at != 0)
     def _():
-        state_ref[...] = jnp.zeros_like(state_ref)
+        if step == 0:
+            state_ref[...] = jnp.zeros_like(state_ref)
+            state_ref[1] = state_in_ref[me]
         raw[1] = rec_ref[me]
         for row in range(2):
             activate(row + 1 - me, lambda chunk, row=row: swish(rec_ref[row, chunk : chunk + 64, :]))
@@ -200,20 +215,17 @@
             total = total + raw[1, channels, :].astype(jnp.float32)
             out_ref[channels, :] = jnp.where(inside, total, 0.0).astype(jnp.bfloat16)
 
+    if step > 0:
+        state_ref[...] = state_in_ref[...]
     final_ref[...] = jnp.zeros_like(final_ref)
 
     @pl.when(at == 3)
     def _():
         noise = jnp.dot(out_weight_ref[...], out_ref[...], preferred_element_type=jnp.float32)[0:8]
         if step == STEPS - 1:
-            noise = (coef_ref[1, 2] - coef_ref[1, 0] * coef_ref[1, 1]) * noise
+            rate, scale_now, scale_next = (coef_ref[1, n] for n in range(3))
+            noise = rate * (state_in_ref[1] - scale_now * noise) + scale_next * noise
         final_ref[...] = noise
-
-    if step == STEPS - 1:
-
-        @pl.when(at == 0)
-        def _():
-            final_ref[...] = coef_ref[1, 0] * state_ref[1]
 
 
 def prepare(feats, latent):
@@ -250,7 +262,7 @@
     return pl.CostEstimate(flops=int(micros * 1e9), bytes_accessed=0, transcendentals=0)
 
 
-def run_latent(coefs, noise, noise_edge, state, in_weight, cond, cond_edge):
+def run_latent(coefs, noise, noise_edge, local, state, in_weight, cond, cond_edge):
     core = functools.partial(lax.axis_index, "cores")
     plane = functools.partial(lax.axis_index, "comp")
     return pl.pallas_call(
@@ -259,12 +271,12 @@
             jax.ShapeDtypeStruct((3, 320, 2 * FRAME), jnp.bfloat16),
             jax.ShapeDtypeStruct((3, 8, 2 * FRAME), jnp.float32),
         ],
-        in_specs=[pl.BlockSpec(memory_space=pltpu.SMEM)] + [in_vmem()] * 6,
+        in_specs=[pl.BlockSpec(memory_space=pltpu.SMEM)] + [in_vmem()] * 7,
         out_specs=[in_vmem()] * 2,
         compiler_params=params(),
         cost_estimate=hint(3),
         name="latent",
-    )(coefs, noise, noise_edge, state, in_weight, cond, cond_edge)
+    )(coefs, noise, noise_edge, local, state, in_weight, cond, cond_edge)
 
 
 def run_edge(edge):
@@ -298,7 +310,7 @@
         ],
         compiler_params=params(),
         name=f"step{step}",
-    )(coefs, inputs, state, edge, rec, in_weight, out_weight, mine, other)
+    )(coefs, edge, rec, inputs, state, in_weight, out_weight, mine, other)
 
 
 def copy_kernel(in_ref, out_ref):
@@ -324,6 +336,7 @@
     edges, swap = [], []
     onward, diagonals = [], []
     noise_onward, noise_diagonals = [], []
+    noise_first, noise_second = [], []
     for comp in range(comps):
         last = comp == comps - 1
         later = 0 if last else comp + 1
@@ -331,18 +344,21 @@
             for core in range(2):
                 me = index(comp, band, core)
                 (noise_onward if last else onward).append((me, index(later, band, core)))
+                if last:
+                    noise_first.append((me, index(1, band, core)))
+                    noise_second.append((me, index(2, band, core)))
                 swap.append((me, index(comp, band, 1 - core)))
                 reached = band + 2 * core - 1
                 if 0 <= reached < bands:
                     edges.append((me, index(comp, reached, 1 - core)))
                     pair = (me, index(later, reached, 1 - core))
                     (noise_diagonals if last else diagonals).append(pair)
-    return edges, swap, onward, diagonals, noise_onward, noise_diagonals
+    return edges, swap, onward, diagonals, noise_onward, noise_diagonals, noise_first, noise_second
 
 
 def body(latent, section_inputs, in_weight, conv_weight, out_weight, timesteps, plan):
     axes = ("comp", "band", "cores")
-    edges, swap, onward, diagonals, noise_onward, noise_diagonals = links(
+    edges, swap, onward, diagonals, noise_onward, noise_diagonals, noise_first, noise_second = links(
         lax.axis_size("comp"), lax.axis_size("band")
     )
     plane = lax.axis_index("comp")
@@ -381,7 +397,14 @@
             noise_edge = lax.ppermute(final, axes, noise_diagonals)
             state = copied(state)
             inputs, state = run_latent(
-                coefs[step : step + 2], noise, noise_edge, state, in_columns, cond, cond_edge
+                coefs[step : step + 2],
+                noise,
+                noise_edge,
+                final,
+                state,
+                in_columns,
+                cond,
+                cond_edge,
             )
 
     whole = lax.all_gather(out, "cores")
@@ -389,7 +412,9 @@
     share = share.reshape(2, 160, 2, FRAME)[..., :240].transpose(2, 0, 1, 3)
     handoff = share.reshape(1, 2, 2, 160 * 240)
 
-    total = lax.psum(final[0:4], "comp")
+    total = final
+    for pairs in (noise_onward, noise_first, noise_second):
+        total = total + lax.ppermute(final, axes, pairs)
     total = lax.all_gather(lax.dynamic_slice_in_dim(total, plane, 1, axis=0)[0], "cores")
     denoised = total.reshape(2, 2, FRAME)[..., :240].transpose(1, 0, 2)[:, None]
     return denoised, handoff

time: 103 us -> 98.2 us (0.953)
  blocking collectives: 45.4 us -> 30.4 us
  waiting for transfers between devices: 0.91 us -> 12.3 us
    psum x1 -> x0, blocking collectives: 13 us -> none  [body(): total = lax.psum(final[0:4], 'comp')]
    ppermute x2, waiting for transfers between devices: 0.89 us -> 11.3 us  [body(): noise = lax.all_gather(lax.ppermute(final, axes, noise_onward), 'cores')]
    ppermute x2, starting transfers between devices: 6.91 us -> 4.04 us  [body(): rec = lax.ppermute(out, axes, onward)]
    ppermute x0 -> x3, starting transfers between devices: none -> 2.6 us  [body(): total = total + lax.ppermute(final, axes, pairs)]
    unnamed x13 -> x12, local copies, waits for them, and re-layouts: 2.17 us -> 2.16 us
  transfers between devices with their start and end apart: 10 -> 13, of which waited for: 1 -> 3; matrix products, arithmetic and copies ran while one was open for 6% -> 9% of each run, Pallas kernels for 3% -> 3%
where the time goes in v4:
time: 98.2 us; the launch traced here: 97.6 us
  starting transfers between devices  30.5 us (31%)
  blocking collectives  30.4 us (31%)
  waiting for transfers between devices  12.3 us (13%)
  Pallas kernels  12 us (12%)
  local copies, waits for them, and re-layouts  7.54 us (8%)
  other arithmetic  3.91 us (4%)
    all_gather x2, blocking collectives, body(): noise = lax.all_gather(lax.ppermute(final, axes, noise_onward), 'cores')  13.6 us
    ppermute x1, starting transfers between devices, body(): other = lax.ppermute(mine, axes, swap)  12.6 us
    ppermute x2, waiting for transfers between devices, body(): noise = lax.all_gather(lax.ppermute(final, axes, noise_onward), 'cores')  11.3 us
    pallas_call x3, Pallas kernels, run_step(): pl.pallas_call(functools.partial(step_kernel, step, core, plane), out_sha...  8.44 us
    all_gather x2, blocking collectives, body(): rec = lax.all_gather(rec, 'cores')  7.13 us
    ppermute x2, starting transfers between devices, body(): rec = lax.ppermute(out, axes, onward)  4.04 us
    convert_element_type x1, other arithmetic, relaid_weight(): weight.astype(jnp.float32)  3.53 us
    ppermute x1, starting transfers between devices, body(): cond_edge = lax.ppermute(message, axes, edges)  3.46 us
  transfers between devices with their start and end apart: 13, of which 3 were waited for; matrix products, arithmetic and copies ran while one was open for 9% of the time, Pallas kernels for 3%

profile of v4, /device:TPU:7, one launch (start us, length us, event | category | flops | bytes accessed | tf_op | source)
XLA Modules:
  0.0 97.6 jit_solution(9038039895542317857)
XLA Ops:
  0.6 1.7 %all_gather_reshape_squeeze.3 = bf16[1,2,2,160,240]{4,3,2,1,0:T(8,128)(2,1)S(1)} reshape(bf16[1,2,2,38400]{3,2,1,0:T(2,128)(2,1)} %param.8) | data formatting | bytes 614400 | tf_op jit(solution)/shard_map/all_gather;reshape;squeeze | solution.py:368
  2.4 2.6 %all_gather.42.feat_ref = bf16[2,2,2,160,240]{4,3,2,1,0:T(8,128)(2,1)S(1)} all-gather(bf16[1,2,2,160,240]{4,3,2,1,0:T(8,128)(2,1)S(1)} %all_gather_reshape_squeeze.3), channel_id=1, replica_groups=mesh['comp'=4,'band'=64,'cores'=2] {'cores'}, dimensions={0}, use_global_device_ids=true | all-gather | bytes 921600 | tf_op jit(solution)/shard_map/all_gather | solution.py:368
  5.8 3.5 %collective-permute-start = (bf16[336,512]{1,0:T(8,128)(2,1)S(1)}, bf16[336,512]{1,0:T(8,128)(2,1)S(1)}, u32[]{:S(2)}, u32[]{:S(2)}) collective-permute-start(bf16[336,512]{1,0:T(8,128)(2,1)S(1)} %get-tuple-element.20), channel_id=1, source_target_pairs={{1,2},{2,1},{3,4},{4,3},{5,6},{6,5},{7,8},{8,7},{9,10},{10,9},{11,... | collective-permute-start | bytes 1032200 | tf_op jit(solution)/shard_map/ppermute | solution.py:371
  9.3 3.5 %convert_element_type.16 = f32[1,460800]{1,0:T(1,128)S(1)} convert(bf16[1,460800]{1,0:T(2,128)(2,1)} %param.10) | non-fusion elementwise | flops 460800 | bytes 2764800 | tf_op jit(solution)/shard_map/convert_element_type | solution.py:249
  13.4 12.6 %collective-permute-start.1 = (bf16[480,960]{1,0:T(8,128)(2,1)S(1)}, bf16[480,960]{1,0:T(8,128)(2,1)S(1)}, u32[]{:S(2)}, u32[]{:S(2)}) collective-permute-start(bf16[480,960]{1,0:T(8,128)(2,1)S(1)} %relay.1.mine_ref), channel_id=1, source_target_pairs={{0,1},{1,0},{2,3},{3,2},{4,5},{5,4},{6,7},{7,6},{8,9},{9,8},{10,11... | collective-permute-start | bytes 2764808 | tf_op jit(solution)/shard_map/ppermute | solution.py:374
  26.9 1.8 %all-gather = f32[16,160]{1,0:T(8,128)S(1)} all-gather(f32[8,160]{1,0:T(8,128)S(1)} %pad_maximum_fusion), channel_id=2, replica_groups=mesh['comp'=4,'band'=64,'cores'=2] {'cores'}, dimensions={0}, use_global_device_ids=true | all-gather | bytes 15360 | tf_op jit(solution)/shard_map/all_gather | solution.py:376
  31.0 3.3 %step0.1 = (bf16[320,512]{1,0:T(8,128)(2,1)S(1)}, f32[3,8,512]{2,1,0:T(8,128)S(1)}, f32[8,512]{1,0:T(8,128)S(1)}) custom-call(f32[2,3]{1,0:T(2,128)S(1)} %get-tuple-element.46.coef_ref, bf16[336,512]{1,0:T(8,128)(2,1)S(1)} %collective-permute-done.edge_ref.cond_edge_ref, bf16[2,320,512]{2,1,0:T(8,128)(2,1)S(1)} %get-tuple-element.21.rec_ref.cond_ref, ...), custom_call_target="tpu_custom_call" | custom-call | tf_op jit(solution)/shard_map/step0/pallas_call | solution.py:297
  34.3 1.3 %collective-permute-start.2 = (bf16[320,512]{1,0:T(8,128)(2,1)S(1)}, bf16[320,512]{1,0:T(8,128)(2,1)S(1)}, u32[]{:S(2)}, u32[]{:S(2)}) collective-permute-start(bf16[320,512]{1,0:T(8,128)(2,1)S(1)} %get-tuple-element.24), channel_id=1, source_target_pairs={{1,130},{2,129},{3,132},{4,131},{5,134},{6,133},{7,136},{8,135},{9... | collective-permute-start | bytes 983048 | tf_op jit(solution)/shard_map/ppermute | solution.py:393
  35.6 2.7 %collective-permute-start.3 = (bf16[320,512]{1,0:T(8,128)(2,1)S(1)}, bf16[320,512]{1,0:T(8,128)(2,1)S(1)}, u32[]{:S(2)}, u32[]{:S(2)}) collective-permute-start(bf16[320,512]{1,0:T(8,128)(2,1)S(1)} %get-tuple-element.24), channel_id=1, source_target_pairs={{0,128},{1,129},{2,130},{3,131},{4,132},{5,133},{6,134},{7,135},{8... | collective-permute-start | bytes 983048 | tf_op jit(solution)/shard_map/ppermute | solution.py:394
  41.0 7.7 %collective-permute-done.4 = f32[8,512]{1,0:T(8,128)S(1)} collective-permute-done((f32[8,512]{1,0:T(8,128)S(1)}, f32[8,512]{1,0:T(8,128)S(1)}, u32[]{:S(2)}, u32[]{:S(2)}) %collective-permute-start.4) | collective-permute-done | bytes 16416 | tf_op jit(solution)/shard_map/ppermute | solution.py:396
  48.6 4.3 %all-gather.2 = f32[16,512]{1,0:T(8,128)S(1)} all-gather(f32[8,512]{1,0:T(8,128)S(1)} %collective-permute-done.4), channel_id=4, replica_groups=mesh['comp'=4,'band'=64,'cores'=2] {'cores'}, dimensions={0}, use_global_device_ids=true | all-gather | bytes 49152 | tf_op jit(solution)/shard_map/all_gather | solution.py:396
  53.0 1.4 %latent.2 = (bf16[3,320,512]{2,1,0:T(8,128)(2,1)S(1)}, f32[3,8,512]{2,1,0:T(8,128)S(1)}) custom-call(f32[2,3]{1,0:T(2,128)S(1)} %get-tuple-element.46.coef_ref, f32[2,8,512]{2,1,0:T(8,128)S(1)} %bitcast.40, f32[8,512]{1,0:T(8,128)S(1)} %collective-permute-done.5.noise_edge_ref, f32[8,512]{1,0:T(8,128)S(1)} %get-tuple-element.25.local_ref, ...), custom_call_target="tpu_custom_call" | custom-call | flops 3000000000 | tf_op jit(solution)/shard_map/latent/pallas_call | solution.py:268
  54.4 3.6 %all-gather.1 = bf16[640,512]{1,0:T(8,128)(2,1)S(1)} all-gather(bf16[320,512]{1,0:T(8,128)(2,1)S(1)} %collective-permute-done.3), channel_id=3, replica_groups=mesh['comp'=4,'band'=64,'cores'=2] {'cores'}, dimensions={0}, use_global_device_ids=true | all-gather | bytes 983040 | tf_op jit(solution)/shard_map/all_gather | solution.py:395
  58.0 2.3 %step1.1 = (bf16[320,512]{1,0:T(8,128)(2,1)S(1)}, f32[3,8,512]{2,1,0:T(8,128)S(1)}, f32[8,512]{1,0:T(8,128)S(1)}) custom-call(f32[2,3]{1,0:T(2,128)S(1)} %get-tuple-element.46.coef_ref, bf16[320,512]{1,0:T(8,128)(2,1)S(1)} %collective-permute-done.2.edge_ref, bf16[2,320,512]{2,1,0:T(8,128)(2,1)S(1)} %bitcast.38, ...), custom_call_target="tpu_custom_call" | custom-call | tf_op jit(solution)/shard_map/step1/pallas_call | solution.py:297
  60.3 1.3 %collective-permute-start.6 = (bf16[320,512]{1,0:T(8,128)(2,1)S(1)}, bf16[320,512]{1,0:T(8,128)(2,1)S(1)}, u32[]{:S(2)}, u32[]{:S(2)}) collective-permute-start(bf16[320,512]{1,0:T(8,128)(2,1)S(1)} %get-tuple-element.29), channel_id=1, source_target_pairs={{1,130},{2,129},{3,132},{4,131},{5,134},{6,133},{7,136},{8,135},{9... | collective-permute-start | bytes 983048 | tf_op jit(solution)/shard_map/ppermute | solution.py:393
  61.6 1.3 %collective-permute-start.7 = (bf16[320,512]{1,0:T(8,128)(2,1)S(1)}, bf16[320,512]{1,0:T(8,128)(2,1)S(1)}, u32[]{:S(2)}, u32[]{:S(2)}) collective-permute-start(bf16[320,512]{1,0:T(8,128)(2,1)S(1)} %get-tuple-element.29), channel_id=1, source_target_pairs={{0,128},{1,129},{2,130},{3,131},{4,132},{5,133},{6,134},{7,135},{8... | collective-permute-start | bytes 983048 | tf_op jit(solution)/shard_map/ppermute | solution.py:394
  65.5 3.7 %collective-permute-done.8 = f32[8,512]{1,0:T(8,128)S(1)} collective-permute-done((f32[8,512]{1,0:T(8,128)S(1)}, f32[8,512]{1,0:T(8,128)S(1)}, u32[]{:S(2)}, u32[]{:S(2)}) %collective-permute-start.8) | collective-permute-done | bytes 16416 | tf_op jit(solution)/shard_map/ppermute | solution.py:396
  69.2 9.3 %all-gather.4 = f32[16,512]{1,0:T(8,128)S(1)} all-gather(f32[8,512]{1,0:T(8,128)S(1)} %collective-permute-done.8), channel_id=6, replica_groups=mesh['comp'=4,'band'=64,'cores'=2] {'cores'}, dimensions={0}, use_global_device_ids=true | all-gather | bytes 49152 | tf_op jit(solution)/shard_map/all_gather | solution.py:396
  78.4 1.4 %latent.3 = (bf16[3,320,512]{2,1,0:T(8,128)(2,1)S(1)}, f32[3,8,512]{2,1,0:T(8,128)S(1)}) custom-call(f32[2,3]{1,0:T(2,128)S(1)} %get-tuple-element.47.coef_ref, f32[2,8,512]{2,1,0:T(8,128)S(1)} %bitcast.39, f32[8,512]{1,0:T(8,128)S(1)} %collective-permute-done.9.noise_edge_ref, f32[8,512]{1,0:T(8,128)S(1)} %get-tuple-element.30.local_ref, ...), custom_call_target="tpu_custom_call" | custom-call | flops 3000000000 | tf_op jit(solution)/shard_map/latent/pallas_call | solution.py:268
  79.9 3.6 %all-gather.3 = bf16[640,512]{1,0:T(8,128)(2,1)S(1)} all-gather(bf16[320,512]{1,0:T(8,128)(2,1)S(1)} %collective-permute-done.7), channel_id=5, replica_groups=mesh['comp'=4,'band'=64,'cores'=2] {'cores'}, dimensions={0}, use_global_device_ids=true | all-gather | bytes 983040 | tf_op jit(solution)/shard_map/all_gather | solution.py:395
  83.4 2.9 %step2.1 = (bf16[320,512]{1,0:T(8,128)(2,1)S(1)}, f32[3,8,512]{2,1,0:T(8,128)}, f32[8,512]{1,0:T(8,128)S(1)}) custom-call(f32[2,3]{1,0:T(2,128)S(1)} %get-tuple-element.47.coef_ref, bf16[320,512]{1,0:T(8,128)(2,1)S(1)} %collective-permute-done.6.edge_ref, bf16[2,320,512]{2,1,0:T(8,128)(2,1)S(1)} %bitcast.37, ...), custom_call_target="tpu_custom_call" | custom-call | tf_op jit(solution)/shard_map/step2/pallas_call | solution.py:297
  89.0 2.3 %all-gather.5 = bf16[640,512]{1,0:T(8,128)(2,1)S(1)} all-gather(bf16[320,512]{1,0:T(8,128)(2,1)S(1)} %get-tuple-element.35), channel_id=7, replica_groups=mesh['comp'=4,'band'=64,'cores'=2] {'cores'}, dimensions={0}, use_global_device_ids=true | all-gather | bytes 983040 | tf_op jit(solution)/shard_map/all_gather | solution.py:410
  91.6 1.4 %reshape.19 = bf16[1,2,2,38400]{3,2,1,0:T(2,128)(2,1)} reshape(bf16[2,2,160,240]{3,2,1,0:T(8,128)(2,1)S(1)} %copy.44) | data formatting | bytes 614400 | tf_op jit(solution)/shard_map/reshape | solution.py:413
  94.0 3.0 %all-gather.6 = f32[2,1,512]{2,1,0:T(1,128)S(1)} all-gather(f32[1,1,512]{2,1,0:T(1,128)S(1)} %fusion.3), channel_id=1, replica_groups=mesh['comp'=4,'band'=64,'cores'=2] {'cores'}, dimensions={0}, use_global_device_ids=true | all-gather | bytes 6144 | tf_op jit(solution)/shard_map/all_gather | solution.py:418
  (62 shorter events, 14.3 us)
Async XLA Ops:
  0.6 25.5 %copy-start = (f32[1000]{0:T(1024)S(1)}, f32[1000]{0:T(1024)}, u32[]{:S(2)}) copy-start(f32[1000]{0:T(1024)} %param.13) | copy-start | bytes 12004
  4.9 0.7 copy-start.1
  5.8 25.2 %collective-permute-start = (bf16[336,512]{1,0:T(8,128)(2,1)S(1)}, bf16[336,512]{1,0:T(8,128)(2,1)S(1)}, u32[]{:S(2)}, u32[]{:S(2)}) collective-permute-start(bf16[336,512]{1,0:T(8,128)(2,1)S(1)} %get-tuple-element.20), channel_id=1, source_target_pairs={{1,2},{2,1},{3,4},{4,3},{5,6},{6,5},{7,8},{8,7},{9,10},{10,9},{11,... | collective-permute-start | bytes 1032200 | tf_op jit(solution)/shard_map/ppermute | solution.py:371
  12.8 13.2 %copy-start.4 = (s32[4]{0:T(128)S(1)}, s32[4]{0:T(128)}, u32[]{:S(2)}) copy-start(s32[4]{0:T(128)} %param.12) | copy-start | bytes 52
  12.8 14.0 %copy-start.3 = (bf16[160,4]{0,1:T(4,128)(2,1)S(1)}, bf16[160,4]{0,1:T(4,128)(2,1)}, u32[]{:S(2)}) copy-start(bf16[160,4]{0,1:T(4,128)(2,1)} %param.11) | copy-start | bytes 3844
  12.9 14.0 %copy-start.2 = (f32[4,160]{1,0:T(4,128)S(1)}, f32[4,160]{1,0:T(4,128)}, u32[]{:S(2)}) copy-start(f32[4,160]{1,0:T(4,128)} %param.9) | copy-start | bytes 7684
  13.4 17.6 %collective-permute-start.1 = (bf16[480,960]{1,0:T(8,128)(2,1)S(1)}, bf16[480,960]{1,0:T(8,128)(2,1)S(1)}, u32[]{:S(2)}, u32[]{:S(2)}) collective-permute-start(bf16[480,960]{1,0:T(8,128)(2,1)S(1)} %relay.1.mine_ref), channel_id=1, source_target_pairs={{0,1},{1,0},{2,3},{3,2},{4,5},{5,4},{6,7},{7,6},{8,9},{9,8},{10,11... | collective-permute-start | bytes 2764808 | tf_op jit(solution)/shard_map/ppermute | solution.py:374
  34.3 23.7 %collective-permute-start.2 = (bf16[320,512]{1,0:T(8,128)(2,1)S(1)}, bf16[320,512]{1,0:T(8,128)(2,1)S(1)}, u32[]{:S(2)}, u32[]{:S(2)}) collective-permute-start(bf16[320,512]{1,0:T(8,128)(2,1)S(1)} %get-tuple-element.24), channel_id=1, source_target_pairs={{1,130},{2,129},{3,132},{4,131},{5,134},{6,133},{7,136},{8,135},{9... | collective-permute-start | bytes 983048 | tf_op jit(solution)/shard_map/ppermute | solution.py:393
  35.6 18.8 %collective-permute-start.3 = (bf16[320,512]{1,0:T(8,128)(2,1)S(1)}, bf16[320,512]{1,0:T(8,128)(2,1)S(1)}, u32[]{:S(2)}, u32[]{:S(2)}) collective-permute-start(bf16[320,512]{1,0:T(8,128)(2,1)S(1)} %get-tuple-element.24), channel_id=1, source_target_pairs={{0,128},{1,129},{2,130},{3,131},{4,132},{5,133},{6,134},{7,135},{8... | collective-permute-start | bytes 983048 | tf_op jit(solution)/shard_map/ppermute | solution.py:394
  38.4 10.3 %collective-permute-start.4 = (f32[8,512]{1,0:T(8,128)S(1)}, f32[8,512]{1,0:T(8,128)S(1)}, u32[]{:S(2)}, u32[]{:S(2)}) collective-permute-start(f32[8,512]{1,0:T(8,128)S(1)} %get-tuple-element.25.local_ref), channel_id=1, source_target_pairs={{384,0},{385,1},{386,2},{387,3},{388,4},{389,5},{390,6},{391,7},{3... | collective-permute-start | bytes 49160 | tf_op jit(solution)/shard_map/ppermute | solution.py:396
  39.7 13.3 %collective-permute-start.5 = (f32[8,512]{1,0:T(8,128)S(1)}, f32[8,512]{1,0:T(8,128)S(1)}, u32[]{:S(2)}, u32[]{:S(2)}) collective-permute-start(f32[8,512]{1,0:T(8,128)S(1)} %get-tuple-element.25.local_ref), channel_id=1, source_target_pairs={{385,2},{386,1},{387,4},{388,3},{389,6},{390,5},{391,8},{392,7},{3... | collective-permute-start | bytes 49160 | tf_op jit(solution)/shard_map/ppermute | solution.py:397
  60.3 23.2 %collective-permute-start.6 = (bf16[320,512]{1,0:T(8,128)(2,1)S(1)}, bf16[320,512]{1,0:T(8,128)(2,1)S(1)}, u32[]{:S(2)}, u32[]{:S(2)}) collective-permute-start(bf16[320,512]{1,0:T(8,128)(2,1)S(1)} %get-tuple-element.29), channel_id=1, source_target_pairs={{1,130},{2,129},{3,132},{4,131},{5,134},{6,133},{7,136},{8,135},{9... | collective-permute-start | bytes 983048 | tf_op jit(solution)/shard_map/ppermute | solution.py:393
  61.6 18.3 %collective-permute-start.7 = (bf16[320,512]{1,0:T(8,128)(2,1)S(1)}, bf16[320,512]{1,0:T(8,128)(2,1)S(1)}, u32[]{:S(2)}, u32[]{:S(2)}) collective-permute-start(bf16[320,512]{1,0:T(8,128)(2,1)S(1)} %get-tuple-element.29), channel_id=1, source_target_pairs={{0,128},{1,129},{2,130},{3,131},{4,132},{5,133},{6,134},{7,135},{8... | collective-permute-start | bytes 983048 | tf_op jit(solution)/shard_map/ppermute | solution.py:394
  62.9 6.3 %collective-permute-start.8 = (f32[8,512]{1,0:T(8,128)S(1)}, f32[8,512]{1,0:T(8,128)S(1)}, u32[]{:S(2)}, u32[]{:S(2)}) collective-permute-start(f32[8,512]{1,0:T(8,128)S(1)} %get-tuple-element.30.local_ref), channel_id=1, source_target_pairs={{384,0},{385,1},{386,2},{387,3},{388,4},{389,5},{390,6},{391,7},{3... | collective-permute-start | bytes 49160 | tf_op jit(solution)/shard_map/ppermute | solution.py:396
  64.2 14.2 %collective-permute-start.9 = (f32[8,512]{1,0:T(8,128)S(1)}, f32[8,512]{1,0:T(8,128)S(1)}, u32[]{:S(2)}, u32[]{:S(2)}) collective-permute-start(f32[8,512]{1,0:T(8,128)S(1)} %get-tuple-element.30.local_ref), channel_id=1, source_target_pairs={{385,2},{386,1},{387,4},{388,3},{389,6},{390,5},{391,8},{392,7},{3... | collective-permute-start | bytes 49160 | tf_op jit(solution)/shard_map/ppermute | solution.py:397
  86.3 6.7 %collective-permute-start.12 = (f32[8,512]{1,0:T(8,128)S(1)}, f32[8,512]{1,0:T(8,128)S(1)}, u32[]{:S(2)}, u32[]{:S(2)}) collective-permute-start(f32[8,512]{1,0:T(8,128)S(1)} %get-tuple-element.34), channel_id=1, source_target_pairs={{384,256},{385,257},{386,258},{387,259},{388,260},{389,261},{390,2... | collective-permute-start | bytes 49160 | tf_op jit(solution)/shard_map/ppermute | solution.py:417
  87.0 6.0 %collective-permute-start.11 = (f32[8,512]{1,0:T(8,128)S(1)}, f32[8,512]{1,0:T(8,128)S(1)}, u32[]{:S(2)}, u32[]{:S(2)}) collective-permute-start(f32[8,512]{1,0:T(8,128)S(1)} %get-tuple-element.34), channel_id=1, source_target_pairs={{384,128},{385,129},{386,130},{387,131},{388,132},{389,133},{390,1... | collective-permute-start | bytes 49160 | tf_op jit(solution)/shard_map/ppermute | solution.py:417
  87.7 6.3 %collective-permute-start.10 = (f32[8,512]{1,0:T(8,128)S(1)}, f32[8,512]{1,0:T(8,128)S(1)}, u32[]{:S(2)}, u32[]{:S(2)}) collective-permute-start(f32[8,512]{1,0:T(8,128)S(1)} %get-tuple-element.34), channel_id=1, source_target_pairs={{384,0},{385,1},{386,2},{387,3},{388,4},{389,5},{390,6},{391,7},{3... | collective-permute-start | bytes 49160 | tf_op jit(solution)/shard_map/ppermute | solution.py:417

commit v5 on v4

--- a/solution.py
+++ b/solution.py
@@ -149,10 +149,10 @@
     core,
     plane,
     coef_ref,
+    input_ref,
+    state_in_ref,
     edge_ref,
     rec_ref,
-    input_ref,
-    state_in_ref,
     in_weight_ref,
     out_weight_ref,
     mine_ref,
@@ -215,7 +215,7 @@
             total = total + raw[1, channels, :].astype(jnp.float32)
             out_ref[channels, :] = jnp.where(inside, total, 0.0).astype(jnp.bfloat16)
 
-    if step > 0:
+    if 0 < step < STEPS - 1:
         state_ref[...] = state_in_ref[...]
     final_ref[...] = jnp.zeros_like(final_ref)
 
@@ -298,7 +298,7 @@
         functools.partial(step_kernel, step, core, plane),
         out_shape=[
             jax.ShapeDtypeStruct((320, 2 * FRAME), jnp.bfloat16),
-            jax.ShapeDtypeStruct((3, 8, 2 * FRAME), jnp.float32),
+            jax.ShapeDtypeStruct((3 if step < STEPS - 1 else 1, 8, 2 * FRAME), jnp.float32),
             jax.ShapeDtypeStruct((8, 2 * FRAME), jnp.float32),
         ],
         in_specs=[pl.BlockSpec(memory_space=pltpu.SMEM)] + [in_vmem()] * 8,
@@ -310,7 +310,7 @@
         ],
         compiler_params=params(),
         name=f"step{step}",
-    )(coefs, edge, rec, inputs, state, in_weight, out_weight, mine, other)
+    )(coefs, inputs, state, edge, rec, in_weight, out_weight, mine, other)
 
 
 def copy_kernel(in_ref, out_ref):
@@ -327,6 +327,27 @@
         cost_estimate=hint(20),
         name="copy_row",
     )(row)
+
+
+def arrange_kernel(small_ref, columns_ref, rows_ref):
+    rows_ref[...] = jnp.zeros_like(rows_ref)
+    for half in range(2):
+        value = small_ref[half]
+        filled = jnp.concatenate([value, jnp.zeros((8, 96), jnp.float32)], axis=1)
+        columns_ref[half * 160 : half * 160 + 160, :] = filled.T[0:160]
+    whole = jnp.concatenate([small_ref[0], small_ref[1]], axis=1)
+    rows_ref[0:4, :] = whole[4:8].astype(jnp.bfloat16)
+
+
+def arranged(small):
+    return pl.pallas_call(
+        arrange_kernel,
+        out_shape=[jax.ShapeDtypeStruct((320, 8), jnp.float32), jax.ShapeDtypeStruct((16, 320), jnp.bfloat16)],
+        in_specs=[in_vmem()],
+        out_specs=[in_vmem()] * 2,
+        compiler_params=params(),
+        name="arrange",
+    )(small)
 
 
 def links(comps, bands):
@@ -374,10 +395,7 @@
     other = lax.ppermute(mine, axes, swap)
     small = jnp.concatenate([in_weight, out_weight.T.astype(jnp.float32)], axis=0)
     small = lax.all_gather(small, "cores")
-    in_columns = jnp.concatenate([small[0, 0:4], small[1, 0:4]], axis=1).T
-    in_columns = jnp.pad(in_columns, ((0, 0), (0, 4)))
-    out_rows = jnp.concatenate([small[0, 4:8], small[1, 4:8]], axis=1)
-    out_rows = jnp.pad(out_rows, ((0, 12), (0, 0))).astype(jnp.bfloat16)
+    in_columns, out_rows = arranged(small)
 
     alphas = plan[timesteps]
     rates = jnp.sqrt(alphas[1:] / alphas[:-1])
@@ -413,7 +431,7 @@
     handoff = share.reshape(1, 2, 2, 160 * 240)
 
     total = final
-    for pairs in (noise_onward, noise_first, noise_second):
+    for pairs in (noise_second, noise_first, noise_onward):
         total = total + lax.ppermute(final, axes, pairs)
     total = lax.all_gather(lax.dynamic_slice_in_dim(total, plane, 1, axis=0)[0], "cores")
     denoised = total.reshape(2, 2, FRAME)[..., :240].transpose(1, 0, 2)[:, None]

time: 98.2 us -> 91.4 us (0.931)
  waiting for transfers between devices: 12.3 us -> 1.58 us
  starting transfers between devices: 30.5 us -> 34.4 us
  blocking collectives: 30.4 us -> 32.3 us
  local copies, waits for them, and re-layouts: 7.54 us -> 5.79 us
    ppermute x2, waiting for transfers between devices: 11.3 us -> 0.89 us  [body(): noise = lax.all_gather(lax.ppermute(final, axes, noise_onward), 'cores')]
    ppermute x2, starting transfers between devices: 4.04 us -> 7.87 us  [body(): rec = lax.ppermute(out, axes, onward)]
    all_gather x2, blocking collectives: 13.6 us -> 15.8 us  [body(): noise = lax.all_gather(lax.ppermute(final, axes, noise_onward), 'cores')]
    unnamed x12 -> x11, local copies, waits for them, and re-layouts: 2.16 us -> 1.34 us
  transfers between devices with their start and end apart: 13 -> 13, of which waited for: 3 -> 2; matrix products, arithmetic and copies ran while one was open for 9% -> 7% of each run, Pallas kernels for 3% -> 4%
where the time goes in v5:
time: 91.4 us; the launch traced here: 90.9 us
  starting transfers between devices  34.4 us (38%)
  blocking collectives  32.3 us (35%)
  Pallas kernels  12.1 us (13%)
  local copies, waits for them, and re-layouts  5.79 us (6%)
  other arithmetic  3.75 us (4%)
  waiting for transfers between devices  1.58 us (2%)
  between operations  0.98 us (1%)
    all_gather x2, blocking collectives, body(): noise = lax.all_gather(lax.ppermute(final, axes, noise_onward), 'cores')  15.8 us
    ppermute x1, starting transfers between devices, body(): other = lax.ppermute(mine, axes, swap)  12.6 us
    pallas_call x3, Pallas kernels, run_step(): pl.pallas_call(functools.partial(step_kernel, step, core, plane), out_sha...  8.42 us
    ppermute x2, starting transfers between devices, body(): rec = lax.ppermute(out, axes, onward)  7.87 us
    all_gather x2, blocking collectives, body(): rec = lax.all_gather(rec, 'cores')  7.16 us
    convert_element_type x1, other arithmetic, relaid_weight(): weight.astype(jnp.float32)  3.53 us
    ppermute x1, starting transfers between devices, body(): cond_edge = lax.ppermute(message, axes, edges)  3.46 us
    pallas_call x2, Pallas kernels, run_latent(): pl.pallas_call(functools.partial(latent_kernel, core, plane), out_shape=[...  2.84 us
  transfers between devices with their start and end apart: 13, of which 2 were waited for; matrix products, arithmetic and copies ran while one was open for 7% of the time, Pallas kernels for 4%

profile of v5, /device:TPU:7, one launch (start us, length us, event | category | flops | bytes accessed | tf_op | source)
XLA Modules:
  0.0 90.9 jit_solution(10155423569356512399)
XLA Ops:
  0.6 1.7 %all_gather_reshape_squeeze.3 = bf16[1,2,2,160,240]{4,3,2,1,0:T(8,128)(2,1)S(1)} reshape(bf16[1,2,2,38400]{3,2,1,0:T(2,128)(2,1)} %param.8) | data formatting | bytes 614400 | tf_op jit(solution)/shard_map/all_gather;reshape;squeeze | solution.py:389
  2.4 2.6 %all_gather.42.feat_ref = bf16[2,2,2,160,240]{4,3,2,1,0:T(8,128)(2,1)S(1)} all-gather(bf16[1,2,2,160,240]{4,3,2,1,0:T(8,128)(2,1)S(1)} %all_gather_reshape_squeeze.3), channel_id=1, replica_groups=mesh['comp'=4,'band'=64,'cores'=2] {'cores'}, dimensions={0}, use_global_device_ids=true | all-gather | bytes 921600 | tf_op jit(solution)/shard_map/all_gather | solution.py:389
  5.8 3.5 %collective-permute-start = (bf16[336,512]{1,0:T(8,128)(2,1)S(1)}, bf16[336,512]{1,0:T(8,128)(2,1)S(1)}, u32[]{:S(2)}, u32[]{:S(2)}) collective-permute-start(bf16[336,512]{1,0:T(8,128)(2,1)S(1)} %get-tuple-element.23), channel_id=1, source_target_pairs={{1,2},{2,1},{3,4},{4,3},{5,6},{6,5},{7,8},{8,7},{9,10},{10,9},{11,... | collective-permute-start | bytes 1032200 | tf_op jit(solution)/shard_map/ppermute | solution.py:392
  9.3 3.5 %convert_element_type.11 = f32[1,460800]{1,0:T(1,128)S(1)} convert(bf16[1,460800]{1,0:T(2,128)(2,1)} %param.10) | non-fusion elementwise | flops 460800 | bytes 2764800 | tf_op jit(solution)/shard_map/convert_element_type | solution.py:249
  13.4 12.6 %collective-permute-start.1 = (bf16[480,960]{1,0:T(8,128)(2,1)S(1)}, bf16[480,960]{1,0:T(8,128)(2,1)S(1)}, u32[]{:S(2)}, u32[]{:S(2)}) collective-permute-start(bf16[480,960]{1,0:T(8,128)(2,1)S(1)} %relay.1.mine_ref), channel_id=1, source_target_pairs={{0,1},{1,0},{2,3},{3,2},{4,5},{5,4},{6,7},{7,6},{8,9},{9,8},{10,11... | collective-permute-start | bytes 2764808 | tf_op jit(solution)/shard_map/ppermute | solution.py:395
  27.2 1.8 %all-gather = f32[16,160]{1,0:T(8,128)S(1)} all-gather(f32[8,160]{1,0:T(8,128)S(1)} %pad_maximum_fusion), channel_id=2, replica_groups=mesh['comp'=4,'band'=64,'cores'=2] {'cores'}, dimensions={0}, use_global_device_ids=true | all-gather | bytes 15360 | tf_op jit(solution)/shard_map/all_gather | solution.py:397
  29.2 3.3 %step0.1 = (bf16[320,512]{1,0:T(8,128)(2,1)S(1)}, f32[3,8,512]{2,1,0:T(8,128)S(1)}, f32[8,512]{1,0:T(8,128)S(1)}) custom-call(f32[2,3]{1,0:T(2,128)S(1)} %get-tuple-element.46.coef_ref, bf16[3,16,128]{2,1,0:T(8,128)(2,1)S(1)} %broadcast_in_dim.10.input_ref, f32[2,8,512]{2,1,0:T(8,128)S(1)} %get-tuple-element.21.state_in_ref, ...), custom_call_target="tpu_custom_call" | custom-call | tf_op jit(solution)/shard_map/step0/pallas_call | solution.py:297
  32.5 1.3 %collective-permute-start.2 = (f32[8,512]{1,0:T(8,128)S(1)}, f32[8,512]{1,0:T(8,128)S(1)}, u32[]{:S(2)}, u32[]{:S(2)}) collective-permute-start(f32[8,512]{1,0:T(8,128)S(1)} %get-tuple-element.28.local_ref), channel_id=1, source_target_pairs={{384,0},{385,1},{386,2},{387,3},{388,4},{389,5},{390,6},{391,7},{3... | collective-permute-start | bytes 49160 | tf_op jit(solution)/shard_map/ppermute | solution.py:414
  33.8 1.3 %collective-permute-start.3 = (f32[8,512]{1,0:T(8,128)S(1)}, f32[8,512]{1,0:T(8,128)S(1)}, u32[]{:S(2)}, u32[]{:S(2)}) collective-permute-start(f32[8,512]{1,0:T(8,128)S(1)} %get-tuple-element.28.local_ref), channel_id=1, source_target_pairs={{385,2},{386,1},{387,4},{388,3},{389,6},{390,5},{391,8},{392,7},{3... | collective-permute-start | bytes 49160 | tf_op jit(solution)/shard_map/ppermute | solution.py:415
  35.1 1.3 %collective-permute-start.4 = (bf16[320,512]{1,0:T(8,128)(2,1)S(1)}, bf16[320,512]{1,0:T(8,128)(2,1)S(1)}, u32[]{:S(2)}, u32[]{:S(2)}) collective-permute-start(bf16[320,512]{1,0:T(8,128)(2,1)S(1)} %get-tuple-element.32), channel_id=1, source_target_pairs={{1,130},{2,129},{3,132},{4,131},{5,134},{6,133},{7,136},{8,135},{9... | collective-permute-start | bytes 983048 | tf_op jit(solution)/shard_map/ppermute | solution.py:411
  36.4 1.5 %collective-permute-start.5 = (bf16[320,512]{1,0:T(8,128)(2,1)S(1)}, bf16[320,512]{1,0:T(8,128)(2,1)S(1)}, u32[]{:S(2)}, u32[]{:S(2)}) collective-permute-start(bf16[320,512]{1,0:T(8,128)(2,1)S(1)} %get-tuple-element.32), channel_id=1, source_target_pairs={{0,128},{1,129},{2,130},{3,131},{4,132},{5,133},{6,134},{7,135},{8... | collective-permute-start | bytes 983048 | tf_op jit(solution)/shard_map/ppermute | solution.py:412
  38.8 8.1 %all-gather.1 = f32[16,512]{1,0:T(8,128)S(1)} all-gather(f32[8,512]{1,0:T(8,128)S(1)} %collective-permute-done.2), channel_id=3, replica_groups=mesh['comp'=4,'band'=64,'cores'=2] {'cores'}, dimensions={0}, use_global_device_ids=true | all-gather | bytes 49152 | tf_op jit(solution)/shard_map/all_gather | solution.py:414
  46.9 1.4 %latent.2 = (bf16[3,320,512]{2,1,0:T(8,128)(2,1)S(1)}, f32[3,8,512]{2,1,0:T(8,128)S(1)}) custom-call(f32[2,3]{1,0:T(2,128)S(1)} %get-tuple-element.46.coef_ref, f32[2,8,512]{2,1,0:T(8,128)S(1)} %bitcast.30, f32[8,512]{1,0:T(8,128)S(1)} %collective-permute-done.3.noise_edge_ref, f32[8,512]{1,0:T(8,128)S(1)} %get-tuple-element.28.local_ref, ...), custom_call_target="tpu_custom_call" | custom-call | flops 3000000000 | tf_op jit(solution)/shard_map/latent/pallas_call | solution.py:268
  48.3 3.5 %all-gather.2 = bf16[640,512]{1,0:T(8,128)(2,1)S(1)} all-gather(bf16[320,512]{1,0:T(8,128)(2,1)S(1)} %collective-permute-done.5), channel_id=4, replica_groups=mesh['comp'=4,'band'=64,'cores'=2] {'cores'}, dimensions={0}, use_global_device_ids=true | all-gather | bytes 983040 | tf_op jit(solution)/shard_map/all_gather | solution.py:413
  51.8 2.3 %step1.1 = (bf16[320,512]{1,0:T(8,128)(2,1)S(1)}, f32[3,8,512]{2,1,0:T(8,128)S(1)}, f32[8,512]{1,0:T(8,128)S(1)}) custom-call(f32[2,3]{1,0:T(2,128)S(1)} %get-tuple-element.46.coef_ref, bf16[3,320,512]{2,1,0:T(8,128)(2,1)S(1)} %get-tuple-element.30.input_ref, f32[3,8,512]{2,1,0:T(8,128)S(1)} %get-tuple-element.31.state_in_ref, ...), custom_call_target="tpu_custom_call" | custom-call | tf_op jit(solution)/shard_map/step1/pallas_call | solution.py:297
  56.7 1.3 %collective-permute-start.8 = (bf16[320,512]{1,0:T(8,128)(2,1)S(1)}, bf16[320,512]{1,0:T(8,128)(2,1)S(1)}, u32[]{:S(2)}, u32[]{:S(2)}) collective-permute-start(bf16[320,512]{1,0:T(8,128)(2,1)S(1)} %get-tuple-element.37), channel_id=1, source_target_pairs={{1,130},{2,129},{3,132},{4,131},{5,134},{6,133},{7,136},{8,135},{9... | collective-permute-start | bytes 983048 | tf_op jit(solution)/shard_map/ppermute | solution.py:411
  58.0 6.4 %collective-permute-start.9 = (bf16[320,512]{1,0:T(8,128)(2,1)S(1)}, bf16[320,512]{1,0:T(8,128)(2,1)S(1)}, u32[]{:S(2)}, u32[]{:S(2)}) collective-permute-start(bf16[320,512]{1,0:T(8,128)(2,1)S(1)} %get-tuple-element.37), channel_id=1, source_target_pairs={{0,128},{1,129},{2,130},{3,131},{4,132},{5,133},{6,134},{7,135},{8... | collective-permute-start | bytes 983048 | tf_op jit(solution)/shard_map/ppermute | solution.py:412
  64.5 7.7 %all-gather.3 = f32[16,512]{1,0:T(8,128)S(1)} all-gather(f32[8,512]{1,0:T(8,128)S(1)} %collective-permute-done.6), channel_id=5, replica_groups=mesh['comp'=4,'band'=64,'cores'=2] {'cores'}, dimensions={0}, use_global_device_ids=true | all-gather | bytes 49152 | tf_op jit(solution)/shard_map/all_gather | solution.py:414
  72.2 1.4 %latent.3 = (bf16[3,320,512]{2,1,0:T(8,128)(2,1)S(1)}, f32[3,8,512]{2,1,0:T(8,128)S(1)}) custom-call(f32[2,3]{1,0:T(2,128)S(1)} %get-tuple-element.47.coef_ref, f32[2,8,512]{2,1,0:T(8,128)S(1)} %bitcast.29, f32[8,512]{1,0:T(8,128)S(1)} %collective-permute-done.7.noise_edge_ref, f32[8,512]{1,0:T(8,128)S(1)} %get-tuple-element.33.local_ref, ...), custom_call_target="tpu_custom_call" | custom-call | flops 3000000000 | tf_op jit(solution)/shard_map/latent/pallas_call | solution.py:268
  73.6 3.7 %all-gather.4 = bf16[640,512]{1,0:T(8,128)(2,1)S(1)} all-gather(bf16[320,512]{1,0:T(8,128)(2,1)S(1)} %collective-permute-done.9), channel_id=6, replica_groups=mesh['comp'=4,'band'=64,'cores'=2] {'cores'}, dimensions={0}, use_global_device_ids=true | all-gather | bytes 983040 | tf_op jit(solution)/shard_map/all_gather | solution.py:413
  77.3 2.9 %step2.1 = (bf16[320,512]{1,0:T(8,128)(2,1)S(1)}, f32[1,8,512]{2,1,0:T(8,128)}, f32[8,512]{1,0:T(8,128)S(1)}) custom-call(f32[2,3]{1,0:T(2,128)S(1)} %get-tuple-element.47.coef_ref, bf16[3,320,512]{2,1,0:T(8,128)(2,1)S(1)} %get-tuple-element.35.input_ref, f32[3,8,512]{2,1,0:T(8,128)S(1)} %get-tuple-element.36.state_in_ref, ...), custom_call_target="tpu_custom_call" | custom-call | tf_op jit(solution)/shard_map/step2/pallas_call | solution.py:297
  82.8 2.3 %all-gather.5 = bf16[640,512]{1,0:T(8,128)(2,1)S(1)} all-gather(bf16[320,512]{1,0:T(8,128)(2,1)S(1)} %get-tuple-element.39), channel_id=7, replica_groups=mesh['comp'=4,'band'=64,'cores'=2] {'cores'}, dimensions={0}, use_global_device_ids=true | all-gather | bytes 983040 | tf_op jit(solution)/shard_map/all_gather | solution.py:428
  85.5 1.4 %reshape.19 = bf16[1,2,2,38400]{3,2,1,0:T(2,128)(2,1)} reshape(bf16[2,2,160,240]{3,2,1,0:T(8,128)(2,1)S(1)} %copy.24) | data formatting | bytes 614400 | tf_op jit(solution)/shard_map/reshape | solution.py:431
  87.5 2.7 %all-gather.6 = f32[2,1,512]{2,1,0:T(1,128)S(1)} all-gather(f32[1,1,512]{2,1,0:T(1,128)S(1)} %fusion), channel_id=1, replica_groups=mesh['comp'=4,'band'=64,'cores'=2] {'cores'}, dimensions={0}, use_global_device_ids=true | all-gather | bytes 6144 | tf_op jit(solution)/shard_map/all_gather | solution.py:436
  (56 shorter events, 10.5 us)
Async XLA Ops:
  0.6 25.5 %copy-start = (f32[1000]{0:T(1024)S(1)}, f32[1000]{0:T(1024)}, u32[]{:S(2)}) copy-start(f32[1000]{0:T(1024)} %param.13) | copy-start | bytes 12004
  4.9 0.7 copy-start.1
  5.8 23.4 %collective-permute-start = (bf16[336,512]{1,0:T(8,128)(2,1)S(1)}, bf16[336,512]{1,0:T(8,128)(2,1)S(1)}, u32[]{:S(2)}, u32[]{:S(2)}) collective-permute-start(bf16[336,512]{1,0:T(8,128)(2,1)S(1)} %get-tuple-element.23), channel_id=1, source_target_pairs={{1,2},{2,1},{3,4},{4,3},{5,6},{6,5},{7,8},{8,7},{9,10},{10,9},{11,... | collective-permute-start | bytes 1032200 | tf_op jit(solution)/shard_map/ppermute | solution.py:392
  12.8 13.2 %copy-start.4 = (s32[4]{0:T(128)S(1)}, s32[4]{0:T(128)}, u32[]{:S(2)}) copy-start(s32[4]{0:T(128)} %param.12) | copy-start | bytes 52
  12.8 14.0 %copy-start.3 = (bf16[160,4]{0,1:T(4,128)(2,1)S(1)}, bf16[160,4]{0,1:T(4,128)(2,1)}, u32[]{:S(2)}) copy-start(bf16[160,4]{0,1:T(4,128)(2,1)} %param.11) | copy-start | bytes 3844
  12.9 14.0 %copy-start.2 = (f32[4,160]{1,0:T(4,128)S(1)}, f32[4,160]{1,0:T(4,128)}, u32[]{:S(2)}) copy-start(f32[4,160]{1,0:T(4,128)} %param.9) | copy-start | bytes 7684
  13.4 15.8 %collective-permute-start.1 = (bf16[480,960]{1,0:T(8,128)(2,1)S(1)}, bf16[480,960]{1,0:T(8,128)(2,1)S(1)}, u32[]{:S(2)}, u32[]{:S(2)}) collective-permute-start(bf16[480,960]{1,0:T(8,128)(2,1)S(1)} %relay.1.mine_ref), channel_id=1, source_target_pairs={{0,1},{1,0},{2,3},{3,2},{4,5},{5,4},{6,7},{7,6},{8,9},{9,8},{10,11... | collective-permute-start | bytes 2764808 | tf_op jit(solution)/shard_map/ppermute | solution.py:395
  32.5 6.3 %collective-permute-start.2 = (f32[8,512]{1,0:T(8,128)S(1)}, f32[8,512]{1,0:T(8,128)S(1)}, u32[]{:S(2)}, u32[]{:S(2)}) collective-permute-start(f32[8,512]{1,0:T(8,128)S(1)} %get-tuple-element.28.local_ref), channel_id=1, source_target_pairs={{384,0},{385,1},{386,2},{387,3},{388,4},{389,5},{390,6},{391,7},{3... | collective-permute-start | bytes 49160 | tf_op jit(solution)/shard_map/ppermute | solution.py:414
  33.8 13.1 %collective-permute-start.3 = (f32[8,512]{1,0:T(8,128)S(1)}, f32[8,512]{1,0:T(8,128)S(1)}, u32[]{:S(2)}, u32[]{:S(2)}) collective-permute-start(f32[8,512]{1,0:T(8,128)S(1)} %get-tuple-element.28.local_ref), channel_id=1, source_target_pairs={{385,2},{386,1},{387,4},{388,3},{389,6},{390,5},{391,8},{392,7},{3... | collective-permute-start | bytes 49160 | tf_op jit(solution)/shard_map/ppermute | solution.py:415
  35.1 16.7 %collective-permute-start.4 = (bf16[320,512]{1,0:T(8,128)(2,1)S(1)}, bf16[320,512]{1,0:T(8,128)(2,1)S(1)}, u32[]{:S(2)}, u32[]{:S(2)}) collective-permute-start(bf16[320,512]{1,0:T(8,128)(2,1)S(1)} %get-tuple-element.32), channel_id=1, source_target_pairs={{1,130},{2,129},{3,132},{4,131},{5,134},{6,133},{7,136},{8,135},{9... | collective-permute-start | bytes 983048 | tf_op jit(solution)/shard_map/ppermute | solution.py:411
  36.4 11.9 %collective-permute-start.5 = (bf16[320,512]{1,0:T(8,128)(2,1)S(1)}, bf16[320,512]{1,0:T(8,128)(2,1)S(1)}, u32[]{:S(2)}, u32[]{:S(2)}) collective-permute-start(bf16[320,512]{1,0:T(8,128)(2,1)S(1)} %get-tuple-element.32), channel_id=1, source_target_pairs={{0,128},{1,129},{2,130},{3,131},{4,132},{5,133},{6,134},{7,135},{8... | collective-permute-start | bytes 983048 | tf_op jit(solution)/shard_map/ppermute | solution.py:412
  54.1 10.4 %collective-permute-start.6 = (f32[8,512]{1,0:T(8,128)S(1)}, f32[8,512]{1,0:T(8,128)S(1)}, u32[]{:S(2)}, u32[]{:S(2)}) collective-permute-start(f32[8,512]{1,0:T(8,128)S(1)} %get-tuple-element.33.local_ref), channel_id=1, source_target_pairs={{384,0},{385,1},{386,2},{387,3},{388,4},{389,5},{390,6},{391,7},{3... | collective-permute-start | bytes 49160 | tf_op jit(solution)/shard_map/ppermute | solution.py:414
  55.4 16.7 %collective-permute-start.7 = (f32[8,512]{1,0:T(8,128)S(1)}, f32[8,512]{1,0:T(8,128)S(1)}, u32[]{:S(2)}, u32[]{:S(2)}) collective-permute-start(f32[8,512]{1,0:T(8,128)S(1)} %get-tuple-element.33.local_ref), channel_id=1, source_target_pairs={{385,2},{386,1},{387,4},{388,3},{389,6},{390,5},{391,8},{392,7},{3... | collective-permute-start | bytes 49160 | tf_op jit(solution)/shard_map/ppermute | solution.py:415
  56.7 20.6 %collective-permute-start.8 = (bf16[320,512]{1,0:T(8,128)(2,1)S(1)}, bf16[320,512]{1,0:T(8,128)(2,1)S(1)}, u32[]{:S(2)}, u32[]{:S(2)}) collective-permute-start(bf16[320,512]{1,0:T(8,128)(2,1)S(1)} %get-tuple-element.37), channel_id=1, source_target_pairs={{1,130},{2,129},{3,132},{4,131},{5,134},{6,133},{7,136},{8,135},{9... | collective-permute-start | bytes 983048 | tf_op jit(solution)/shard_map/ppermute | solution.py:411
  58.0 15.6 %collective-permute-start.9 = (bf16[320,512]{1,0:T(8,128)(2,1)S(1)}, bf16[320,512]{1,0:T(8,128)(2,1)S(1)}, u32[]{:S(2)}, u32[]{:S(2)}) collective-permute-start(bf16[320,512]{1,0:T(8,128)(2,1)S(1)} %get-tuple-element.37), channel_id=1, source_target_pairs={{0,128},{1,129},{2,130},{3,131},{4,132},{5,133},{6,134},{7,135},{8... | collective-permute-start | bytes 983048 | tf_op jit(solution)/shard_map/ppermute | solution.py:412
  80.2 7.3 %collective-permute-start.12 = (f32[8,512]{1,0:T(8,128)S(1)}, f32[8,512]{1,0:T(8,128)S(1)}, u32[]{:S(2)}, u32[]{:S(2)}) collective-permute-start(f32[8,512]{1,0:T(8,128)S(1)} %get-tuple-element.38), channel_id=1, source_target_pairs={{384,0},{385,1},{386,2},{387,3},{388,4},{389,5},{390,6},{391,7},{3... | collective-permute-start | bytes 49160 | tf_op jit(solution)/shard_map/ppermute | solution.py:435
  81.5 6.0 %collective-permute-start.11 = (f32[8,512]{1,0:T(8,128)S(1)}, f32[8,512]{1,0:T(8,128)S(1)}, u32[]{:S(2)}, u32[]{:S(2)}) collective-permute-start(f32[8,512]{1,0:T(8,128)S(1)} %get-tuple-element.38), channel_id=1, source_target_pairs={{384,128},{385,129},{386,130},{387,131},{388,132},{389,133},{390,1... | collective-permute-start | bytes 49160 | tf_op jit(solution)/shard_map/ppermute | solution.py:435
  82.1 5.4 %collective-permute-start.10 = (f32[8,512]{1,0:T(8,128)S(1)}, f32[8,512]{1,0:T(8,128)S(1)}, u32[]{:S(2)}, u32[]{:S(2)}) collective-permute-start(f32[8,512]{1,0:T(8,128)S(1)} %get-tuple-element.38), channel_id=1, source_target_pairs={{384,256},{385,257},{386,258},{387,259},{388,260},{389,261},{390,2... | collective-permute-start | bytes 49160 | tf_op jit(solution)/shard_map/ppermute | solution.py:435

commit v6 on v5

--- a/solution.py
+++ b/solution.py
@@ -158,12 +158,10 @@
     mine_ref,
     other_ref,
     out_ref,
-    state_ref,
-    final_ref,
-    raw,
-    active,
-    sums,
+    *rest,
 ):
+    *kept, final_ref, raw, active, sums = rest
+    state_ref = kept[0] if kept else None
     me = core()
     at = plane()
     lanes = lax.broadcasted_iota(jnp.int32, (1, 2 * FRAME), 1)
@@ -237,7 +235,7 @@
             jax.ShapeDtypeStruct((320 + MESSAGE_EXTRA, 2 * FRAME), jnp.bfloat16),
             jax.ShapeDtypeStruct((2, 8, 2 * FRAME), jnp.float32),
         ],
-        in_specs=[in_vmem(), pl.BlockSpec(memory_space=pl.ANY)],
+        in_specs=[in_vmem(), pl.BlockSpec(memory_space=pltpu.HBM)],
         out_specs=[in_vmem()] * 3,
         scratch_shapes=[pltpu.VMEM(latent.shape, latent.dtype), pltpu.SemaphoreType.DMA],
         compiler_params=params(),
@@ -298,11 +296,11 @@
         functools.partial(step_kernel, step, core, plane),
         out_shape=[
             jax.ShapeDtypeStruct((320, 2 * FRAME), jnp.bfloat16),
-            jax.ShapeDtypeStruct((3 if step < STEPS - 1 else 1, 8, 2 * FRAME), jnp.float32),
-            jax.ShapeDtypeStruct((8, 2 * FRAME), jnp.float32),
-        ],
+        ]
+        + [jax.ShapeDtypeStruct((3, 8, 2 * FRAME), jnp.float32)] * (step < STEPS - 1)
+        + [jax.ShapeDtypeStruct((8, 2 * FRAME), jnp.float32)],
         in_specs=[pl.BlockSpec(memory_space=pltpu.SMEM)] + [in_vmem()] * 8,
-        out_specs=[in_vmem()] * 3,
+        out_specs=[in_vmem()] * (3 if step < STEPS - 1 else 2),
         scratch_shapes=[
             pltpu.VMEM((3, 320, 2 * FRAME), jnp.bfloat16),
             pltpu.VMEM((960, 2 * FRAME), jnp.bfloat16),
@@ -327,6 +325,23 @@
         cost_estimate=hint(20),
         name="copy_row",
     )(row)
+
+
+def finish_kernel(rows_ref, out_ref):
+    for row in range(2):
+        for frame in range(2):
+            out_ref[frame, 0, row : row + 1, :] = rows_ref[row : row + 1, frame * FRAME : frame * FRAME + 240]
+
+
+def finished(rows):
+    return pl.pallas_call(
+        finish_kernel,
+        out_shape=jax.ShapeDtypeStruct((2, 1, 2, 240), jnp.float32),
+        in_specs=[in_vmem()],
+        out_specs=in_vmem(),
+        compiler_params=params(),
+        name="finish",
+    )(rows)
 
 
 def arrange_kernel(small_ref, columns_ref, rows_ref):
@@ -406,8 +421,9 @@
     inputs = jnp.zeros((3, 16, LANES), jnp.bfloat16)
     for step in range(STEPS):
         pair = coefs[max(step - 1, 0) : max(step - 1, 0) + 2]
-        out, state, final = run_step(step, pair, rec, edge, inputs, state, in_columns, out_rows, mine, other)
+        out, *kept, final = run_step(step, pair, rec, edge, inputs, state, in_columns, out_rows, mine, other)
         if step + 1 < STEPS:
+            state = kept[0]
             edge = lax.ppermute(out, axes, diagonals)
             rec = lax.ppermute(out, axes, onward)
             rec = lax.all_gather(rec, "cores")
@@ -434,7 +450,7 @@
     for pairs in (noise_second, noise_first, noise_onward):
         total = total + lax.ppermute(final, axes, pairs)
     total = lax.all_gather(lax.dynamic_slice_in_dim(total, plane, 1, axis=0)[0], "cores")
-    denoised = total.reshape(2, 2, FRAME)[..., :240].transpose(1, 0, 2)[:, None]
+    denoised = finished(total)
     return denoised, handoff
 
 

time: 91.4 us -> 90.8 us (level)
  no operation moved by 1% of the time
where the time goes in v6:
time: 90.8 us; the launch traced here: 90.2 us
  starting transfers between devices  34.4 us (38%)
  blocking collectives  32.3 us (36%)
  Pallas kernels  12.1 us (13%)
  local copies, waits for them, and re-layouts  5.17 us (6%)
  other arithmetic  3.73 us (4%)
  waiting for transfers between devices  1.56 us (2%)
  between operations  0.99 us (1%)
    all_gather x2, blocking collectives, body(): noise = lax.all_gather(lax.ppermute(final, axes, noise_onward), 'cores')  15.8 us
    ppermute x1, starting transfers between devices, body(): other = lax.ppermute(mine, axes, swap)  12.6 us
    ppermute x2, starting transfers between devices, body(): rec = lax.ppermute(out, axes, onward)  7.87 us
    pallas_call x3, Pallas kernels, run_step(): pl.pallas_call(functools.partial(step_kernel, step, core, plane), out_sha...  7.81 us
    all_gather x2, blocking collectives, body(): rec = lax.all_gather(rec, 'cores')  7.16 us
    convert_element_type x1, other arithmetic, relaid_weight(): weight.astype(jnp.float32)  3.53 us
    ppermute x1, starting transfers between devices, body(): cond_edge = lax.ppermute(message, axes, edges)  3.46 us
    pallas_call x2, Pallas kernels, run_latent(): pl.pallas_call(functools.partial(latent_kernel, core, plane), out_shape=[...  2.84 us
  transfers between devices with their start and end apart: 13, of which 2 were waited for; matrix products, arithmetic and copies ran while one was open for 7% of the time, Pallas kernels for 4%

profile of v6, /device:TPU:7, one launch (start us, length us, event | category | flops | bytes accessed | tf_op | source)
XLA Modules:
  0.0 90.2 jit_solution(7880559150154052084)
XLA Ops:
  0.6 1.7 %all_gather_reshape_squeeze.3 = bf16[1,2,2,160,240]{4,3,2,1,0:T(8,128)(2,1)S(1)} reshape(bf16[1,2,2,38400]{3,2,1,0:T(2,128)(2,1)} %param.8) | data formatting | bytes 614400 | tf_op jit(solution)/shard_map/all_gather;reshape;squeeze | solution.py:404
  2.4 2.6 %all_gather.42.feat_ref = bf16[2,2,2,160,240]{4,3,2,1,0:T(8,128)(2,1)S(1)} all-gather(bf16[1,2,2,160,240]{4,3,2,1,0:T(8,128)(2,1)S(1)} %all_gather_reshape_squeeze.3), channel_id=1, replica_groups=mesh['comp'=4,'band'=64,'cores'=2] {'cores'}, dimensions={0}, use_global_device_ids=true | all-gather | bytes 921600 | tf_op jit(solution)/shard_map/all_gather | solution.py:404
  5.8 3.5 %collective-permute-start = (bf16[336,512]{1,0:T(8,128)(2,1)S(1)}, bf16[336,512]{1,0:T(8,128)(2,1)S(1)}, u32[]{:S(2)}, u32[]{:S(2)}) collective-permute-start(bf16[336,512]{1,0:T(8,128)(2,1)S(1)} %get-tuple-element.23), channel_id=1, source_target_pairs={{1,2},{2,1},{3,4},{4,3},{5,6},{6,5},{7,8},{8,7},{9,10},{10,9},{11,... | collective-permute-start | bytes 1032200 | tf_op jit(solution)/shard_map/ppermute | solution.py:407
  9.3 3.5 %convert_element_type.11 = f32[1,460800]{1,0:T(1,128)S(1)} convert(bf16[1,460800]{1,0:T(2,128)(2,1)} %param.10) | non-fusion elementwise | flops 460800 | bytes 2764800 | tf_op jit(solution)/shard_map/convert_element_type | solution.py:247
  13.4 12.6 %collective-permute-start.1 = (bf16[480,960]{1,0:T(8,128)(2,1)S(1)}, bf16[480,960]{1,0:T(8,128)(2,1)S(1)}, u32[]{:S(2)}, u32[]{:S(2)}) collective-permute-start(bf16[480,960]{1,0:T(8,128)(2,1)S(1)} %relay.1.mine_ref), channel_id=1, source_target_pairs={{0,1},{1,0},{2,3},{3,2},{4,5},{5,4},{6,7},{7,6},{8,9},{9,8},{10,11... | collective-permute-start | bytes 2764808 | tf_op jit(solution)/shard_map/ppermute | solution.py:410
  27.2 1.8 %all-gather = f32[16,160]{1,0:T(8,128)S(1)} all-gather(f32[8,160]{1,0:T(8,128)S(1)} %pad_maximum_fusion), channel_id=2, replica_groups=mesh['comp'=4,'band'=64,'cores'=2] {'cores'}, dimensions={0}, use_global_device_ids=true | all-gather | bytes 15360 | tf_op jit(solution)/shard_map/all_gather | solution.py:412
  29.2 3.3 %step0.1 = (bf16[320,512]{1,0:T(8,128)(2,1)S(1)}, f32[3,8,512]{2,1,0:T(8,128)S(1)}, f32[8,512]{1,0:T(8,128)S(1)}) custom-call(f32[2,3]{1,0:T(2,128)S(1)} %get-tuple-element.40.coef_ref, bf16[3,16,128]{2,1,0:T(8,128)(2,1)S(1)} %broadcast_in_dim.7.input_ref, f32[2,8,512]{2,1,0:T(8,128)S(1)} %get-tuple-element.21.state_in_ref, ...), custom_call_target="tpu_custom_call" | custom-call | tf_op jit(solution)/shard_map/step0/pallas_call | solution.py:295
  32.5 1.3 %collective-permute-start.2 = (f32[8,512]{1,0:T(8,128)S(1)}, f32[8,512]{1,0:T(8,128)S(1)}, u32[]{:S(2)}, u32[]{:S(2)}) collective-permute-start(f32[8,512]{1,0:T(8,128)S(1)} %get-tuple-element.28.local_ref), channel_id=1, source_target_pairs={{384,0},{385,1},{386,2},{387,3},{388,4},{389,5},{390,6},{391,7},{3... | collective-permute-start | bytes 49160 | tf_op jit(solution)/shard_map/ppermute | solution.py:430
  33.8 1.3 %collective-permute-start.3 = (f32[8,512]{1,0:T(8,128)S(1)}, f32[8,512]{1,0:T(8,128)S(1)}, u32[]{:S(2)}, u32[]{:S(2)}) collective-permute-start(f32[8,512]{1,0:T(8,128)S(1)} %get-tuple-element.28.local_ref), channel_id=1, source_target_pairs={{385,2},{386,1},{387,4},{388,3},{389,6},{390,5},{391,8},{392,7},{3... | collective-permute-start | bytes 49160 | tf_op jit(solution)/shard_map/ppermute | solution.py:431
  35.1 1.3 %collective-permute-start.4 = (bf16[320,512]{1,0:T(8,128)(2,1)S(1)}, bf16[320,512]{1,0:T(8,128)(2,1)S(1)}, u32[]{:S(2)}, u32[]{:S(2)}) collective-permute-start(bf16[320,512]{1,0:T(8,128)(2,1)S(1)} %get-tuple-element.32), channel_id=1, source_target_pairs={{1,130},{2,129},{3,132},{4,131},{5,134},{6,133},{7,136},{8,135},{9... | collective-permute-start | bytes 983048 | tf_op jit(solution)/shard_map/ppermute | solution.py:427
  36.4 1.5 %collective-permute-start.5 = (bf16[320,512]{1,0:T(8,128)(2,1)S(1)}, bf16[320,512]{1,0:T(8,128)(2,1)S(1)}, u32[]{:S(2)}, u32[]{:S(2)}) collective-permute-start(bf16[320,512]{1,0:T(8,128)(2,1)S(1)} %get-tuple-element.32), channel_id=1, source_target_pairs={{0,128},{1,129},{2,130},{3,131},{4,132},{5,133},{6,134},{7,135},{8... | collective-permute-start | bytes 983048 | tf_op jit(solution)/shard_map/ppermute | solution.py:428
  38.8 8.1 %all-gather.1 = f32[16,512]{1,0:T(8,128)S(1)} all-gather(f32[8,512]{1,0:T(8,128)S(1)} %collective-permute-done.2), channel_id=3, replica_groups=mesh['comp'=4,'band'=64,'cores'=2] {'cores'}, dimensions={0}, use_global_device_ids=true | all-gather | bytes 49152 | tf_op jit(solution)/shard_map/all_gather | solution.py:430
  46.9 1.4 %latent.2 = (bf16[3,320,512]{2,1,0:T(8,128)(2,1)S(1)}, f32[3,8,512]{2,1,0:T(8,128)S(1)}) custom-call(f32[2,3]{1,0:T(2,128)S(1)} %get-tuple-element.40.coef_ref, f32[2,8,512]{2,1,0:T(8,128)S(1)} %bitcast.29, f32[8,512]{1,0:T(8,128)S(1)} %collective-permute-done.3.noise_edge_ref, f32[8,512]{1,0:T(8,128)S(1)} %get-tuple-element.28.local_ref, ...), custom_call_target="tpu_custom_call" | custom-call | flops 3000000000 | tf_op jit(solution)/shard_map/latent/pallas_call | solution.py:266
  48.3 3.5 %all-gather.2 = bf16[640,512]{1,0:T(8,128)(2,1)S(1)} all-gather(bf16[320,512]{1,0:T(8,128)(2,1)S(1)} %collective-permute-done.5), channel_id=4, replica_groups=mesh['comp'=4,'band'=64,'cores'=2] {'cores'}, dimensions={0}, use_global_device_ids=true | all-gather | bytes 983040 | tf_op jit(solution)/shard_map/all_gather | solution.py:429
  51.8 2.3 %step1.1 = (bf16[320,512]{1,0:T(8,128)(2,1)S(1)}, f32[3,8,512]{2,1,0:T(8,128)S(1)}, f32[8,512]{1,0:T(8,128)S(1)}) custom-call(f32[2,3]{1,0:T(2,128)S(1)} %get-tuple-element.40.coef_ref, bf16[3,320,512]{2,1,0:T(8,128)(2,1)S(1)} %get-tuple-element.30.input_ref, f32[3,8,512]{2,1,0:T(8,128)S(1)} %get-tuple-element.31.state_in_ref, ...), custom_call_target="tpu_custom_call" | custom-call | tf_op jit(solution)/shard_map/step1/pallas_call | solution.py:295
  56.7 1.3 %collective-permute-start.8 = (bf16[320,512]{1,0:T(8,128)(2,1)S(1)}, bf16[320,512]{1,0:T(8,128)(2,1)S(1)}, u32[]{:S(2)}, u32[]{:S(2)}) collective-permute-start(bf16[320,512]{1,0:T(8,128)(2,1)S(1)} %get-tuple-element.37), channel_id=1, source_target_pairs={{1,130},{2,129},{3,132},{4,131},{5,134},{6,133},{7,136},{8,135},{9... | collective-permute-start | bytes 983048 | tf_op jit(solution)/shard_map/ppermute | solution.py:427
  58.0 6.4 %collective-permute-start.9 = (bf16[320,512]{1,0:T(8,128)(2,1)S(1)}, bf16[320,512]{1,0:T(8,128)(2,1)S(1)}, u32[]{:S(2)}, u32[]{:S(2)}) collective-permute-start(bf16[320,512]{1,0:T(8,128)(2,1)S(1)} %get-tuple-element.37), channel_id=1, source_target_pairs={{0,128},{1,129},{2,130},{3,131},{4,132},{5,133},{6,134},{7,135},{8... | collective-permute-start | bytes 983048 | tf_op jit(solution)/shard_map/ppermute | solution.py:428
  64.5 7.7 %all-gather.3 = f32[16,512]{1,0:T(8,128)S(1)} all-gather(f32[8,512]{1,0:T(8,128)S(1)} %collective-permute-done.6), channel_id=5, replica_groups=mesh['comp'=4,'band'=64,'cores'=2] {'cores'}, dimensions={0}, use_global_device_ids=true | all-gather | bytes 49152 | tf_op jit(solution)/shard_map/all_gather | solution.py:430
  72.2 1.4 %latent.3 = (bf16[3,320,512]{2,1,0:T(8,128)(2,1)S(1)}, f32[3,8,512]{2,1,0:T(8,128)S(1)}) custom-call(f32[2,3]{1,0:T(2,128)S(1)} %get-tuple-element.41.coef_ref, f32[2,8,512]{2,1,0:T(8,128)S(1)} %bitcast.28, f32[8,512]{1,0:T(8,128)S(1)} %collective-permute-done.7.noise_edge_ref, f32[8,512]{1,0:T(8,128)S(1)} %get-tuple-element.33.local_ref, ...), custom_call_target="tpu_custom_call" | custom-call | flops 3000000000 | tf_op jit(solution)/shard_map/latent/pallas_call | solution.py:266
  73.6 3.7 %all-gather.4 = bf16[640,512]{1,0:T(8,128)(2,1)S(1)} all-gather(bf16[320,512]{1,0:T(8,128)(2,1)S(1)} %collective-permute-done.9), channel_id=6, replica_groups=mesh['comp'=4,'band'=64,'cores'=2] {'cores'}, dimensions={0}, use_global_device_ids=true | all-gather | bytes 983040 | tf_op jit(solution)/shard_map/all_gather | solution.py:429
  77.3 2.3 %step2.1 = (bf16[320,512]{1,0:T(8,128)(2,1)S(1)}, f32[8,512]{1,0:T(8,128)S(1)}) custom-call(f32[2,3]{1,0:T(2,128)S(1)} %get-tuple-element.41.coef_ref, bf16[3,320,512]{2,1,0:T(8,128)(2,1)S(1)} %get-tuple-element.35.input_ref, f32[3,8,512]{2,1,0:T(8,128)S(1)} %get-tuple-element.36.state_in_ref, bf16[320,512]{1,0:T(8,128)(2,1)S(1)} %collective-permute-done.8.edge_ref, ...), custom_call_target="tpu_custom_call" | custom-call | tf_op jit(solution)/shard_map/step2/pallas_call | solution.py:295
  82.2 2.3 %all-gather.5 = bf16[640,512]{1,0:T(8,128)(2,1)S(1)} all-gather(bf16[320,512]{1,0:T(8,128)(2,1)S(1)} %get-tuple-element.39), channel_id=7, replica_groups=mesh['comp'=4,'band'=64,'cores'=2] {'cores'}, dimensions={0}, use_global_device_ids=true | all-gather | bytes 983040 | tf_op jit(solution)/shard_map/all_gather | solution.py:444
  84.9 1.4 %reshape.15 = bf16[1,2,2,38400]{3,2,1,0:T(2,128)(2,1)} reshape(bf16[2,2,160,240]{3,2,1,0:T(8,128)(2,1)S(1)} %copy.22) | data formatting | bytes 614400 | tf_op jit(solution)/shard_map/reshape | solution.py:447
  86.9 2.7 %all-gather.6 = f32[2,1,512]{2,1,0:T(1,128)S(1)} all-gather(f32[1,1,512]{2,1,0:T(1,128)S(1)} %fusion), channel_id=1, replica_groups=mesh['comp'=4,'band'=64,'cores'=2] {'cores'}, dimensions={0}, use_global_device_ids=true | all-gather | bytes 6144 | tf_op jit(solution)/shard_map/all_gather | solution.py:452
  (54 shorter events, 10.5 us)
Async XLA Ops:
  0.6 25.5 %copy-start = (f32[1000]{0:T(1024)S(1)}, f32[1000]{0:T(1024)}, u32[]{:S(2)}) copy-start(f32[1000]{0:T(1024)} %param.13) | copy-start | bytes 12004
  4.9 0.7 copy-start.1
  5.8 23.4 %collective-permute-start = (bf16[336,512]{1,0:T(8,128)(2,1)S(1)}, bf16[336,512]{1,0:T(8,128)(2,1)S(1)}, u32[]{:S(2)}, u32[]{:S(2)}) collective-permute-start(bf16[336,512]{1,0:T(8,128)(2,1)S(1)} %get-tuple-element.23), channel_id=1, source_target_pairs={{1,2},{2,1},{3,4},{4,3},{5,6},{6,5},{7,8},{8,7},{9,10},{10,9},{11,... | collective-permute-start | bytes 1032200 | tf_op jit(solution)/shard_map/ppermute | solution.py:407
  12.8 13.2 %copy-start.4 = (s32[4]{0:T(128)S(1)}, s32[4]{0:T(128)}, u32[]{:S(2)}) copy-start(s32[4]{0:T(128)} %param.12) | copy-start | bytes 52
  12.8 14.0 %copy-start.3 = (bf16[160,4]{0,1:T(4,128)(2,1)S(1)}, bf16[160,4]{0,1:T(4,128)(2,1)}, u32[]{:S(2)}) copy-start(bf16[160,4]{0,1:T(4,128)(2,1)} %param.11) | copy-start | bytes 3844
  12.9 14.0 %copy-start.2 = (f32[4,160]{1,0:T(4,128)S(1)}, f32[4,160]{1,0:T(4,128)}, u32[]{:S(2)}) copy-start(f32[4,160]{1,0:T(4,128)} %param.9) | copy-start | bytes 7684
  13.4 15.8 %collective-permute-start.1 = (bf16[480,960]{1,0:T(8,128)(2,1)S(1)}, bf16[480,960]{1,0:T(8,128)(2,1)S(1)}, u32[]{:S(2)}, u32[]{:S(2)}) collective-permute-start(bf16[480,960]{1,0:T(8,128)(2,1)S(1)} %relay.1.mine_ref), channel_id=1, source_target_pairs={{0,1},{1,0},{2,3},{3,2},{4,5},{5,4},{6,7},{7,6},{8,9},{9,8},{10,11... | collective-permute-start | bytes 2764808 | tf_op jit(solution)/shard_map/ppermute | solution.py:410
  32.5 6.3 %collective-permute-start.2 = (f32[8,512]{1,0:T(8,128)S(1)}, f32[8,512]{1,0:T(8,128)S(1)}, u32[]{:S(2)}, u32[]{:S(2)}) collective-permute-start(f32[8,512]{1,0:T(8,128)S(1)} %get-tuple-element.28.local_ref), channel_id=1, source_target_pairs={{384,0},{385,1},{386,2},{387,3},{388,4},{389,5},{390,6},{391,7},{3... | collective-permute-start | bytes 49160 | tf_op jit(solution)/shard_map/ppermute | solution.py:430
  33.8 13.1 %collective-permute-start.3 = (f32[8,512]{1,0:T(8,128)S(1)}, f32[8,512]{1,0:T(8,128)S(1)}, u32[]{:S(2)}, u32[]{:S(2)}) collective-permute-start(f32[8,512]{1,0:T(8,128)S(1)} %get-tuple-element.28.local_ref), channel_id=1, source_target_pairs={{385,2},{386,1},{387,4},{388,3},{389,6},{390,5},{391,8},{392,7},{3... | collective-permute-start | bytes 49160 | tf_op jit(solution)/shard_map/ppermute | solution.py:431
  35.1 16.7 %collective-permute-start.4 = (bf16[320,512]{1,0:T(8,128)(2,1)S(1)}, bf16[320,512]{1,0:T(8,128)(2,1)S(1)}, u32[]{:S(2)}, u32[]{:S(2)}) collective-permute-start(bf16[320,512]{1,0:T(8,128)(2,1)S(1)} %get-tuple-element.32), channel_id=1, source_target_pairs={{1,130},{2,129},{3,132},{4,131},{5,134},{6,133},{7,136},{8,135},{9... | collective-permute-start | bytes 983048 | tf_op jit(solution)/shard_map/ppermute | solution.py:427
  36.4 11.9 %collective-permute-start.5 = (bf16[320,512]{1,0:T(8,128)(2,1)S(1)}, bf16[320,512]{1,0:T(8,128)(2,1)S(1)}, u32[]{:S(2)}, u32[]{:S(2)}) collective-permute-start(bf16[320,512]{1,0:T(8,128)(2,1)S(1)} %get-tuple-element.32), channel_id=1, source_target_pairs={{0,128},{1,129},{2,130},{3,131},{4,132},{5,133},{6,134},{7,135},{8... | collective-permute-start | bytes 983048 | tf_op jit(solution)/shard_map/ppermute | solution.py:428
  54.1 10.4 %collective-permute-start.6 = (f32[8,512]{1,0:T(8,128)S(1)}, f32[8,512]{1,0:T(8,128)S(1)}, u32[]{:S(2)}, u32[]{:S(2)}) collective-permute-start(f32[8,512]{1,0:T(8,128)S(1)} %get-tuple-element.33.local_ref), channel_id=1, source_target_pairs={{384,0},{385,1},{386,2},{387,3},{388,4},{389,5},{390,6},{391,7},{3... | collective-permute-start | bytes 49160 | tf_op jit(solution)/shard_map/ppermute | solution.py:430
  55.4 16.7 %collective-permute-start.7 = (f32[8,512]{1,0:T(8,128)S(1)}, f32[8,512]{1,0:T(8,128)S(1)}, u32[]{:S(2)}, u32[]{:S(2)}) collective-permute-start(f32[8,512]{1,0:T(8,128)S(1)} %get-tuple-element.33.local_ref), channel_id=1, source_target_pairs={{385,2},{386,1},{387,4},{388,3},{389,6},{390,5},{391,8},{392,7},{3... | collective-permute-start | bytes 49160 | tf_op jit(solution)/shard_map/ppermute | solution.py:431
  56.7 20.6 %collective-permute-start.8 = (bf16[320,512]{1,0:T(8,128)(2,1)S(1)}, bf16[320,512]{1,0:T(8,128)(2,1)S(1)}, u32[]{:S(2)}, u32[]{:S(2)}) collective-permute-start(bf16[320,512]{1,0:T(8,128)(2,1)S(1)} %get-tuple-element.37), channel_id=1, source_target_pairs={{1,130},{2,129},{3,132},{4,131},{5,134},{6,133},{7,136},{8,135},{9... | collective-permute-start | bytes 983048 | tf_op jit(solution)/shard_map/ppermute | solution.py:427
  58.0 15.6 %collective-permute-start.9 = (bf16[320,512]{1,0:T(8,128)(2,1)S(1)}, bf16[320,512]{1,0:T(8,128)(2,1)S(1)}, u32[]{:S(2)}, u32[]{:S(2)}) collective-permute-start(bf16[320,512]{1,0:T(8,128)(2,1)S(1)} %get-tuple-element.37), channel_id=1, source_target_pairs={{0,128},{1,129},{2,130},{3,131},{4,132},{5,133},{6,134},{7,135},{8... | collective-permute-start | bytes 983048 | tf_op jit(solution)/shard_map/ppermute | solution.py:428
  79.6 7.3 %collective-permute-start.12 = (f32[8,512]{1,0:T(8,128)S(1)}, f32[8,512]{1,0:T(8,128)S(1)}, u32[]{:S(2)}, u32[]{:S(2)}) collective-permute-start(f32[8,512]{1,0:T(8,128)S(1)} %get-tuple-element.38), channel_id=1, source_target_pairs={{384,0},{385,1},{386,2},{387,3},{388,4},{389,5},{390,6},{391,7},{3... | collective-permute-start | bytes 49160 | tf_op jit(solution)/shard_map/ppermute | solution.py:451
  80.9 6.0 %collective-permute-start.11 = (f32[8,512]{1,0:T(8,128)S(1)}, f32[8,512]{1,0:T(8,128)S(1)}, u32[]{:S(2)}, u32[]{:S(2)}) collective-permute-start(f32[8,512]{1,0:T(8,128)S(1)} %get-tuple-element.38), channel_id=1, source_target_pairs={{384,128},{385,129},{386,130},{387,131},{388,132},{389,133},{390,1... | collective-permute-start | bytes 49160 | tf_op jit(solution)/shard_map/ppermute | solution.py:451
  81.5 5.3 %collective-permute-start.10 = (f32[8,512]{1,0:T(8,128)S(1)}, f32[8,512]{1,0:T(8,128)S(1)}, u32[]{:S(2)}, u32[]{:S(2)}) collective-permute-start(f32[8,512]{1,0:T(8,128)S(1)} %get-tuple-element.38), channel_id=1, source_target_pairs={{384,256},{385,257},{386,258},{387,259},{388,260},{389,261},{390,2... | collective-permute-start | bytes 49160 | tf_op jit(solution)/shard_map/ppermute | solution.py:451
